TPU v7x, 512 devices: a whole 4x8x8 slice. The times are simulated.
512 devices in a mesh: dp: 4 (over x), pipe: 8 (over z_lo, core), seq: 16 (over z_hi, y).
Axes of the slice: x: 4, y: 8, z: 8 (z_hi: 2, z_lo: 4; z = z_hi * 4 + z_lo), core: 2. Of those that a mesh axis runs over, the one named last changes fastest.
Arguments:
- query_first: bfloat16 [4, 8, 1024, 4096], P('dp', 'pipe', 'seq'), may hold values from -5 to 5
- key_first: bfloat16 [4, 8, 1024, 512], P('dp', 'pipe', 'seq'), may hold values from -5 to 5
- value_first: bfloat16 [4, 8, 1024, 512], P('dp', 'pipe', 'seq'), may hold values from -36 to 36
- query_second: bfloat16 [4, 8, 1024, 4096], P('dp', 'pipe', 'seq'), may hold values from -5 to 5
- key_second: bfloat16 [4, 8, 1024, 512], P('dp', 'pipe', 'seq'), may hold values from -5 to 5
- value_second: bfloat16 [4, 8, 1024, 512], P('dp', 'pipe', 'seq'), may hold values from -36 to 36
- grad_output: bfloat16 [4, 8, 1024, 4096], P('dp', 'pipe', 'seq'), may hold values from -6 to 6
- gain: bfloat16 [8, 4096], P('pipe'), may hold values from 0.5 to 1.5
Outputs:
- next_input: bfloat16 [4, 8, 1024, 4096], P('dp', 'pipe', 'seq')
- grad_query: bfloat16 [4, 8, 1024, 4096], P('dp', 'pipe', 'seq')
- grad_key: bfloat16 [4, 8, 1024, 512], P('dp', 'pipe', 'seq')
- grad_value: bfloat16 [4, 8, 1024, 512], P('dp', 'pipe', 'seq')
- grad_gain: float32 [8, 4096], P('pipe', 'seq')
All inputs are finite; a program needn't handle non-finite values.
Results may differ from a plain program's by a relative error of at most 0.012.
The roundings to bfloat16 on the way count: a program that leaves them out, or rounds other values in their place, can miss the bound.
Values may be sent and summed in bfloat16 or wider, within the bound.
No kernel may reach another device: no remote copies, remote signals or barrier semaphores. Data moves between devices by JAX's collectives and lax.ppermute only.
A program may use at most 64 MiB of HBM per device.

v0:
```python
import math

import jax
import jax.numpy as jnp
from jax import lax
from jax.sharding import PartitionSpec as P

QH = 32
KVH = 4
HD = 128


epsilon = 1e-05


def from_behind(value, axis, steps):
    count = lax.axis_size(axis)
    pairs = [(source, (source + steps) % count) for source in range(count)]
    return lax.ppermute(value, axis, pairs)


def local(
    query_first, key_first, value_first, query_second, key_second, value_second, grad_output, gain
):
    seq_count = lax.axis_size("seq")
    seq_index = lax.axis_index("seq")
    local_heads = QH // seq_count
    kv_share = seq_count // KVH
    kv_index = seq_index // kv_share
    head_width = local_heads * HD
    scaling = 1.0 / math.sqrt(HD)
    gain_row = gain[0].astype(jnp.float32)

    def heads_layout(query, keys, values):
        query_local = lax.all_to_all(query, "seq", split_axis=1, concat_axis=0, tiled=True)
        keys_all, values_all = (
            lax.all_gather(keys, "seq", axis=0, tiled=True),
            lax.all_gather(values, "seq", axis=0, tiled=True),
        )
        keys_local = lax.dynamic_slice_in_dim(keys_all, kv_index * HD, HD, 1)
        values_local = lax.dynamic_slice_in_dim(values_all, kv_index * HD, HD, 1)
        return (query_local, keys_local, values_local)

    def probabilities(query_block, keys, offset):
        block_rows = query_block.shape[0]
        scores = (
            jnp.einsum("ihd,jd->hij", query_block, keys, preferred_element_type=jnp.float32)
            * scaling
        )
        row_ids = offset + lax.iota(jnp.int32, block_rows)
        column_ids = lax.iota(jnp.int32, keys.shape[0])
        allowed = column_ids[None, :] <= row_ids[:, None]
        scores = jnp.where(allowed[None], scores, -jnp.inf)
        highest = jnp.max(scores, axis=-1, keepdims=True)
        exponent = jnp.exp(scores - highest)
        return exponent / jnp.sum(exponent, axis=-1, keepdims=True)

    def causal_forward(query_local, keys_local, values_local):
        length = query_local.shape[0]
        block_rows = min(512, length)
        outputs = []
        for offset in range(0, length, block_rows):
            finish = offset + block_rows
            query_block = query_local[offset:finish].reshape(block_rows, local_heads, HD)
            weights = probabilities(query_block, keys_local[:finish], offset).astype(jnp.bfloat16)
            result = jnp.einsum(
                "hij,jd->ihd", weights, values_local[:finish], preferred_element_type=jnp.float32
            )
            outputs.append(result.reshape(block_rows, head_width).astype(jnp.bfloat16))
        return jnp.concatenate(outputs, axis=0)

    first_query, first_keys, first_values = heads_layout(
        query_first[0, 0], key_first[0, 0], value_first[0, 0]
    )
    first_out = causal_forward(first_query, first_keys, first_values)
    first_tokens = lax.all_to_all(first_out, "seq", split_axis=0, concat_axis=1, tiled=True).astype(
        jnp.float32
    )
    first_inverse = lax.rsqrt(
        jnp.mean(first_tokens * first_tokens, axis=-1, keepdims=True) + epsilon
    )
    sending = (gain_row * first_tokens * first_inverse).astype(jnp.bfloat16)
    next_input = from_behind(sending, "pipe", 1)
    upstream = from_behind(grad_output[0, 0], "pipe", -1)
    second_query, second_keys, second_values = heads_layout(
        query_second[0, 0], key_second[0, 0], value_second[0, 0]
    )
    second_out = causal_forward(second_query, second_keys, second_values)
    activity = lax.all_to_all(second_out, "seq", split_axis=0, concat_axis=1, tiled=True).astype(
        jnp.float32
    )
    inverse = lax.rsqrt(jnp.mean(activity * activity, axis=-1, keepdims=True) + epsilon)
    upstream_float = upstream.astype(jnp.float32)
    gained = gain_row * upstream_float
    cross_mean = jnp.mean(gained * activity, axis=-1, keepdims=True)
    grad_tokens = (gained * inverse - activity * inverse**3 * cross_mean).astype(jnp.bfloat16)
    partial_gain = jnp.sum(upstream_float * activity * inverse, axis=0)
    gain_share = lax.psum_scatter(partial_gain, "seq", scatter_dimension=0, tiled=True)
    grad_gain = lax.psum(gain_share, "dp")
    grad_local = lax.all_to_all(grad_tokens, "seq", split_axis=1, concat_axis=0, tiled=True)
    length = second_query.shape[0]
    block_rows = min(512, length)
    grad_keys = jnp.zeros((length, HD), jnp.float32)
    grad_values = jnp.zeros((length, HD), jnp.float32)
    pieces = []
    for offset in range(0, length, block_rows):
        finish = offset + block_rows
        query_block = second_query[offset:finish].reshape(block_rows, local_heads, HD)
        grad_block = grad_local[offset:finish].reshape(block_rows, local_heads, HD)
        output_block = second_out[offset:finish].reshape(block_rows, local_heads, HD)
        probability = probabilities(query_block, second_keys[:finish], offset)
        weights = probability.astype(jnp.bfloat16)
        grad_values = grad_values.at[:finish].add(
            jnp.einsum("hij,ihd->jd", weights, grad_block, preferred_element_type=jnp.float32)
        )
        grad_weights = jnp.einsum(
            "ihd,jd->hij", grad_block, second_values[:finish], preferred_element_type=jnp.float32
        )
        row_dots = jnp.sum(
            grad_block.astype(jnp.float32) * output_block.astype(jnp.float32), axis=-1
        )
        grad_scores = (probability * (grad_weights - row_dots.T[:, :, None]) * scaling).astype(
            jnp.bfloat16
        )
        query_part = jnp.einsum(
            "hij,jd->ihd", grad_scores, second_keys[:finish], preferred_element_type=jnp.float32
        )
        pieces.append(query_part.reshape(block_rows, head_width).astype(jnp.bfloat16))
        grad_keys = grad_keys.at[:finish].add(
            jnp.einsum("hij,ihd->jd", grad_scores, query_block, preferred_element_type=jnp.float32)
        )
    query_grads_local, grad_keys, grad_values = (
        jnp.concatenate(pieces, axis=0),
        grad_keys,
        grad_values,
    )
    grad_query = lax.all_to_all(query_grads_local, "seq", split_axis=0, concat_axis=1, tiled=True)
    key_back, value_back = (
        lax.all_to_all(grad_keys, "seq", split_axis=0, concat_axis=1, tiled=True),
        lax.all_to_all(grad_values, "seq", split_axis=0, concat_axis=1, tiled=True),
    )
    row_count = key_back.shape[0]
    grad_key = (
        key_back.reshape(row_count, KVH, kv_share, HD)
        .sum(axis=2)
        .reshape(row_count, KVH * HD)
        .astype(jnp.bfloat16)
    )
    grad_value = (
        value_back.reshape(row_count, KVH, kv_share, HD)
        .sum(axis=2)
        .reshape(row_count, KVH * HD)
        .astype(jnp.bfloat16)
    )
    return (
        next_input[None, None],
        grad_query[None, None],
        grad_key[None, None],
        grad_value[None, None],
        grad_gain[None],
    )


def solution(mesh):
    return jax.shard_map(
        local,
        mesh=mesh,
        in_specs=(
            P("dp", "pipe", "seq", None),
            P("dp", "pipe", "seq", None),
            P("dp", "pipe", "seq", None),
            P("dp", "pipe", "seq", None),
            P("dp", "pipe", "seq", None),
            P("dp", "pipe", "seq", None),
            P("dp", "pipe", "seq", None),
            P("pipe", None),
        ),
        out_specs=(
            P("dp", "pipe", "seq", None),
            P("dp", "pipe", "seq", None),
            P("dp", "pipe", "seq", None),
            P("dp", "pipe", "seq", None),
            P("pipe", "seq"),
        ),
        check_vma=False,
    )
```

profile of v0, /device:TPU:2, one launch (start us, length us, event | category | flops | bytes accessed | tf_op | source)
XLA Modules:
  0.0 670.8 jit_solution(13109293143807202582)
XLA Ops:
  9.4 1.1 copy.197
  10.5 1.0 copy.139
  11.5 15.6 %all-to-all-start = ((bf16[64,16,256]{2,0,1:T(8,128)(2,1)}), bf16[64,16,256]{2,0,1:T(8,128)(2,1)S(1)}, u32[]{:S(2)}, u32[]{:S(2)}) async-start(bf16[64,16,256]{2,0,1:T(8,128)(2,1)} %copy.139), calls=%async_computation | async-start | bytes 1048576 | tf_op jit(solution)/shard_map/all_to_all | solution.py:35
  27.9 1.0 copy.147
  28.8 18.5 %all-to-all-done = bf16[64,16,256]{2,0,1:T(8,128)(2,1)S(1)} async-done(((bf16[64,16,256]{2,0,1:T(8,128)(2,1)}), bf16[64,16,256]{2,0,1:T(8,128)(2,1)S(1)}, u32[]{:S(2)}, u32[]{:S(2)}) %all-to-all-start) | async-done | bytes 524320 | tf_op jit(solution)/shard_map/all_to_all | solution.py:35
  47.3 4.8 all-to-all-start.2
  52.2 1.2 iota_compare_fusion
  54.3 17.0 %all-to-all-done.2 = bf16[64,16,256]{2,0,1:T(8,128)(2,1)S(1)} async-done(((bf16[64,16,256]{2,0,1:T(8,128)(2,1)}), bf16[64,16,256]{2,0,1:T(8,128)(2,1)S(1)}, u32[]{:S(2)}, u32[]{:S(2)}) %all-to-all-start.2) | async-done | bytes 524320 | tf_op jit(solution)/shard_map/all_to_all | solution.py:35
  71.5 46.9 %all-gather.15.cloned.1.call-done = bf16[1,1,1024,512]{3,2,1,0:T(8,128)(2,1)} async-done(((bf16[1,1,64,512]{3,2,1,0:T(8,128)(2,1)}), bf16[1,1,1024,512]{3,2,1,0:T(8,128)(2,1)}) %all-gather.15.cloned.1.call-update) | async-done | bytes 1048592 | tf_op jit(solution)/shard_map/all_gather | solution.py:38
  118.4 1.0 constant_dynamic-slice_fusion
  120.3 88.3 %all-gather.9.cloned.1.call-done = bf16[1,1,1024,512]{3,2,1,0:T(8,128)(2,1)} async-done(((bf16[1,1,64,512]{3,2,1,0:T(8,128)(2,1)}), bf16[1,1,1024,512]{3,2,1,0:T(8,128)(2,1)}) %all-gather.9.cloned.1.call-update) | async-done | bytes 1048592 | tf_op jit(solution)/shard_map/all_gather | solution.py:38
  208.6 1.0 constant_dynamic-slice_fusion.1
  209.7 89.0 %all-gather.11.cloned.1.call-done = bf16[1,1,1024,512]{3,2,1,0:T(8,128)(2,1)} async-done(((bf16[1,1,64,512]{3,2,1,0:T(8,128)(2,1)}), bf16[1,1,1024,512]{3,2,1,0:T(8,128)(2,1)}) %all-gather.11.cloned.1.call-update) | async-done | bytes 1048592 | tf_op jit(solution)/shard_map/all_gather | solution.py:37
  298.7 1.8 fusion.160
  300.5 2.1 convolution_convert_fusion.4
  303.5 85.3 %all-gather.13.cloned.1.call-done = bf16[1,1,1024,512]{3,2,1,0:T(8,128)(2,1)} async-done(((bf16[1,1,64,512]{3,2,1,0:T(8,128)(2,1)}), bf16[1,1,1024,512]{3,2,1,0:T(8,128)(2,1)}) %all-gather.13.cloned.1.call-update) | async-done | bytes 1048592 | tf_op jit(solution)/shard_map/all_gather | solution.py:37
  388.7 2.0 fusion.148
  390.7 1.3 copy-done.6
  392.6 0.9 copy.153
  393.5 4.8 fusion.151
  398.3 2.7 fusion.26
  402.0 4.2 all-to-all-start.1
  406.3 4.5 fusion.139
  410.8 2.8 fusion.21
  414.1 0.9 copy.154
  415.0 1.9 pad_maximum_fusion.1
  416.8 5.5 all-to-all-done.1
  422.3 6.5 all-to-all-start.3
  428.8 2.1 collective-permute-start.1
  431.7 1.1 convert_bitcast_fusion
  432.8 1.1 copy.195
  433.9 10.6 %all-to-all-done.3 = bf16[16,64,256]{2,1,0:T(8,128)(2,1)} async-done(((bf16[16,64,256]{2,1,0:T(8,128)(2,1)}), bf16[16,64,256]{2,1,0:T(8,128)(2,1)}, u32[]{:S(2)}, u32[]{:S(2)}) %all-to-all-start.3) | async-done | bytes 524320 | tf_op jit(solution)/shard_map/all_to_all | solution.py:89
  444.5 1.1 convert_bitcast_fusion.1
  445.7 1.3 fusion.33
  447.1 1.3 fusion.32
  448.4 1.9 fusion.31
  450.3 2.2 fusion.28
  452.6 25.7 %all_to_all.122 = bf16[64,16,256]{2,0,1:T(8,128)(2,1)S(1)} all-to-all(bf16[64,16,256]{2,0,1:T(8,128)(2,1)S(1)} %bitcast.245), channel_id=1, replica_groups=mesh['dp'=4,'pipe'=8,'seq'=16] {'seq'}, dimensions={1} | all-to-all | bytes 1048576 | tf_op jit(solution)/shard_map/all_to_all | solution.py:100
  479.1 1.7 reshape.293
  480.8 1.8 copy.159
  482.6 2.2 convolution_bitcast_fusion.2
  484.8 1.1 multiply_reduce_fusion.1
  485.9 2.1 fusion.11
  488.0 1.0 copy-done.1
  489.0 1.3 convolution_convert_fusion.1
  491.5 1.5 fusion.25
  493.0 4.7 all-to-all-start.7
  497.7 3.0 fusion.6
  500.8 2.2 convolution_convert_fusion
  503.0 1.8 copy.168
  504.8 1.9 pad_maximum_fusion.2
  506.7 10.7 %all-to-all-done.7 = f32[16,64,128]{2,1,0:T(8,128)} async-done(((f32[16,64,128]{2,1,0:T(8,128)}), f32[16,64,128]{2,1,0:T(8,128)}, u32[]{:S(2)}, u32[]{:S(2)}) %all-to-all-start.7) | async-done | bytes 524320 | tf_op jit(solution)/shard_map/all_to_all | solution.py:140
  517.4 4.8 all-to-all-start.5
  522.2 1.4 convolution_bitcast_fusion.3
  523.7 1.5 fusion.24
  525.2 17.5 %all-to-all-done.5 = bf16[16,64,256]{2,1,0:T(8,128)(2,1)} async-done(((bf16[16,64,256]{2,1,0:T(8,128)(2,1)}), bf16[16,64,256]{2,1,0:T(8,128)(2,1)}, u32[]{:S(2)}, u32[]{:S(2)}) %all-to-all-start.5) | async-done | bytes 524320 | tf_op jit(solution)/shard_map/all_to_all | solution.py:137
  542.6 3.9 all-to-all-start.6
  546.6 1.9 collective-permute-start
  548.5 1.3 dynamic-slice.28
  550.4 98.9 %all-reduce.2 = f32[4096]{0:T(1024)S(1)} all-reduce(f32[4096]{0:T(1024)S(1)} %copy-done.22), channel_id=6, replica_groups=mesh['dp'=4,'pipe'=8,'seq'=16] {'seq'}, use_global_device_ids=true, to_apply=%region_16.17.clone | all-reduce | flops 4096 | bytes 32768
  649.4 9.2 %psum.7 = f32[1,256]{1,0:T(1,128)} all-reduce(f32[1,256]{1,0:T(1,128)S(1)} %bitcast.259), channel_id=1, replica_groups=mesh['dp'=4,'pipe'=8,'seq'=16] {'dp'}, use_global_device_ids=true, to_apply=%region_17.18 | all-reduce | flops 256 | bytes 2048 | tf_op jit(solution)/shard_map/psum | solution.py:99
  658.6 1.1 bitcast_reduce_fusion
  660.4 1.3 copy.169
  661.7 1.0 broadcast_in_dim.55
  (100 shorter events, 13.1 us)
Async XLA Ops:
  7.2 20.6 %copy-start.19 = (bf16[1,1,64,4096]{3,2,1,0:T(8,128)(2,1)S(1)}, bf16[1,1,64,4096]{3,2,1,0:T(8,128)(2,1)}, u32[]{:S(2)}) copy-start(bf16[1,1,64,4096]{3,2,1,0:T(8,128)(2,1)} %param.23) | copy-start | bytes 1572868
  7.2 111.3 %all-gather.15.cloned.1.call-start = ((), (), s32[]{:S(2)}) async-start(), calls=%async_computation.11 | async-start | bytes 1114112 | tf_op jit(solution)/shard_map/all_gather | solution.py:38
  7.9 200.7 %all-gather.9.cloned.1.call-start = ((), (), s32[]{:S(2)}) async-start(), calls=%async_computation.8 | async-start | bytes 1114112 | tf_op jit(solution)/shard_map/all_gather | solution.py:38
  8.7 290.1 %all-gather.11.cloned.1.call-start = ((), (), s32[]{:S(2)}) async-start(), calls=%async_computation.9 | async-start | bytes 1114112 | tf_op jit(solution)/shard_map/all_gather | solution.py:37
  11.5 35.8 %all-to-all-start = ((bf16[64,16,256]{2,0,1:T(8,128)(2,1)}), bf16[64,16,256]{2,0,1:T(8,128)(2,1)S(1)}, u32[]{:S(2)}, u32[]{:S(2)}) async-start(bf16[64,16,256]{2,0,1:T(8,128)(2,1)} %copy.139), calls=%async_computation | async-start | bytes 1048576 | tf_op jit(solution)/shard_map/all_to_all | solution.py:35
  27.2 361.6 %all-gather.13.cloned.1.call-start = ((), (), s32[]{:S(2)}) async-start(), calls=%async_computation.10 | async-start | bytes 1114112 | tf_op jit(solution)/shard_map/all_gather | solution.py:37
  47.3 24.1 %all-to-all-start.2 = ((bf16[64,16,256]{2,0,1:T(8,128)(2,1)}), bf16[64,16,256]{2,0,1:T(8,128)(2,1)S(1)}, u32[]{:S(2)}, u32[]{:S(2)}) async-start(bf16[64,16,256]{2,0,1:T(8,128)(2,1)} %copy.147), calls=%async_computation.2 | async-start | bytes 1048576 | tf_op jit(solution)/shard_map/all_to_all | solution.py:35
  52.2 248.3 %copy-start.21 = (pred[512,512]{0,1:T(8,128)(4,1)}, pred[512,512]{0,1:T(8,128)(4,1)S(1)}, u32[]{:S(2)}) copy-start(pred[512,512]{0,1:T(8,128)(4,1)S(1)} %iota_compare_fusion.1) | copy-start | bytes 786436
  71.5 317.3 %copy-start.13 = (bf16[512,2,128]{2,1,0:T(2,128)(2,1)}, bf16[512,2,128]{2,1,0:T(2,128)(2,1)S(1)}, u32[]{:S(2)}) copy-start(bf16[512,2,128]{2,1,0:T(2,128)(2,1)S(1)} %reshape.291) | copy-start | bytes 786436
  71.5 334.7 %copy-start.10 = (bf16[512,2,128]{2,1,0:T(2,128)(2,1)}, bf16[512,2,128]{2,1,0:T(2,128)(2,1)S(1)}, u32[]{:S(2)}) copy-start(bf16[512,2,128]{2,1,0:T(2,128)(2,1)S(1)} %reshape.292) | copy-start | bytes 786436
  119.4 0.7 copy-start.7
  209.6 91.0 %copy-start.16 = (bf16[1,1,1024,128]{3,2,1,0:T(8,128)(2,1)}, bf16[1,1,1024,128]{3,2,1,0:T(8,128)(2,1)S(1)}, u32[]{:S(2)}) copy-start(bf16[1,1,1024,128]{3,2,1,0:T(8,128)(2,1)S(1)} %constant_dynamic-slice_fusion.1) | copy-start | bytes 786436
  390.7 1.3 copy-start.6
  390.7 1.9 copy-start.23
  392.6 5.7 copy-start.4
  393.5 4.8 copy-start.17
  398.3 2.9 copy-start.14
  401.0 5.2 copy-start.20
  402.0 20.3 %all-to-all-start.1 = ((bf16[16,64,256]{2,1,0:T(8,128)(2,1)}), bf16[16,64,256]{2,1,0:T(8,128)(2,1)}, u32[]{:S(2)}, u32[]{:S(2)}) async-start(bf16[16,64,256]{2,1,0:T(8,128)(2,1)} %bitcast.16), calls=%async_computation.1 | async-start | bytes 1048576 | tf_op jit(solution)/shard_map/all_to_all | solution.py:76
  410.8 2.8 copy-start.25
  410.8 2.8 copy-start.8
  422.3 22.2 %all-to-all-start.3 = ((bf16[16,64,256]{2,1,0:T(8,128)(2,1)}), bf16[16,64,256]{2,1,0:T(8,128)(2,1)}, u32[]{:S(2)}, u32[]{:S(2)}) async-start(bf16[16,64,256]{2,1,0:T(8,128)(2,1)} %bitcast.242), calls=%async_computation.3 | async-start | bytes 1048576 | tf_op jit(solution)/shard_map/all_to_all | solution.py:89
  428.8 19.6 %collective-permute-start.1 = (bf16[64,4096]{1,0:T(8,128)(2,1)}, bf16[64,4096]{1,0:T(8,128)(2,1)}, u32[]{:S(2)}, u32[]{:S(2)}) collective-permute-start(bf16[64,4096]{1,0:T(8,128)(2,1)} %bitcast.260), channel_id=1, source_target_pairs={{0,112},{16,0},{32,16},{48,32},{64,48},{80,64},{96,80},{112,96},{1... | collective-permute-start | bytes 1572872 | tf_op jit(solution)/shard_map/ppermute | solution.py:19
  445.6 4.7 copy-start
  478.3 7.6 %copy-start.24 = (f32[2,512]{1,0:T(2,128)S(1)}, f32[2,512]{1,0:T(2,128)}, u32[]{:S(2)}) copy-start(f32[2,512]{1,0:T(2,128)} %copy-done.23) | copy-start | bytes 12292
  482.6 3.3 copy-start.5
  488.0 1.0 copy-start.1
  489.0 2.1 copy-start.15
  489.0 2.5 copy-start.12
  491.3 1.6 copy-start.3
  491.4 6.3 copy-start.9
  491.5 6.3 copy-start.26
  493.0 24.4 %all-to-all-start.7 = ((f32[16,64,128]{2,1,0:T(8,128)}), f32[16,64,128]{2,1,0:T(8,128)}, u32[]{:S(2)}, u32[]{:S(2)}) async-start(f32[16,64,128]{2,1,0:T(8,128)} %bitcast.59), calls=%async_computation.7 | async-start | bytes 1048576 | tf_op jit(solution)/shard_map/all_to_all | solution.py:140
  500.8 21.5 %copy-start.2 = (bf16[2,512,512]{1,2,0:T(8,128)(2,1)S(1)}, bf16[2,512,512]{1,2,0:T(8,128)(2,1)}, u32[]{:S(2)}) copy-start(bf16[2,512,512]{1,2,0:T(8,128)(2,1)} %copy-done.1) | copy-start | bytes 3145732
  503.0 20.6 %copy-start.11 = (bf16[512,2,128]{2,1,0:T(2,128)(2,1)S(1)}, bf16[512,2,128]{2,1,0:T(2,128)(2,1)}, u32[]{:S(2)}) copy-start(bf16[512,2,128]{2,1,0:T(2,128)(2,1)} %copy-done.10) | copy-start | bytes 786436
  517.4 25.2 %all-to-all-start.5 = ((bf16[16,64,256]{2,1,0:T(8,128)(2,1)}), bf16[16,64,256]{2,1,0:T(8,128)(2,1)}, u32[]{:S(2)}, u32[]{:S(2)}) async-start(bf16[16,64,256]{2,1,0:T(8,128)(2,1)} %bitcast.243), calls=%async_computation.5 | async-start | bytes 1048576 | tf_op jit(solution)/shard_map/all_to_all | solution.py:137
  523.6 22.9 %copy-start.18 = (bf16[64,4096]{1,0:T(8,128)(2,1)S(1)}, bf16[64,4096]{1,0:T(8,128)(2,1)}, u32[]{:S(2)}) copy-start(bf16[64,4096]{1,0:T(8,128)(2,1)} %get-tuple-element.78) | copy-start | bytes 1572868
  523.7 26.8 %copy-start.22 = (f32[4096]{0:T(1024)S(1)}, f32[4096]{0:T(1024)}, u32[]{:S(2)}) copy-start(f32[4096]{0:T(1024)} %get-tuple-element.69) | copy-start | bytes 49156
  542.6 120.1 %all-to-all-start.6 = ((f32[16,64,128]{2,1,0:T(8,128)}), f32[16,64,128]{2,1,0:T(8,128)S(1)}, u32[]{:S(2)}, u32[]{:S(2)}) async-start(f32[16,64,128]{2,1,0:T(8,128)} %bitcast.54), calls=%async_computation.6 | async-start | bytes 1048576 | tf_op jit(solution)/shard_map/all_to_all | solution.py:139
  546.6 112.0 %collective-permute-start = (bf16[64,4096]{1,0:T(8,128)(2,1)S(1)}, bf16[64,4096]{1,0:T(8,128)(2,1)S(1)}, u32[]{:S(2)}, u32[]{:S(2)}) collective-permute-start(bf16[64,4096]{1,0:T(8,128)(2,1)S(1)} %copy-done.18), channel_id=1, source_target_pairs={{0,16},{16,32},{32,48},{48,64},{64,80},{80,96},{96,112},{112,0},{1... | collective-permute-start | bytes 1572872 | tf_op jit(solution)/shard_map/ppermute | solution.py:19
Sparse Core Ops, SparseCore 0:
  11.2 107.1 all-gather.14
  121.6 86.8 all-gather.8
  211.8 86.8 all-gather.10
  301.8 86.8 all-gather.12
where the time goes:
time: 674 us; the launch traced here: 671 us
  waiting for transfers between devices  392 us (58%)
  blocking collectives  134 us (20%)
  starting transfers between devices  48.9 us (7%)
  matrix products  33.8 us (5%)
  local copies, waits for them, and re-layouts  26.6 us (4%)
  other arithmetic  21 us (3%)
  between operations  15.1 us (2%)
    all_gather x2, waiting for transfers between devices, heads_layout(): lax.all_gather(keys, 'seq', axis=0, tiled=True)  174 us
    all_gather x2, waiting for transfers between devices, heads_layout(): lax.all_gather(values, 'seq', axis=0, tiled=True)  135 us
    unnamed x1, blocking collectives  98.9 us
    all_to_all x2, waiting for transfers between devices, heads_layout(): lax.all_to_all(query, 'seq', split_axis=1, concat_axis=0, tiled=True)  35.5 us
    all_to_all x1, blocking collectives, local(): lax.all_to_all(grad_tokens, 'seq', split_axis=1, concat_axis=0, tiled=True)  25.7 us
    all_to_all x2, starting transfers between devices, heads_layout(): lax.all_to_all(query, 'seq', split_axis=1, concat_axis=0, tiled=True)  20.5 us
    all_to_all x1, waiting for transfers between devices, local(): lax.all_to_all(query_grads_local, 'seq', split_axis=0, concat_axis=1, til...  17.5 us
  transfers between devices with their start and end apart: 13, of which 10 were waited for; matrix products, arithmetic and copies ran while one was open for 7% of the time, Pallas kernels for 0%

commit v1 on v0

v1 whole, which is shorter than its diff:
```python
import functools
import math

import jax
import jax.numpy as jnp
from jax import lax
from jax.experimental import pallas as pl
from jax.experimental.pallas import tpu as pltpu
from jax.sharding import Mesh
from jax.sharding import PartitionSpec as P

HD = 128
EPSILON = 1e-05
SCALE = 1.0 / math.sqrt(HD)
F32 = jnp.float32
BF16 = jnp.bfloat16

NEAR = ((0, 1), (2, 3))
FAR = ((0, 2), (1, 3))
CROSS = ((1, 2), (0, 3))
GROUP = ("zhi", "yhi")
SEQ = ("zhi", "yhi", "ylo")

VMEM = pl.BlockSpec(memory_space=pltpu.VMEM)
SMEM = pl.BlockSpec(memory_space=pltpu.SMEM)


def call(body, outs, inputs, scratch=(), flops=0, moved=0, name=None):
    return pl.pallas_call(
        body,
        out_shape=outs,
        in_specs=[SMEM] + [VMEM] * (len(inputs) - 1),
        out_specs=jax.tree.map(lambda _: VMEM, outs),
        scratch_shapes=list(scratch),
        compiler_params=pltpu.CompilerParams(vmem_limit_bytes=48 * 1024 * 1024),
        cost_estimate=pl.CostEstimate(
            flops=flops, bytes_accessed=moved, transcendentals=0
        ),
        name=name,
    )(*inputs)


def dot_nt(a, b):
    return lax.dot_general(a, b, (((1,), (1,)), ((), ())), preferred_element_type=F32)


def dot_nn(a, b):
    return lax.dot_general(a, b, (((1,), (0,)), ((), ())), preferred_element_type=F32)


def column(row):
    return jnp.broadcast_to(row, (HD, row.shape[1])).T


def row_of(block):
    return jnp.sum(block.T, axis=0, keepdims=True)


def from_place(index, step, count):
    return lax.rem(index - step + count, count)


def biases(where):
    group = where[0]
    odd = lax.rem(group, 2) == 1
    late = group >= 2
    near = jnp.where(odd, 0.0, -jnp.inf).astype(F32)
    far = jnp.where(late, 0.0, -jnp.inf).astype(F32)
    return near, far, far


def masked_scores(keys, queries, bias, n):
    scores = dot_nt(keys, queries) * SCALE
    key_ids = lax.broadcasted_iota(jnp.int32, (n, n), 0)
    query_ids = lax.broadcasted_iota(jnp.int32, (n, n), 1)
    parts = [jnp.where(key_ids <= query_ids, scores[:n], -jnp.inf)]
    for i in range(3):
        parts.append(scores[(i + 1) * n : (i + 2) * n] + bias[i])
    return jnp.concatenate(parts, axis=0)


def forward_head(keys, values_t, queries, bias, n):
    scores = masked_scores(keys, queries, bias, n)
    highest = jnp.max(scores, axis=0, keepdims=True)
    exponent = jnp.exp(scores - highest)
    total = jnp.sum(exponent, axis=0, keepdims=True)
    weights = (exponent * (1.0 / total)).astype(BF16)
    out = dot_nn(values_t, weights).T.astype(BF16)
    return out, highest + jnp.log(total)


def load_keys(kv_refs, at, k_ref, n):
    for i, ref in enumerate(kv_refs):
        k_ref[i * n : (i + 1) * n, :] = ref[:, at : at + HD]


def load_values_t(kv_refs, at, vt_ref, n):
    for i, ref in enumerate(kv_refs):
        vt_ref[:, i * n : (i + 1) * n] = ref[:, at : at + HD].T


def forward_first_body(heads, n, where, q, kv0, kv1, kv2, kv3, out, stats, k_s, vt_s):
    kvs = (kv0, kv1, kv2, kv3)
    load_keys(kvs, 2 * HD, k_s, n)
    load_values_t(kvs, 3 * HD, vt_s, n)
    bias = biases(where)
    square = jnp.zeros((n, HD), F32)
    for h in range(heads):
        cols = slice(h * HD, (h + 1) * HD)
        result, _ = forward_head(k_s[...], vt_s[...], q[:, cols], bias, n)
        out[:, cols] = result
        result = result.astype(F32)
        square = square + result * result
    row = row_of(square)
    for copy in range(stats.shape[0]):
        stats[copy] = jnp.broadcast_to(row, stats.shape[1:])


def assemble(where, pieces, up_s):
    rows = pieces[0].shape[0]
    for k, piece in enumerate(pieces):
        at = pl.multiple_of(from_place(where[1], k, len(pieces)) * rows, rows)
        up_s[pl.ds(at, rows), :] = piece[...]


def forward_second_body(
    heads, n, where, q, kv0, kv1, kv2, kv3, up0, up1, up2, up3, gain, out, lse, stats, k_s, vt_s, up_s
):
    kvs = (kv0, kv1, kv2, kv3)
    assemble(where, (up0, up1, up2, up3), up_s)
    load_keys(kvs, 0, k_s, n)
    load_values_t(kvs, HD, vt_s, n)
    bias = biases(where)
    square = jnp.zeros((n, HD), F32)
    cross = jnp.zeros((n, HD), F32)
    for h in range(heads):
        cols = slice(h * HD, (h + 1) * HD)
        result, logs = forward_head(k_s[...], vt_s[...], q[:, cols], bias, n)
        out[:, cols] = result
        lse[h : h + 1, :] = logs
        result = result.astype(F32)
        square = square + result * result
        cross = cross + gain[:, cols].astype(F32) * up_s[:, cols].astype(F32) * result
    rows = jnp.concatenate(
        [row_of(square), row_of(cross), jnp.zeros((stats.shape[1] - 2, n), F32)], axis=0
    )
    for copy in range(stats.shape[0]):
        stats[copy] = rows


def normed_body(heads, width, where, act, stats, gain, o0, o1, o2, o3):
    outs = (o0, o1, o2, o3)
    rows = o0.shape[0]
    total = stats[0, 0:1] + stats[1, 0:1] + stats[2, 0:1] + stats[3, 0:1]
    inverse = column(lax.rsqrt(total / width + EPSILON))
    inverse = jnp.concatenate([inverse] * heads, axis=1)
    normed = (gain[...].astype(F32) * act[...].astype(F32) * inverse).astype(BF16)
    full = normed
    for k in range(4):
        wanted = lax.rem(where[1] + k, 4)
        for block in range(4):

            @pl.when(wanted == block)
            def _(block=block, k=k):
                outs[k][...] = full[block * rows : (block + 1) * rows]


def gain_body(heads, width, where, act, stats, up0, up1, up2, up3, out, up_s):
    assemble(where, (up0, up1, up2, up3), up_s)
    total = stats[0, 0:1] + stats[1, 0:1] + stats[2, 0:1] + stats[3, 0:1]
    inverse = column(lax.rsqrt(total / width + EPSILON))
    for h in range(heads):
        cols = slice(h * HD, (h + 1) * HD)
        product = up_s[:, cols].astype(F32) * act[:, cols].astype(F32) * inverse
        out[h : h + 1, :] = jnp.sum(product, axis=0, keepdims=True)


def backward_body(
    heads, n, width, where, q, kv0, kv1, kv2, kv3, up0, up1, up2, up3, gain, act, lse, stats,
    dq, dkv0, dkv1, dkv2, dkv3, k_s, kt_s, v_s, up_s, dk_s, dv_s,
):
    kvs = (kv0, kv1, kv2, kv3)
    assemble(where, (up0, up1, up2, up3), up_s)
    load_keys(kvs, 0, k_s, n)
    load_values_t(kvs, 0, kt_s, n)
    load_keys(kvs, HD, v_s, n)
    bias = biases(where)
    totals = stats[0] + stats[1] + stats[2] + stats[3]
    inverse_row = lax.rsqrt(totals[0:1] / width + EPSILON)
    inverse = column(inverse_row)
    shrink = column(inverse_row * inverse_row * inverse_row * (totals[1:2] / width))
    for h in range(heads):
        cols = slice(h * HD, (h + 1) * HD)
        queries = q[:, cols]
        act_h = act[:, cols].astype(F32)
        gained = gain[:, cols].astype(F32) * up_s[:, cols].astype(F32)
        grad = (gained * inverse - act_h * shrink).astype(BF16)
        dots = row_of(grad.astype(F32) * act_h)
        scores = masked_scores(k_s[...], queries, bias, n)
        probs = jnp.exp(scores - lse[h : h + 1, :])
        grad_weights = dot_nt(v_s[...], grad)
        grad_scores = (probs * (grad_weights - dots) * SCALE).astype(BF16)
        dv = dot_nn(probs.astype(BF16), grad)
        dk = dot_nn(grad_scores, queries)
        if h == 0:
            dv_s[...] = dv
            dk_s[...] = dk
        else:
            dv_s[...] += dv
            dk_s[...] += dk
        dq[:, cols] = dot_nn(kt_s[...], grad_scores).T.astype(BF16)
    for i, ref in enumerate((dkv0, dkv1, dkv2, dkv3)):
        ref[:, :HD] = dk_s[i * n : (i + 1) * n].astype(ref.dtype)
        ref[:, HD:] = dv_s[i * n : (i + 1) * n].astype(ref.dtype)


def split_body(where, full, o0, o1, o2, o3):
    width = o0.shape[1]
    for k, out in enumerate((o0, o1, o2, o3)):
        at = pl.multiple_of(lax.rem(where[1] + k, 4) * width, width)
        out[...] = full[:, pl.ds(at, width)]


def join_body(where, p0, p1, p2, p3, out):
    width = p0.shape[1]
    for k, piece in enumerate((p0, p1, p2, p3)):
        at = pl.multiple_of(from_place(where[1], k, 4) * width, width)
        out[:, pl.ds(at, width)] = piece[...]


def sds(shape, dtype):
    return jax.ShapeDtypeStruct(shape, dtype)


def swap_lo(packed):
    return lax.all_to_all(packed, "ylo", split_axis=0, concat_axis=0, tiled=True)


def local(
    query_first, key_first, value_first, query_second, key_second, value_second, grad_output, gain
):
    lo = lax.axis_size("ylo")
    tokens, width = query_first.shape[2:]
    n = tokens * lo
    cols = width // lo
    heads = cols // HD
    pipes = lax.axis_size("pipe")
    ylo = lax.axis_index("ylo")
    group = lax.axis_index(GROUP)
    where = jnp.stack([group, ylo]).astype(jnp.int32)
    gain_cols = lax.dynamic_slice_in_dim(gain, ylo * cols, cols, 1)

    def shifted(pieces, steps):
        got = []
        for k, piece in enumerate(pieces):
            pairs = [
                (p * lo + y, ((p + steps) % pipes) * lo + (y + k) % lo)
                for p in range(pipes)
                for y in range(lo)
            ]
            got.append(lax.ppermute(piece, ("pipe", "ylo"), pairs))
        return got

    kv = jnp.concatenate(
        [
            x[0, 0].reshape(tokens, lo, HD)
            for x in (key_second, value_second, key_first, value_first)
        ],
        axis=2,
    ).transpose(1, 0, 2)
    kv0 = swap_lo(kv).reshape(n, 4 * HD)
    kvs = [kv0] + [lax.ppermute(kv0, GROUP, pairs) for pairs in (NEAR, FAR, CROSS)]

    pieces = call(
        split_body, (sds((tokens, cols), BF16),) * 4, (where, grad_output[0, 0]), name="split"
    )
    up = shifted(pieces, -1)

    def by_heads(query):
        packed = query[0, 0].reshape(tokens, lo, cols).transpose(1, 0, 2)
        return swap_lo(packed).reshape(n, cols)

    q2 = by_heads(query_second)
    q1 = by_heads(query_first)
    keys_shape = (4 * n, HD)
    turned = (HD, 4 * n)
    unit = 2 * 4 * n * n * HD * heads

    out2, lse, stats2 = call(
        functools.partial(forward_second_body, heads, n),
        (sds((n, cols), BF16), sds((heads, n), F32), sds((lo, 8, n), F32)),
        (where, q2, *kvs, *up, gain_cols),
        [pltpu.VMEM(keys_shape, BF16), pltpu.VMEM(turned, BF16), pltpu.VMEM((n, cols), BF16)],
        flops=2 * unit,
        moved=4 << 20,
        name="forward_second",
    )
    stats2 = swap_lo(stats2)
    out1, stats1 = call(
        functools.partial(forward_first_body, heads, n),
        (sds((n, cols), BF16), sds((lo, 8, n), F32)),
        (where, q1, *kvs),
        [pltpu.VMEM(keys_shape, BF16), pltpu.VMEM(turned, BF16)],
        flops=2 * unit,
        moved=4 << 20,
        name="forward_first",
    )
    stats1 = swap_lo(stats1)

    gain_part = call(
        functools.partial(gain_body, heads, width),
        sds((heads, HD), F32),
        (where, out2, stats2, *up),
        [pltpu.VMEM((n, cols), BF16)],
        name="gain_rows",
    )
    replicas = lax.axis_size("dp")
    spread = jnp.broadcast_to(
        gain_part.reshape(1, 4, heads // 4, HD), (replicas, 4, heads // 4, HD)
    ).reshape(replicas * 4, heads // 4, HD)
    shares = lax.all_to_all(spread, ("dp",) + GROUP, split_axis=0, concat_axis=0, tiled=True)
    share = jnp.sum(shares, axis=0)
    turn = [(g * lo + y, y * lo + g) for g in range(4) for y in range(lo)]
    grad_gain = lax.ppermute(share, SEQ, turn).reshape(1, cols // 4)

    dq, dkv0, dkv1, dkv2, dkv3 = call(
        functools.partial(backward_body, heads, n, width),
        (sds((n, cols), BF16), sds((n, 2 * HD), F32)) + (sds((n, 2 * HD), BF16),) * 3,
        (where, q2, *kvs, *up, gain_cols, out2, lse, stats2),
        [
            pltpu.VMEM(keys_shape, BF16),
            pltpu.VMEM(turned, BF16),
            pltpu.VMEM(keys_shape, BF16),
            pltpu.VMEM((n, cols), BF16),
            pltpu.VMEM(keys_shape, F32),
            pltpu.VMEM(keys_shape, F32),
        ],
        flops=5 * unit,
        moved=6 << 20,
        name="backward",
    )
    back = [
        lax.ppermute(part, GROUP, [(b, a) for a, b in pairs])
        for part, pairs in ((dkv1, NEAR), (dkv2, FAR), (dkv3, CROSS))
    ]
    dkv = dkv0 + (back[0].astype(F32) + back[1].astype(F32) + back[2].astype(F32))
    dq = swap_lo(dq.reshape(lo, tokens, cols))
    grad_query = dq.transpose(1, 0, 2).reshape(tokens, width)
    dkv = swap_lo(dkv.astype(BF16).reshape(lo, tokens, 2 * HD))
    grad_key = dkv[:, :, :HD].transpose(1, 0, 2).reshape(tokens, lo * HD)
    grad_value = dkv[:, :, HD:].transpose(1, 0, 2).reshape(tokens, lo * HD)

    normed = call(
        functools.partial(normed_body, heads, width),
        (sds((tokens, cols), BF16),) * 4,
        (where, out1, stats1, gain_cols),
        name="normed",
    )
    arrived = shifted(normed, 1)
    next_input = call(
        join_body, sds((tokens, width), BF16), (where, *arrived), name="join"
    )
    return (
        next_input[None, None],
        grad_query[None, None],
        grad_key[None, None],
        grad_value[None, None],
        grad_gain,
    )


def solution(mesh):
    shape = mesh.devices.shape
    fine = Mesh(
        mesh.devices.reshape(shape[0], shape[1], 2, 2, shape[2] // 4),
        ("dp", "pipe", "zhi", "yhi", "ylo"),
    )
    big = P("dp", "pipe", SEQ, None)
    return jax.shard_map(
        local,
        mesh=fine,
        in_specs=(big,) * 7 + (P("pipe", None),),
        out_specs=(big,) * 4 + (P("pipe", SEQ),),
        check_vma=False,
    )
```

time: 674 us -> 205 us (0.30)
  the two profiles are of different devices: /device:TPU:2 before, /device:TPU:1 now
where the time goes in v1:
time: 205 us; the launch traced here: 202 us
  starting transfers between devices  105 us (51%)
  waiting for transfers between devices  47.1 us (23%)
  Pallas kernels  26.5 us (13%)
  local copies, waits for them, and re-layouts  13.3 us (6%)
  blocking collectives  7.15 us (3%)
    ppermute x8, starting transfers between devices, shifted(): got.append(lax.ppermute(piece, ('pipe', 'ylo'), pairs))  42.7 us
    all_to_all x6, starting transfers between devices, swap_lo(): lax.all_to_all(packed, 'ylo', split_axis=0, concat_axis=0, tiled=True)  26.7 us
    pallas_call x7, Pallas kernels, call(): pl.pallas_call(body, out_shape=outs, in_specs=[SMEM] + [VMEM] * (len(inpu...  26.5 us
    ppermute x8, waiting for transfers between devices, shifted(): got.append(lax.ppermute(piece, ('pipe', 'ylo'), pairs))  21.7 us
    all_to_all x1, starting transfers between devices, local(): lax.all_to_all(spread, ('dp',) + GROUP, split_axis=0, concat_axis=0, tile...  15.7 us
    ppermute x3, starting transfers between devices, local(): lax.ppermute(kv0, GROUP, pairs)  15.4 us
    all_to_all x6, waiting for transfers between devices, swap_lo(): lax.all_to_all(packed, 'ylo', split_axis=0, concat_axis=0, tiled=True)  12.9 us
    all_to_all x1, waiting for transfers between devices, local(): lax.all_to_all(spread, ('dp',) + GROUP, split_axis=0, concat_axis=0, tile...  12.5 us
  transfers between devices with their start and end apart: 22, of which 9 were waited for; matrix products, arithmetic and copies ran while one was open for 3% of the time, Pallas kernels for 9%

profile of v1, /device:TPU:1, one launch (start us, length us, event | category | flops | bytes accessed | tf_op | source)
XLA Modules:
  0.0 202.0 jit_solution(6361651746878070555)
XLA Ops:
  0.6 0.0 copy-start
  0.6 0.9 reshape_squeeze.19
  1.5 0.0 copy-start.7
  1.5 0.8 copy-done.7
  2.4 0.0 copy-start.8
  2.4 0.8 copy-done.8
  3.3 0.8 copy-done.9
  4.1 0.0 copy-start.6
  4.1 0.7 maximum_bitcast_fusion
  4.9 5.4 %all-to-all-start.1 = ((bf16[4,64,512]{2,1,0:T(8,128)(2,1)}), bf16[4,64,512]{2,1,0:T(8,128)(2,1)S(1)}, u32[]{:S(2)}, u32[]{:S(2)}) async-start(bf16[4,64,512]{2,1,0:T(8,128)(2,1)} %maximum_bitcast_fusion), calls=%async_computation.1 | async-start | bytes 524288 | tf_op jit(solution)/shard_map/all_to_all | solution.py:236
  10.3 0.4 reshape_squeeze.23
  10.7 1.0 copy.45
  11.6 4.3 %all-to-all-done.1 = bf16[4,64,512]{2,1,0:T(8,128)(2,1)S(1)} async-done(((bf16[4,64,512]{2,1,0:T(8,128)(2,1)}), bf16[4,64,512]{2,1,0:T(8,128)(2,1)S(1)}, u32[]{:S(2)}, u32[]{:S(2)}) %all-to-all-start.1) | async-done | bytes 262176 | tf_op jit(solution)/shard_map/all_to_all | solution.py:236
  15.9 3.6 %all-to-all-start.3 = ((bf16[4,64,1024]{2,1,0:T(8,128)(2,1)}), bf16[4,64,1024]{2,1,0:T(8,128)(2,1)S(1)}, u32[]{:S(2)}, u32[]{:S(2)}) async-start(bf16[4,64,1024]{2,1,0:T(8,128)(2,1)} %bitcast.35), calls=%async_computation.3 | async-start | bytes 1048576 | tf_op jit(solution)/shard_map/all_to_all | solution.py:236
  19.5 0.1 pad_add_fusion.where
  19.6 0.6 split.1
  20.2 11.3 %collective-permute-start.10 = (bf16[64,1024]{1,0:T(8,128)(2,1)S(1)}, bf16[64,1024]{1,0:T(8,128)(2,1)S(1)}, u32[]{:S(2)}, u32[]{:S(2)}) collective-permute-start(bf16[64,1024]{1,0:T(8,128)(2,1)S(1)} %get-tuple-element.32), channel_id=1, source_target_pairs={{0,115},{1,112},{2,113},{3,114},{16,3},{17,0},{18,1},{19,2},{32,19... | collective-permute-start | bytes 393224 | tf_op jit(solution)/shard_map/ppermute | solution.py:261
  31.5 3.5 %collective-permute-start.7 = (bf16[64,1024]{1,0:T(8,128)(2,1)S(1)}, bf16[64,1024]{1,0:T(8,128)(2,1)S(1)}, u32[]{:S(2)}, u32[]{:S(2)}) collective-permute-start(bf16[64,1024]{1,0:T(8,128)(2,1)S(1)} %get-tuple-element.29), channel_id=1, source_target_pairs={{0,112},{1,113},{2,114},{3,115},{16,0},{17,1},{18,2},{19,3},{32,16... | collective-permute-start | bytes 393224 | tf_op jit(solution)/shard_map/ppermute | solution.py:261
  35.0 6.1 %collective-permute-start = (bf16[256,512]{1,0:T(8,128)(2,1)S(1)}, bf16[256,512]{1,0:T(8,128)(2,1)S(1)}, u32[]{:S(2)}, u32[]{:S(2)}) collective-permute-start(bf16[256,512]{1,0:T(8,128)(2,1)S(1)} %bitcast.41), channel_id=1, source_target_pairs={{0,4},{8,12},{1,5},{9,13},{2,6},{10,14},{3,7},{11,15},{16,20},{24,... | collective-permute-start | bytes 786440 | tf_op jit(solution)/shard_map/ppermute | solution.py:272
  41.2 8.0 %collective-permute-start.1 = (bf16[256,512]{1,0:T(8,128)(2,1)S(1)}, bf16[256,512]{1,0:T(8,128)(2,1)S(1)}, u32[]{:S(2)}, u32[]{:S(2)}) collective-permute-start(bf16[256,512]{1,0:T(8,128)(2,1)S(1)} %bitcast.42), channel_id=1, source_target_pairs={{0,8},{4,12},{1,9},{5,13},{2,10},{6,14},{3,11},{7,15},{16,24},{20,... | collective-permute-start | bytes 786440 | tf_op jit(solution)/shard_map/ppermute | solution.py:272
  49.1 1.3 collective-permute-start.2
  50.4 3.2 %collective-permute-start.8 = (bf16[64,1024]{1,0:T(8,128)(2,1)S(1)}, bf16[64,1024]{1,0:T(8,128)(2,1)S(1)}, u32[]{:S(2)}, u32[]{:S(2)}) collective-permute-start(bf16[64,1024]{1,0:T(8,128)(2,1)S(1)} %get-tuple-element.30), channel_id=1, source_target_pairs={{0,113},{1,114},{2,115},{3,112},{16,1},{17,2},{18,3},{19,0},{32,17... | collective-permute-start | bytes 393224 | tf_op jit(solution)/shard_map/ppermute | solution.py:261
  53.7 3.7 %collective-permute-start.9 = (bf16[64,1024]{1,0:T(8,128)(2,1)S(1)}, bf16[64,1024]{1,0:T(8,128)(2,1)S(1)}, u32[]{:S(2)}, u32[]{:S(2)}) collective-permute-start(bf16[64,1024]{1,0:T(8,128)(2,1)S(1)} %get-tuple-element.31), channel_id=1, source_target_pairs={{0,114},{1,115},{2,112},{3,113},{16,2},{17,3},{18,0},{19,1},{32,18... | collective-permute-start | bytes 393224 | tf_op jit(solution)/shard_map/ppermute | solution.py:261
  57.4 12.4 %collective-permute-done.8.up1 = bf16[64,1024]{1,0:T(8,128)(2,1)S(1)} collective-permute-done((bf16[64,1024]{1,0:T(8,128)(2,1)S(1)}, bf16[64,1024]{1,0:T(8,128)(2,1)S(1)}, u32[]{:S(2)}, u32[]{:S(2)}) %collective-permute-start.8) | collective-permute-done | bytes 131104 | tf_op jit(solution)/shard_map/ppermute | solution.py:261
  69.8 3.0 %collective-permute-done.9.up2 = bf16[64,1024]{1,0:T(8,128)(2,1)S(1)} collective-permute-done((bf16[64,1024]{1,0:T(8,128)(2,1)S(1)}, bf16[64,1024]{1,0:T(8,128)(2,1)S(1)}, u32[]{:S(2)}, u32[]{:S(2)}) %collective-permute-start.9) | collective-permute-done | bytes 131104 | tf_op jit(solution)/shard_map/ppermute | solution.py:261
  72.8 8.0 %forward_second.1 = (bf16[256,1024]{1,0:T(8,128)(2,1)S(1)}, f32[8,256]{1,0:T(8,128)S(1)}, f32[4,8,256]{2,1,0:T(8,128)}) custom-call(s32[2]{0:T(128)S(1)} %pad_add_fusion.where, bf16[256,1024]{1,0:T(8,128)(2,1)S(1)} %bitcast.38, bf16[256,512]{1,0:T(8,128)(2,1)S(1)} %bitcast.44, bf16[256,512]{1,0:T(8,128)(2,1)S(1)} %collective-permute-done.kv1, ...), custom_call_target="tpu_custom_call" | custom-call | flops 1073741824 | bytes 4194304 | tf_op jit(solution)/shard_map/forward_second/pallas_call | solution.py:29
  80.8 7.3 %all-to-all-start.4 = ((f32[4,8,256]{2,1,0:T(8,128)}), f32[4,8,256]{2,1,0:T(8,128)S(1)}, u32[]{:S(2)}, u32[]{:S(2)}) async-start(f32[4,8,256]{2,1,0:T(8,128)} %get-tuple-element.35), calls=%async_computation.4 | async-start | bytes 65536 | tf_op jit(solution)/shard_map/all_to_all | solution.py:236
  88.1 1.4 reshape_squeeze.18
  89.5 1.0 copy.46
  90.5 2.1 %all-to-all-done.4.stats = f32[4,8,256]{2,1,0:T(8,128)S(1)} async-done(((f32[4,8,256]{2,1,0:T(8,128)}), f32[4,8,256]{2,1,0:T(8,128)S(1)}, u32[]{:S(2)}, u32[]{:S(2)}) %all-to-all-start.4) | async-done | bytes 32800 | tf_op jit(solution)/shard_map/all_to_all | solution.py:236
  92.6 3.7 %all-to-all-start = ((bf16[4,64,1024]{2,1,0:T(8,128)(2,1)}), bf16[4,64,1024]{2,1,0:T(8,128)(2,1)S(1)}, u32[]{:S(2)}, u32[]{:S(2)}) async-start(bf16[4,64,1024]{2,1,0:T(8,128)(2,1)} %bitcast.49), calls=%async_computation | async-start | bytes 1048576 | tf_op jit(solution)/shard_map/all_to_all | solution.py:236
  96.3 7.1 %backward.1 = (bf16[256,1024]{1,0:T(8,128)(2,1)}, f32[256,256]{1,0:T(8,128)S(1)}, bf16[256,256]{1,0:T(8,128)(2,1)}, bf16[256,256]{1,0:T(8,128)(2,1)}, bf16[256,256]{1,0:T(8,128)(2,1)}) custom-call(s32[2]{0:T(128)S(1)} %pad_add_fusion.where, bf16[256,1024]{1,0:T(8,128)(2,1)S(1)} %bitcast.39, bf16[256,512]{1,0:T(8,128)(2,1)S(1)} %bitcast.45, ...), custom_call_target="tpu_custom_call" | custom-call | flops 2684354560 | bytes 6291456 | tf_op jit(solution)/shard_map/backward/pallas_call | solution.py:29
  103.4 1.3 collective-permute-start.11
  104.7 1.3 collective-permute-start.12
  106.0 1.3 collective-permute-start.13
  107.3 2.8 %all-to-all-done = bf16[4,64,1024]{2,1,0:T(8,128)(2,1)S(1)} async-done(((bf16[4,64,1024]{2,1,0:T(8,128)(2,1)}), bf16[4,64,1024]{2,1,0:T(8,128)(2,1)S(1)}, u32[]{:S(2)}, u32[]{:S(2)}) %all-to-all-start) | async-done | bytes 524320 | tf_op jit(solution)/shard_map/all_to_all | solution.py:236
  110.0 0.9 copy-done.3
  111.0 0.9 copy-done.5
  111.9 7.8 %forward_first.1 = (bf16[256,1024]{1,0:T(8,128)(2,1)S(1)}, f32[4,8,256]{2,1,0:T(8,128)}) custom-call(s32[2]{0:T(128)S(1)} %pad_add_fusion.where, bf16[256,1024]{1,0:T(8,128)(2,1)S(1)} %bitcast.40, bf16[256,512]{1,0:T(8,128)(2,1)S(1)} %bitcast.46, bf16[256,512]{1,0:T(8,128)(2,1)S(1)} %collective-permute-done.kv1, bf16[256,512]{1,0:T(8,128)(2,1)S(1)} %copy-done.3, ...), custom_call_target="tpu_custom_call" | custom-call | flops 1073741824 | bytes 4194304 | tf_op jit(solution)/shard_map/forward_first/pallas_call | solution.py:29
  119.7 3.3 %all-to-all-start.2 = ((f32[4,8,256]{2,1,0:T(8,128)}), f32[4,8,256]{2,1,0:T(8,128)S(1)}, u32[]{:S(2)}, u32[]{:S(2)}) async-start(f32[4,8,256]{2,1,0:T(8,128)} %get-tuple-element.24), calls=%async_computation.2 | async-start | bytes 65536 | tf_op jit(solution)/shard_map/all_to_all | solution.py:236
  123.0 0.8 gain_rows.1
  123.8 3.7 %all-to-all-done.2.stats = f32[4,8,256]{2,1,0:T(8,128)S(1)} async-done(((f32[4,8,256]{2,1,0:T(8,128)}), f32[4,8,256]{2,1,0:T(8,128)S(1)}, u32[]{:S(2)}, u32[]{:S(2)}) %all-to-all-start.2) | async-done | bytes 32800 | tf_op jit(solution)/shard_map/all_to_all | solution.py:236
  127.5 0.6 broadcast_in_dim.12
  128.1 15.7 %all-to-all-start.7 = ((f32[16,2,128]{2,1,0:T(2,128)}), f32[16,2,128]{2,1,0:T(2,128)S(1)}, u32[]{:S(2)}, u32[]{:S(2)}) async-start(f32[16,2,128]{2,1,0:T(2,128)} %bitcast.16), calls=%async_computation.7 | async-start | bytes 32768 | tf_op jit(solution)/shard_map/all_to_all | solution.py:321
  143.9 1.1 add_convert_fusion
  145.0 12.5 %all-to-all-done.7 = f32[16,2,128]{2,1,0:T(2,128)S(1)} async-done(((f32[16,2,128]{2,1,0:T(2,128)}), f32[16,2,128]{2,1,0:T(2,128)S(1)}, u32[]{:S(2)}, u32[]{:S(2)}) %all-to-all-start.7) | async-done | bytes 16416 | tf_op jit(solution)/shard_map/all_to_all | solution.py:321
  157.5 7.1 %all_to_all.40 = bf16[4,64,256]{2,1,0:T(8,128)(2,1)S(1)} all-to-all(bf16[4,64,256]{2,1,0:T(8,128)(2,1)S(1)} %bitcast.51), channel_id=1, replica_groups=mesh['dp'=4,'pipe'=8,'zhi'=2,'yhi'=2,'ylo'=4] {'ylo'}, dimensions={0} | all-to-all | bytes 262144 | tf_op jit(solution)/shard_map/all_to_all | solution.py:236
  164.7 3.5 %all-to-all-start.5 = ((bf16[4,64,1024]{2,1,0:T(8,128)(2,1)}), bf16[4,64,1024]{2,1,0:T(8,128)(2,1)S(1)}, u32[]{:S(2)}, u32[]{:S(2)}) async-start(bf16[4,64,1024]{2,1,0:T(8,128)(2,1)} %bitcast.10), calls=%async_computation.5 | async-start | bytes 1048576 | tf_op jit(solution)/shard_map/all_to_all | solution.py:236
  168.2 0.8 normed.1
  169.0 12.0 %collective-permute-start.3 = (bf16[64,1024]{1,0:T(8,128)(2,1)S(1)}, bf16[64,1024]{1,0:T(8,128)(2,1)S(1)}, u32[]{:S(2)}, u32[]{:S(2)}) collective-permute-start(bf16[64,1024]{1,0:T(8,128)(2,1)S(1)} %get-tuple-element.25), channel_id=1, source_target_pairs={{0,16},{1,17},{2,18},{3,19},{16,32},{17,33},{18,34},{19,35},{32,48... | collective-permute-start | bytes 393224 | tf_op jit(solution)/shard_map/ppermute | solution.py:261
  180.9 3.4 %collective-permute-start.4 = (bf16[64,1024]{1,0:T(8,128)(2,1)S(1)}, bf16[64,1024]{1,0:T(8,128)(2,1)S(1)}, u32[]{:S(2)}, u32[]{:S(2)}) collective-permute-start(bf16[64,1024]{1,0:T(8,128)(2,1)S(1)} %get-tuple-element.26), channel_id=1, source_target_pairs={{0,17},{1,18},{2,19},{3,16},{16,33},{17,34},{18,35},{19,32},{32,49... | collective-permute-start | bytes 393224 | tf_op jit(solution)/shard_map/ppermute | solution.py:261
  184.3 2.8 %collective-permute-start.5 = (bf16[64,1024]{1,0:T(8,128)(2,1)S(1)}, bf16[64,1024]{1,0:T(8,128)(2,1)S(1)}, u32[]{:S(2)}, u32[]{:S(2)}) collective-permute-start(bf16[64,1024]{1,0:T(8,128)(2,1)S(1)} %get-tuple-element.27), channel_id=1, source_target_pairs={{0,18},{1,19},{2,16},{3,17},{16,34},{17,35},{18,32},{19,33},{32,50... | collective-permute-start | bytes 393224 | tf_op jit(solution)/shard_map/ppermute | solution.py:261
  187.2 2.8 %collective-permute-start.6 = (bf16[64,1024]{1,0:T(8,128)(2,1)S(1)}, bf16[64,1024]{1,0:T(8,128)(2,1)S(1)}, u32[]{:S(2)}, u32[]{:S(2)}) collective-permute-start(bf16[64,1024]{1,0:T(8,128)(2,1)S(1)} %get-tuple-element.28), channel_id=1, source_target_pairs={{0,19},{1,16},{2,17},{3,18},{16,35},{17,32},{18,33},{19,34},{32,51... | collective-permute-start | bytes 393224 | tf_op jit(solution)/shard_map/ppermute | solution.py:261
  190.0 0.7 collective-permute-start.14
  190.7 5.5 %collective-permute-done.5.p2 = bf16[64,1024]{1,0:T(8,128)(2,1)S(1)} collective-permute-done((bf16[64,1024]{1,0:T(8,128)(2,1)S(1)}, bf16[64,1024]{1,0:T(8,128)(2,1)S(1)}, u32[]{:S(2)}, u32[]{:S(2)}) %collective-permute-start.5) | collective-permute-done | bytes 131104 | tf_op jit(solution)/shard_map/ppermute | solution.py:261
  196.2 0.8 collective-permute-done.6.p3
  197.0 1.4 join.1
  198.4 0.1 copy.39
  198.5 0.7 broadcast_in_dim_reshape.10
  199.1 0.1 copy.40
  199.2 0.7 broadcast_in_dim_reshape.11
  199.9 0.4 copy.38
  200.3 1.2 broadcast_in_dim_reshape.9
  201.4 0.6 copy.48
  (34 shorter events, 0.2 us)
Async XLA Ops:
  0.6 56.7 %copy-start = (bf16[1,4096]{1,0:T(2,128)(2,1)S(1)}, bf16[1,4096]{1,0:T(2,128)(2,1)}, u32[]{:S(2)}) copy-start(bf16[1,4096]{1,0:T(2,128)(2,1)} %param.15) | copy-start | bytes 24580
  1.5 0.8 copy-start.7
  2.4 0.8 copy-start.8
  3.2 0.8 copy-start.9
  4.1 6.2 %copy-start.6 = (bf16[1,1,64,4096]{3,2,1,0:T(8,128)(2,1)S(1)}, bf16[1,1,64,4096]{3,2,1,0:T(8,128)(2,1)}, u32[]{:S(2)}) copy-start(bf16[1,1,64,4096]{3,2,1,0:T(8,128)(2,1)} %param.11) | copy-start | bytes 1572868
  4.9 11.0 %all-to-all-start.1 = ((bf16[4,64,512]{2,1,0:T(8,128)(2,1)}), bf16[4,64,512]{2,1,0:T(8,128)(2,1)S(1)}, u32[]{:S(2)}, u32[]{:S(2)}) async-start(bf16[4,64,512]{2,1,0:T(8,128)(2,1)} %maximum_bitcast_fusion), calls=%async_computation.1 | async-start | bytes 524288 | tf_op jit(solution)/shard_map/all_to_all | solution.py:236
  15.9 3.7 %copy-start.1 = (bf16[1,1,64,4096]{3,2,1,0:T(8,128)(2,1)S(1)}, bf16[1,1,64,4096]{3,2,1,0:T(8,128)(2,1)}, u32[]{:S(2)}) copy-start(bf16[1,1,64,4096]{3,2,1,0:T(8,128)(2,1)} %param.14) | copy-start | bytes 1572868
  15.9 56.8 %all-to-all-start.3 = ((bf16[4,64,1024]{2,1,0:T(8,128)(2,1)}), bf16[4,64,1024]{2,1,0:T(8,128)(2,1)S(1)}, u32[]{:S(2)}, u32[]{:S(2)}) async-start(bf16[4,64,1024]{2,1,0:T(8,128)(2,1)} %bitcast.35), calls=%async_computation.3 | async-start | bytes 1048576 | tf_op jit(solution)/shard_map/all_to_all | solution.py:236
  20.2 30.2 %collective-permute-start.10 = (bf16[64,1024]{1,0:T(8,128)(2,1)S(1)}, bf16[64,1024]{1,0:T(8,128)(2,1)S(1)}, u32[]{:S(2)}, u32[]{:S(2)}) collective-permute-start(bf16[64,1024]{1,0:T(8,128)(2,1)S(1)} %get-tuple-element.32), channel_id=1, source_target_pairs={{0,115},{1,112},{2,113},{3,114},{16,3},{17,0},{18,1},{19,2},{32,19... | collective-permute-start | bytes 393224 | tf_op jit(solution)/shard_map/ppermute | solution.py:261
  31.5 22.2 %collective-permute-start.7 = (bf16[64,1024]{1,0:T(8,128)(2,1)S(1)}, bf16[64,1024]{1,0:T(8,128)(2,1)S(1)}, u32[]{:S(2)}, u32[]{:S(2)}) collective-permute-start(bf16[64,1024]{1,0:T(8,128)(2,1)S(1)} %get-tuple-element.29), channel_id=1, source_target_pairs={{0,112},{1,113},{2,114},{3,115},{16,0},{17,1},{18,2},{19,3},{32,16... | collective-permute-start | bytes 393224 | tf_op jit(solution)/shard_map/ppermute | solution.py:261
  35.0 37.7 %collective-permute-start = (bf16[256,512]{1,0:T(8,128)(2,1)S(1)}, bf16[256,512]{1,0:T(8,128)(2,1)S(1)}, u32[]{:S(2)}, u32[]{:S(2)}) collective-permute-start(bf16[256,512]{1,0:T(8,128)(2,1)S(1)} %bitcast.41), channel_id=1, source_target_pairs={{0,4},{8,12},{1,5},{9,13},{2,6},{10,14},{3,7},{11,15},{16,20},{24,... | collective-permute-start | bytes 786440 | tf_op jit(solution)/shard_map/ppermute | solution.py:272
  41.2 31.6 %collective-permute-start.1 = (bf16[256,512]{1,0:T(8,128)(2,1)S(1)}, bf16[256,512]{1,0:T(8,128)(2,1)S(1)}, u32[]{:S(2)}, u32[]{:S(2)}) collective-permute-start(bf16[256,512]{1,0:T(8,128)(2,1)S(1)} %bitcast.42), channel_id=1, source_target_pairs={{0,8},{4,12},{1,9},{5,13},{2,10},{6,14},{3,11},{7,15},{16,24},{20,... | collective-permute-start | bytes 786440 | tf_op jit(solution)/shard_map/ppermute | solution.py:272
  49.1 23.6 %collective-permute-start.2 = (bf16[256,512]{1,0:T(8,128)(2,1)S(1)}, bf16[256,512]{1,0:T(8,128)(2,1)S(1)}, u32[]{:S(2)}, u32[]{:S(2)}) collective-permute-start(bf16[256,512]{1,0:T(8,128)(2,1)S(1)} %bitcast.43), channel_id=1, source_target_pairs={{4,8},{0,12},{5,9},{1,13},{6,10},{2,14},{7,11},{3,15},{20,24},{16,... | collective-permute-start | bytes 786440 | tf_op jit(solution)/shard_map/ppermute | solution.py:272
  50.4 19.3 %collective-permute-start.8 = (bf16[64,1024]{1,0:T(8,128)(2,1)S(1)}, bf16[64,1024]{1,0:T(8,128)(2,1)S(1)}, u32[]{:S(2)}, u32[]{:S(2)}) collective-permute-start(bf16[64,1024]{1,0:T(8,128)(2,1)S(1)} %get-tuple-element.30), channel_id=1, source_target_pairs={{0,113},{1,114},{2,115},{3,112},{16,1},{17,2},{18,3},{19,0},{32,17... | collective-permute-start | bytes 393224 | tf_op jit(solution)/shard_map/ppermute | solution.py:261
  53.7 19.1 %collective-permute-start.9 = (bf16[64,1024]{1,0:T(8,128)(2,1)S(1)}, bf16[64,1024]{1,0:T(8,128)(2,1)S(1)}, u32[]{:S(2)}, u32[]{:S(2)}) collective-permute-start(bf16[64,1024]{1,0:T(8,128)(2,1)S(1)} %get-tuple-element.31), channel_id=1, source_target_pairs={{0,114},{1,115},{2,112},{3,113},{16,2},{17,3},{18,0},{19,1},{32,18... | collective-permute-start | bytes 393224 | tf_op jit(solution)/shard_map/ppermute | solution.py:261
  72.7 23.5 %copy-start.2 = (bf16[256,512]{1,0:T(8,128)(2,1)}, bf16[256,512]{1,0:T(8,128)(2,1)S(1)}, u32[]{:S(2)}) copy-start(bf16[256,512]{1,0:T(8,128)(2,1)S(1)} %collective-permute-done.1.kv2) | copy-start | bytes 786436
  72.8 23.5 %copy-start.4 = (bf16[256,512]{1,0:T(8,128)(2,1)}, bf16[256,512]{1,0:T(8,128)(2,1)S(1)}, u32[]{:S(2)}) copy-start(bf16[256,512]{1,0:T(8,128)(2,1)S(1)} %collective-permute-done.2.kv3) | copy-start | bytes 786436
  80.8 11.8 %all-to-all-start.4 = ((f32[4,8,256]{2,1,0:T(8,128)}), f32[4,8,256]{2,1,0:T(8,128)S(1)}, u32[]{:S(2)}, u32[]{:S(2)}) async-start(f32[4,8,256]{2,1,0:T(8,128)} %get-tuple-element.35), calls=%async_computation.4 | async-start | bytes 65536 | tf_op jit(solution)/shard_map/all_to_all | solution.py:236
  92.6 17.4 %all-to-all-start = ((bf16[4,64,1024]{2,1,0:T(8,128)(2,1)}), bf16[4,64,1024]{2,1,0:T(8,128)(2,1)S(1)}, u32[]{:S(2)}, u32[]{:S(2)}) async-start(bf16[4,64,1024]{2,1,0:T(8,128)(2,1)} %bitcast.49), calls=%async_computation | async-start | bytes 1048576 | tf_op jit(solution)/shard_map/all_to_all | solution.py:236
  103.4 40.5 %collective-permute-start.11 = (bf16[256,256]{1,0:T(8,128)(2,1)}, bf16[256,256]{1,0:T(8,128)(2,1)}, u32[]{:S(2)}, u32[]{:S(2)}) collective-permute-start(bf16[256,256]{1,0:T(8,128)(2,1)} %get-tuple-element.38), channel_id=1, source_target_pairs={{4,0},{12,8},{5,1},{13,9},{6,2},{14,10},{7,3},{15,11},{20,16},{28,... | collective-permute-start | bytes 393224 | tf_op jit(solution)/shard_map/ppermute | solution.py:343
  104.7 39.2 %collective-permute-start.12 = (bf16[256,256]{1,0:T(8,128)(2,1)}, bf16[256,256]{1,0:T(8,128)(2,1)}, u32[]{:S(2)}, u32[]{:S(2)}) collective-permute-start(bf16[256,256]{1,0:T(8,128)(2,1)} %get-tuple-element.39), channel_id=1, source_target_pairs={{8,0},{12,4},{9,1},{13,5},{10,2},{14,6},{11,3},{15,7},{24,16},{28,... | collective-permute-start | bytes 393224 | tf_op jit(solution)/shard_map/ppermute | solution.py:343
  106.0 37.9 %collective-permute-start.13 = (bf16[256,256]{1,0:T(8,128)(2,1)}, bf16[256,256]{1,0:T(8,128)(2,1)}, u32[]{:S(2)}, u32[]{:S(2)}) collective-permute-start(bf16[256,256]{1,0:T(8,128)(2,1)} %get-tuple-element.40), channel_id=1, source_target_pairs={{8,4},{12,0},{9,5},{13,1},{10,6},{14,2},{11,7},{15,3},{24,20},{28,... | collective-permute-start | bytes 393224 | tf_op jit(solution)/shard_map/ppermute | solution.py:343
  110.0 1.0 copy-start.3
  111.0 0.9 copy-start.5
  119.7 7.7 %all-to-all-start.2 = ((f32[4,8,256]{2,1,0:T(8,128)}), f32[4,8,256]{2,1,0:T(8,128)S(1)}, u32[]{:S(2)}, u32[]{:S(2)}) async-start(f32[4,8,256]{2,1,0:T(8,128)} %get-tuple-element.24), calls=%async_computation.2 | async-start | bytes 65536 | tf_op jit(solution)/shard_map/all_to_all | solution.py:236
  128.1 29.4 %all-to-all-start.7 = ((f32[16,2,128]{2,1,0:T(2,128)}), f32[16,2,128]{2,1,0:T(2,128)S(1)}, u32[]{:S(2)}, u32[]{:S(2)}) async-start(f32[16,2,128]{2,1,0:T(2,128)} %bitcast.16), calls=%async_computation.7 | async-start | bytes 32768 | tf_op jit(solution)/shard_map/all_to_all | solution.py:321
  164.7 35.2 %all-to-all-start.5 = ((bf16[4,64,1024]{2,1,0:T(8,128)(2,1)}), bf16[4,64,1024]{2,1,0:T(8,128)(2,1)S(1)}, u32[]{:S(2)}, u32[]{:S(2)}) async-start(bf16[4,64,1024]{2,1,0:T(8,128)(2,1)} %bitcast.10), calls=%async_computation.5 | async-start | bytes 1048576 | tf_op jit(solution)/shard_map/all_to_all | solution.py:236
  169.0 21.7 %collective-permute-start.3 = (bf16[64,1024]{1,0:T(8,128)(2,1)S(1)}, bf16[64,1024]{1,0:T(8,128)(2,1)S(1)}, u32[]{:S(2)}, u32[]{:S(2)}) collective-permute-start(bf16[64,1024]{1,0:T(8,128)(2,1)S(1)} %get-tuple-element.25), channel_id=1, source_target_pairs={{0,16},{1,17},{2,18},{3,19},{16,32},{17,33},{18,34},{19,35},{32,48... | collective-permute-start | bytes 393224 | tf_op jit(solution)/shard_map/ppermute | solution.py:261
  180.9 9.8 %collective-permute-start.4 = (bf16[64,1024]{1,0:T(8,128)(2,1)S(1)}, bf16[64,1024]{1,0:T(8,128)(2,1)S(1)}, u32[]{:S(2)}, u32[]{:S(2)}) collective-permute-start(bf16[64,1024]{1,0:T(8,128)(2,1)S(1)} %get-tuple-element.26), channel_id=1, source_target_pairs={{0,17},{1,18},{2,19},{3,16},{16,33},{17,34},{18,35},{19,32},{32,49... | collective-permute-start | bytes 393224 | tf_op jit(solution)/shard_map/ppermute | solution.py:261
  184.3 11.8 %collective-permute-start.5 = (bf16[64,1024]{1,0:T(8,128)(2,1)S(1)}, bf16[64,1024]{1,0:T(8,128)(2,1)S(1)}, u32[]{:S(2)}, u32[]{:S(2)}) collective-permute-start(bf16[64,1024]{1,0:T(8,128)(2,1)S(1)} %get-tuple-element.27), channel_id=1, source_target_pairs={{0,18},{1,19},{2,16},{3,17},{16,34},{17,35},{18,32},{19,33},{32,50... | collective-permute-start | bytes 393224 | tf_op jit(solution)/shard_map/ppermute | solution.py:261
  187.2 9.9 %collective-permute-start.6 = (bf16[64,1024]{1,0:T(8,128)(2,1)S(1)}, bf16[64,1024]{1,0:T(8,128)(2,1)S(1)}, u32[]{:S(2)}, u32[]{:S(2)}) collective-permute-start(bf16[64,1024]{1,0:T(8,128)(2,1)S(1)} %get-tuple-element.28), channel_id=1, source_target_pairs={{0,19},{1,16},{2,17},{3,18},{16,35},{17,32},{18,33},{19,34},{32,51... | collective-permute-start | bytes 393224 | tf_op jit(solution)/shard_map/ppermute | solution.py:261
  190.0 0.7 collective-permute-start.14

commit v2 on v0

v2 whole, which is shorter than its diff:
```python
import functools
import math

import jax
import jax.numpy as jnp
from jax import lax
from jax.experimental import pallas as pl
from jax.experimental.pallas import tpu as pltpu
from jax.sharding import Mesh
from jax.sharding import PartitionSpec as P

HD = 128
EPSILON = 1e-05
SCALE = 1.0 / math.sqrt(HD)
F32 = jnp.float32
BF16 = jnp.bfloat16

ROW = ("yhi", "ylo")
SEQ = ("zhi", "yhi", "ylo")
FOUR = 4

VMEM = pl.BlockSpec(memory_space=pltpu.VMEM)
SMEM = pl.BlockSpec(memory_space=pltpu.SMEM)


def call(body, outs, inputs, scratch=(), micros=1.0, name=None):
    return pl.pallas_call(
        body,
        out_shape=outs,
        in_specs=[SMEM] + [VMEM] * (len(inputs) - 1),
        out_specs=jax.tree.map(lambda _: VMEM, outs),
        scratch_shapes=list(scratch),
        compiler_params=pltpu.CompilerParams(vmem_limit_bytes=48 * 1024 * 1024),
        cost_estimate=pl.CostEstimate(
            flops=int(micros * 1e9), bytes_accessed=0, transcendentals=0
        ),
        name=name,
    )(*inputs)


def sds(shape, dtype):
    return jax.ShapeDtypeStruct(shape, dtype)


def dot_nt(a, b):
    return lax.dot_general(a, b, (((1,), (1,)), ((), ())), preferred_element_type=F32)


def dot_nn(a, b):
    return lax.dot_general(a, b, (((1,), (0,)), ((), ())), preferred_element_type=F32)


def column(row):
    return jnp.broadcast_to(row, (HD, row.shape[1])).T


def row_of(block):
    return jnp.sum(block.T, axis=0, keepdims=True)


def attend(keys, values_t, bias, queries):
    scores = dot_nt(keys, queries) + bias[...]
    highest = jnp.max(scores, axis=0, keepdims=True)
    exponent = jnp.exp((scores - highest) * SCALE)
    total = jnp.sum(exponent, axis=0, keepdims=True)
    out = dot_nn(values_t, exponent.astype(BF16)) * (1.0 / total)
    return out.T.astype(BF16), highest * SCALE + jnp.log(total)


def set_bias(where, bias):
    shape = bias.shape
    ahead = lax.broadcasted_iota(jnp.int32, shape, 0) - lax.broadcasted_iota(jnp.int32, shape, 1)
    bias[...] = jnp.where(ahead <= where[0] * shape[1], 0.0, -jnp.inf).astype(F32)


def assemble(where, pieces, full):
    rows = pieces[0].shape[0]
    for k, piece in enumerate(pieces):
        at = pl.multiple_of(lax.rem(where[2] - k + FOUR, FOUR) * rows, rows)
        full[pl.ds(at, rows), :] = piece[...]


def open_body(where, query, keys, values, kv, q0, q1, q2, q3):
    for s in range(kv.shape[0]):
        cols = slice((s % FOUR) * HD, (s % FOUR + 1) * HD)
        kv[s, :, :HD] = keys[:, cols]
        kv[s, :, HD:] = values[:, cols]
    width = q0.shape[1]
    for k, out in enumerate((q0, q1, q2, q3)):
        at = pl.multiple_of(lax.rem(where[2] + k, FOUR) * width, width)
        out[...] = query[:, pl.ds(at, width)]


def pack_body(where, full, out):
    width = out.shape[2]
    for place in range(FOUR):
        out[place] = full[:, place * width : (place + 1) * width]


def join_body(where, p0, p1, p2, p3, out):
    width = p0.shape[1]
    for k, piece in enumerate((p0, p1, p2, p3)):
        at = pl.multiple_of(lax.rem(where[2] - k + FOUR, FOUR) * width, width)
        out[:, pl.ds(at, width)] = piece[...]


def gather_body(where, parts, keys, values, share):
    tokens = keys.shape[0]
    for h in range(FOUR):
        cols = slice(h * HD, (h + 1) * HD)
        total = parts[h, :tokens].astype(F32)
        for s in range(h + FOUR, parts.shape[0], FOUR):
            total = total + parts[s, :tokens].astype(F32)
        keys[:, cols] = total[:, :HD].astype(BF16)
        values[:, cols] = total[:, HD:].astype(BF16)
    terms = parts[0, tokens:].astype(F32)
    for s in range(1, parts.shape[0]):
        terms = terms + parts[s, tokens:].astype(F32)
    share[...] = terms[0:1] + terms[1:2] + terms[2:3]


def forward_body(heads, where, q0, q1, q2, q3, kv, out, lse, q_s, vt_s, bias):
    assemble(where, (q0, q1, q2, q3), q_s)
    set_bias(where, bias)
    vt_s[...] = kv[:, HD:].T
    for h in range(heads):
        cols = slice(h * HD, (h + 1) * HD)
        out[:, cols], lse[h : h + 1, :] = attend(kv[:, :HD], vt_s[...], bias, q_s[:, cols])


def stats_body(heads, where, act, up, gain, stats):
    n = act.shape[0]
    square = jnp.zeros((n, HD), F32)
    cross = jnp.zeros((n, HD), F32)
    for h in range(heads):
        cols = slice(h * HD, (h + 1) * HD)
        value = act[:, cols].astype(F32)
        square = square + value * value
        cross = cross + gain[:, cols].astype(F32) * up[:, cols].astype(F32) * value
    rows = jnp.concatenate(
        [row_of(square), row_of(cross), jnp.zeros((stats.shape[1] - 2, n), F32)], axis=0
    )
    for place in range(FOUR):
        stats[place] = rows


def backward_body(
    heads, width, where, q0, q1, q2, q3, kv, up, gain, act, lse, stats,
    dq0, dq1, dq2, dq3, dkv, q_s, kt_s, bias, dk_s, dv_s, dq_s,
):
    assemble(where, (q0, q1, q2, q3), q_s)
    set_bias(where, bias)
    kt_s[...] = kv[:, :HD].T
    totals = (stats[0] + stats[1]) + (stats[2] + stats[3])
    inverse_row = lax.rsqrt(totals[0:1] / width + EPSILON)
    inverse = column(inverse_row)
    shrink = column(inverse_row * inverse_row * inverse_row * (totals[1:2] / width))
    sums = []
    for h in range(heads):
        cols = slice(h * HD, (h + 1) * HD)
        queries = q_s[:, cols]
        act_h = act[:, cols].astype(F32)
        upstream = up[:, cols].astype(F32)
        sums.append(jnp.sum(upstream * act_h * inverse, axis=0, keepdims=True))
        grad = (gain[:, cols].astype(F32) * upstream * inverse - act_h * shrink).astype(BF16)
        dots = row_of(grad.astype(F32) * act_h)
        scores = dot_nt(kv[:, :HD], queries) * SCALE + bias[...]
        probs = jnp.exp(scores - lse[h : h + 1, :])
        grad_weights = dot_nt(kv[:, HD:], grad)
        grad_scores = (probs * (grad_weights - dots) * SCALE).astype(BF16)
        dv = dot_nn(probs.astype(BF16), grad)
        dk = dot_nn(grad_scores, queries)
        if h == 0:
            dv_s[...] = dv
            dk_s[...] = dk
        else:
            dv_s[...] += dv
            dk_s[...] += dk
        dq_s[:, cols] = dot_nn(kt_s[...], grad_scores).T.astype(BF16)
    tokens = dq0.shape[0]
    for k, out in enumerate((dq0, dq1, dq2, dq3)):
        at = pl.multiple_of(lax.rem(where[2] + k, FOUR) * tokens, tokens)
        out[...] = dq_s[pl.ds(at, tokens), :]
    per = heads // FOUR
    extra = dkv.shape[1] - tokens
    for s in range(dkv.shape[0]):
        rows = slice(s * tokens, (s + 1) * tokens)
        dkv[s, :tokens, :HD] = dk_s[rows].astype(BF16)
        dkv[s, :tokens, HD:] = dv_s[rows].astype(BF16)
        j = s % FOUR
        value = jnp.concatenate(sums[j * per : (j + 1) * per], axis=1)
        value = jnp.where(where[2] == s // FOUR, value, 0.0)
        terms = []
        for _ in range(3):
            term = value.astype(BF16).astype(F32)
            terms.append(term)
            value = value - term
        terms.append(jnp.zeros((extra - 3, value.shape[1]), F32))
        dkv[s, tokens:] = jnp.concatenate(terms, axis=0).astype(BF16)


def first_body(where, q, kv, gain, out, k_s, vt_s, q_s, o_s, bias):
    tokens, width = q.shape
    length = kv.shape[0]
    kv_heads = kv.shape[1] // (2 * HD)
    heads = width // HD
    n = bias.shape[1]
    together = n // tokens
    ids = lax.broadcasted_iota(jnp.int32, (length, n), 0)
    query_ids = lax.broadcasted_iota(jnp.int32, (length, n), 1) % tokens
    block = ids // tokens
    half = (block % 2 + where[1]) % 2
    key_at = half * (length // 2) + (block // 2) * tokens + ids % tokens
    query_at = where[1] * (length // 2) + where[3] * tokens + query_ids
    bias[...] = jnp.where(key_at <= query_at, 0.0, -jnp.inf).astype(F32)
    square = jnp.zeros((tokens, HD), F32)
    for g in range(kv_heads):
        k_s[...] = kv[:, g * HD : (g + 1) * HD]
        vt_s[...] = kv[:, (kv_heads + g) * HD : (kv_heads + g + 1) * HD].T
        for part in range(heads // kv_heads // together):
            start = g * (heads // kv_heads) + part * together
            for i in range(together):
                q_s[i * tokens : (i + 1) * tokens, :] = q[:, (start + i) * HD : (start + i + 1) * HD]
            result, _ = attend(k_s[...], vt_s[...], bias, q_s[...])
            for i in range(together):
                piece = result[i * tokens : (i + 1) * tokens]
                o_s[:, (start + i) * HD : (start + i + 1) * HD] = piece
                piece = piece.astype(F32)
                square = square + piece * piece
    mean = jnp.sum(square, axis=1, keepdims=True) / width
    inverse = jnp.broadcast_to(lax.rsqrt(mean + EPSILON), (tokens, HD))
    for h in range(heads):
        cols = slice(h * HD, (h + 1) * HD)
        out[:, cols] = (gain[:, cols].astype(F32) * o_s[:, cols].astype(F32) * inverse).astype(BF16)


def local(
    query_first, key_first, value_first, query_second, key_second, value_second, grad_output, gain
):
    tokens, width = query_first.shape[2:]
    kv_width = key_first.shape[3]
    n = tokens * FOUR
    cols = width // FOUR
    heads = cols // HD
    places = lax.axis_size(SEQ)
    length = tokens * places
    pipes = lax.axis_size("pipe")
    zhi, yhi, ylo = (lax.axis_index(axis) for axis in SEQ)
    where = jnp.stack([zhi * 2 + yhi, zhi, ylo, yhi * FOUR + ylo]).astype(jnp.int32)
    gain_cols = lax.dynamic_slice_in_dim(gain, ylo * cols, cols, 1)

    def swap(packed, axes):
        return lax.all_to_all(packed, axes, split_axis=0, concat_axis=0, tiled=True)

    def along(value, axis, step, count):
        return lax.ppermute(value, axis, [(i, (i + step) % count) for i in range(count)])

    def ahead(pieces):
        return [pieces[0]] + [along(pieces[k], "ylo", k, FOUR) for k in range(1, FOUR)]

    piece = sds((tokens, cols), BF16)
    kv1 = jnp.concatenate([key_first[0, 0], value_first[0, 0]], axis=1)
    other = lax.ppermute(kv1, "zhi", [(0, 1)])
    up_raw = along(grad_output[0, 0], "pipe", -1, pipes)
    packed, *q2 = call(
        open_body,
        (sds((places, tokens, 2 * HD), BF16),) + (piece,) * 4,
        (where, query_second[0, 0], key_second[0, 0], value_second[0, 0]),
        name="open_second",
    )
    kv1, other, packed = lax.optimization_barrier((kv1, other, packed))
    kv = swap(packed, SEQ).reshape(length, 2 * HD)
    q2 = ahead(q2)
    up = call(pack_body, sds((FOUR, tokens, cols), BF16), (where, up_raw), name="pack")
    kv, up, q2 = lax.optimization_barrier((kv, up, q2))
    up = swap(up, "ylo").reshape(n, cols)
    kv_first = lax.all_gather(
        jnp.concatenate([kv1, other], axis=0), ROW, axis=0, tiled=True
    )

    turned = pltpu.VMEM((HD, length), BF16)
    bias = pltpu.VMEM((length, n), F32)
    rows = pltpu.VMEM((n, cols), BF16)
    total = pltpu.VMEM((length, HD), F32)

    out2, lse = call(
        functools.partial(forward_body, heads),
        (sds((n, cols), BF16), sds((heads, n), F32)),
        (where, *q2, kv),
        [rows, turned, bias],
        micros=6.4,
        name="forward_second",
    )
    stats = swap(
        call(
            functools.partial(stats_body, heads),
            sds((FOUR, 8, n), F32),
            (where, out2, up, gain_cols),
            name="stats",
        ),
        "ylo",
    )
    *dq, dkv = call(
        functools.partial(backward_body, heads, width),
        (piece,) * 4 + (sds((places, tokens + 16, 2 * HD), BF16),),
        (where, *q2, kv, up, gain_cols, out2, lse, stats),
        [rows, turned, bias, total, total, rows],
        micros=7.0,
        name="backward",
    )
    dkv = swap(dkv, SEQ)
    dq = ahead(dq)

    normed = call(
        first_body,
        sds((tokens, width), BF16),
        (where, query_first[0, 0], kv_first, gain),
        [
            pltpu.VMEM((length, HD), BF16),
            turned,
            pltpu.VMEM((n, HD), BF16),
            pltpu.VMEM((tokens, width), BF16),
            bias,
        ],
        micros=7.0,
        name="forward_first",
    )
    next_input = along(normed, "pipe", 1, pipes)

    dkv, normed, dq = lax.optimization_barrier((dkv, normed, dq))
    grad_key, grad_value, share = call(
        gather_body,
        (sds((tokens, kv_width), BF16),) * 2 + (sds((1, 2 * HD), F32),),
        (where, dkv),
        name="gather",
    )
    grad_gain = lax.psum(share, "dp")
    grad_query = call(join_body, sds((tokens, width), BF16), (where, *dq), name="join")
    return (
        next_input[None, None],
        grad_query[None, None],
        grad_key[None, None],
        grad_value[None, None],
        grad_gain,
    )


def solution(mesh):
    shape = mesh.devices.shape
    fine = Mesh(
        mesh.devices.reshape(shape[0], shape[1], 2, 2, shape[2] // 4),
        ("dp", "pipe", "zhi", "yhi", "ylo"),
    )
    big = P("dp", "pipe", SEQ, None)
    return jax.shard_map(
        local,
        mesh=fine,
        in_specs=(big,) * 7 + (P("pipe", None),),
        out_specs=(big,) * 4 + (P("pipe", SEQ),),
        check_vma=False,
    )
```

time: 674 us -> 169 us (0.25)
  the two profiles are of different devices: /device:TPU:2 before, /device:TPU:1 now
where the time goes in v2:
time: 169 us; the launch traced here: 167 us
  starting transfers between devices  74.2 us (44%)
  Pallas kernels  27.3 us (16%)
  waiting for transfers between devices  27.3 us (16%)
  blocking collectives  17.3 us (10%)
  between operations  14.2 us (8%)
  local copies, waits for them, and re-layouts  5.12 us (3%)
    ppermute x8, starting transfers between devices, along(): lax.ppermute(value, axis, [(i, (i + step) % count) for i in range(count)])  34.6 us
    all_to_all x3, starting transfers between devices, swap(): return lax.all_to_all(packed, axes, split_axis=0, concat_axis=0, tiled=True)  28.1 us
    pallas_call x8, Pallas kernels, call(): pl.pallas_call(body, out_shape=outs, in_specs=[SMEM] + [VMEM] * (len(inpu...  27.3 us
    ppermute x8, waiting for transfers between devices, along(): lax.ppermute(value, axis, [(i, (i + step) % count) for i in range(count)])  16.3 us
    ppermute x1, starting transfers between devices, local(): other = lax.ppermute(kv1, 'zhi', [(0, 1)])  11.5 us
    all_to_all x3, waiting for transfers between devices, swap(): return lax.all_to_all(packed, axes, split_axis=0, concat_axis=0, tiled=True)  11 us
    psum x1, blocking collectives, local(): grad_gain = lax.psum(share, 'dp')  8.99 us
    all_to_all x1, blocking collectives, swap(): return lax.all_to_all(packed, axes, split_axis=0, concat_axis=0, tiled=True)  8.36 us
  transfers between devices with their start and end apart: 13, of which 6 were waited for; matrix products, arithmetic and copies ran while one was open for 0% of the time, Pallas kernels for 16%

profile of v2, /device:TPU:1, one launch (start us, length us, event | category | flops | bytes accessed | tf_op | source)
XLA Modules:
  0.0 167.2 jit_solution(211427316645106361)
XLA Ops:
  7.2 0.0 all-gather.2.cloned.1.call-start
  7.2 0.9 pad_maximum_fusion.1
  8.1 11.5 %collective-permute-start = (bf16[64,1024]{1,0:T(8,128)(2,1)S(1)}, bf16[64,1024]{1,0:T(8,128)(2,1)S(1)}, u32[]{:S(2)}, u32[]{:S(2)}) collective-permute-start(bf16[64,1024]{1,0:T(8,128)(2,1)S(1)} %pad_maximum_fusion.1), channel_id=1, source_target_pairs={{0,8},{1,9},{2,10},{3,11},{4,12},{5,13},{6,14},{7,15},{16,24},{17,... | collective-permute-start | bytes 393224 | tf_op jit(solution)/shard_map/ppermute | solution.py:263
  19.6 0.1 pad_add_fusion.where
  19.7 0.0 copy-start.2
  19.7 1.0 copy-done.2
  20.7 0.0 copy-start.4
  20.7 0.8 copy-done.4
  21.5 0.0 copy-start.5
  21.5 0.8 copy-done.5
  22.4 0.0 copy-start.6
  22.4 1.4 open_second.1
  23.8 0.0 collective-permute-done
  23.8 0.7 pad_maximum_fusion
  24.5 0.0 all-gather.2.cloned.1.call-update
  24.5 10.7 %all-to-all-start = ((bf16[16,64,256]{2,1,0:T(8,128)(2,1)}), bf16[16,64,256]{2,1,0:T(8,128)(2,1)S(1)}, u32[]{:S(2)}, u32[]{:S(2)}) async-start(bf16[16,64,256]{2,1,0:T(8,128)(2,1)} %get-tuple-element.37), calls=%async_computation | async-start | bytes 1048576 | tf_op jit(solution)/shard_map/all_to_all | solution.py:253
  35.2 0.0 copy-done.6
  35.2 3.8 %collective-permute-start.2 = (bf16[64,4096]{1,0:T(8,128)(2,1)S(1)}, bf16[64,4096]{1,0:T(8,128)(2,1)S(1)}, u32[]{:S(2)}, u32[]{:S(2)}) collective-permute-start(bf16[64,4096]{1,0:T(8,128)(2,1)S(1)} %bitcast.28), channel_id=1, source_target_pairs={{0,112},{16,0},{32,16},{48,32},{64,48},{80,64},{96,80},{112,96},{1... | collective-permute-start | bytes 1572872 | tf_op jit(solution)/shard_map/ppermute | solution.py:256
  39.1 3.5 %collective-permute-start.3 = (bf16[64,1024]{1,0:T(8,128)(2,1)S(1)}, bf16[64,1024]{1,0:T(8,128)(2,1)S(1)}, u32[]{:S(2)}, u32[]{:S(2)}) collective-permute-start(bf16[64,1024]{1,0:T(8,128)(2,1)S(1)} %get-tuple-element.39), channel_id=1, source_target_pairs={{0,1},{1,2},{2,3},{3,0},{4,5},{5,6},{6,7},{7,4},{8,9},{9,10},{10,1... | collective-permute-start | bytes 393224 | tf_op jit(solution)/shard_map/ppermute | solution.py:256
  42.6 4.0 %collective-permute-start.4 = (bf16[64,1024]{1,0:T(8,128)(2,1)S(1)}, bf16[64,1024]{1,0:T(8,128)(2,1)S(1)}, u32[]{:S(2)}, u32[]{:S(2)}) collective-permute-start(bf16[64,1024]{1,0:T(8,128)(2,1)S(1)} %get-tuple-element.40), channel_id=1, source_target_pairs={{0,2},{1,3},{2,0},{3,1},{4,6},{5,7},{6,4},{7,5},{8,10},{9,11},{10,... | collective-permute-start | bytes 393224 | tf_op jit(solution)/shard_map/ppermute | solution.py:256
  46.6 0.0 copy-start
  46.6 3.1 %collective-permute-start.5 = (bf16[64,1024]{1,0:T(8,128)(2,1)S(1)}, bf16[64,1024]{1,0:T(8,128)(2,1)S(1)}, u32[]{:S(2)}, u32[]{:S(2)}) collective-permute-start(bf16[64,1024]{1,0:T(8,128)(2,1)S(1)} %get-tuple-element.41), channel_id=1, source_target_pairs={{0,3},{1,0},{2,1},{3,2},{4,7},{5,4},{6,5},{7,6},{8,11},{9,8},{10,9... | collective-permute-start | bytes 393224 | tf_op jit(solution)/shard_map/ppermute | solution.py:256
  49.7 6.8 %collective-permute-done.2.full = bf16[64,4096]{1,0:T(8,128)(2,1)S(1)} collective-permute-done((bf16[64,4096]{1,0:T(8,128)(2,1)S(1)}, bf16[64,4096]{1,0:T(8,128)(2,1)S(1)}, u32[]{:S(2)}, u32[]{:S(2)}) %collective-permute-start.2) | collective-permute-done | bytes 524320 | tf_op jit(solution)/shard_map/ppermute | solution.py:256
  56.5 1.4 pack.1
  57.9 0.0 collective-permute-done.3.q1
  57.9 0.3 collective-permute-done.4.q2
  58.2 3.7 %collective-permute-done.5.q3 = bf16[64,1024]{1,0:T(8,128)(2,1)S(1)} collective-permute-done((bf16[64,1024]{1,0:T(8,128)(2,1)S(1)}, bf16[64,1024]{1,0:T(8,128)(2,1)S(1)}, u32[]{:S(2)}, u32[]{:S(2)}) %collective-permute-start.5) | collective-permute-done | bytes 131104 | tf_op jit(solution)/shard_map/ppermute | solution.py:256
  61.9 0.0 all-to-all-done
  61.9 7.4 %all-to-all-start.1 = ((bf16[4,64,1024]{2,1,0:T(8,128)(2,1)}), bf16[4,64,1024]{2,1,0:T(8,128)(2,1)S(1)}, u32[]{:S(2)}, u32[]{:S(2)}) async-start(bf16[4,64,1024]{2,1,0:T(8,128)(2,1)} %pack.1), calls=%async_computation.1 | async-start | bytes 1048576 | tf_op jit(solution)/shard_map/all_to_all | solution.py:253
  69.3 0.0 copy-done
  69.3 6.5 %forward_second.1 = (bf16[256,1024]{1,0:T(8,128)(2,1)S(1)}, f32[8,256]{1,0:T(8,128)S(1)}) custom-call(s32[4]{0:T(128)S(1)} %pad_add_fusion.where, bf16[64,1024]{1,0:T(8,128)(2,1)S(1)} %get-tuple-element.42.q0, bf16[64,1024]{1,0:T(8,128)(2,1)S(1)} %collective-permute-done.3.q1, bf16[64,1024]{1,0:T(8,128)(2,1)S(1)} %collective-permute-done.4.q2, ...), custom_call_target="tpu_custom_call" | custom-call | flops 6400000000 | tf_op jit(solution)/shard_map/forward_second/pallas_call | solution.py:27
  75.9 11.0 %all-to-all-done.1 = bf16[4,64,1024]{2,1,0:T(8,128)(2,1)S(1)} async-done(((bf16[4,64,1024]{2,1,0:T(8,128)(2,1)}), bf16[4,64,1024]{2,1,0:T(8,128)(2,1)S(1)}, u32[]{:S(2)}, u32[]{:S(2)}) %all-to-all-start.1) | async-done | bytes 524320 | tf_op jit(solution)/shard_map/all_to_all | solution.py:253
  86.8 0.8 stats.1
  87.7 8.4 %all_to_all.20.stats = f32[4,8,256]{2,1,0:T(8,128)S(1)} all-to-all(f32[4,8,256]{2,1,0:T(8,128)S(1)} %stats.1), channel_id=1, replica_groups=mesh['dp'=4,'pipe'=8,'zhi'=2,'yhi'=2,'ylo'=4] {'ylo'}, dimensions={0} | all-to-all | bytes 65536 | tf_op jit(solution)/shard_map/all_to_all | solution.py:253
  96.1 0.0 copy-start.3
  96.1 7.4 %backward.1 = (bf16[64,1024]{1,0:T(8,128)(2,1)S(1)}, bf16[64,1024]{1,0:T(8,128)(2,1)S(1)}, bf16[64,1024]{1,0:T(8,128)(2,1)S(1)}, bf16[64,1024]{1,0:T(8,128)(2,1)S(1)}, bf16[16,80,256]{2,1,0:T(8,128)(2,1)}) custom-call(s32[4]{0:T(128)S(1)} %pad_add_fusion.where, bf16[64,1024]{1,0:T(8,128)(2,1)S(1)} %get-tuple-element.42.q0, ...), custom_call_target="tpu_custom_call" | custom-call | flops 7000000000 | tf_op jit(solution)/shard_map/backward/pallas_call | solution.py:27
  103.4 10.0 %all-to-all-start.3 = ((bf16[16,80,256]{2,1,0:T(8,128)(2,1)}), bf16[16,80,256]{2,1,0:T(8,128)(2,1)S(1)}, u32[]{:S(2)}, u32[]{:S(2)}) async-start(bf16[16,80,256]{2,1,0:T(8,128)(2,1)} %get-tuple-element.50), calls=%async_computation.3 | async-start | bytes 1310720 | tf_op jit(solution)/shard_map/all_to_all | solution.py:253
  113.5 0.0 all-gather.2.cloned.1.call-done.kv
  113.5 0.0 copy-done.3
  113.5 0.0 copy-start.1
  113.5 1.6 copy-done.1
  115.1 7.1 %forward_first.1 = bf16[64,4096]{1,0:T(8,128)(2,1)S(1)} custom-call(s32[4]{0:T(128)S(1)} %pad_add_fusion.where, bf16[64,4096]{1,0:T(8,128)(2,1)S(1)} %bitcast.22, bf16[1024,1024]{1,0:T(8,128)(2,1)S(1)} %copy-done.1, bf16[1,4096]{1,0:T(2,128)(2,1)S(1)} %copy-done), custom_call_target="tpu_custom_call" | custom-call | flops 7000000000 | tf_op jit(solution)/shard_map/forward_first/pallas_call | solution.py:27
  122.2 9.5 %collective-permute-start.1 = (bf16[64,4096]{1,0:T(8,128)(2,1)S(1)}, bf16[64,4096]{1,0:T(8,128)(2,1)S(1)}, u32[]{:S(2)}, u32[]{:S(2)}) collective-permute-start(bf16[64,4096]{1,0:T(8,128)(2,1)S(1)} %forward_first.1), channel_id=1, source_target_pairs={{0,16},{16,32},{32,48},{48,64},{64,80},{80,96},{96,112},{112,0},{1... | collective-permute-start | bytes 1572872 | tf_op jit(solution)/shard_map/ppermute | solution.py:256
  131.7 3.5 %collective-permute-start.6 = (bf16[64,1024]{1,0:T(8,128)(2,1)S(1)}, bf16[64,1024]{1,0:T(8,128)(2,1)S(1)}, u32[]{:S(2)}, u32[]{:S(2)}) collective-permute-start(bf16[64,1024]{1,0:T(8,128)(2,1)S(1)} %get-tuple-element.52), channel_id=1, source_target_pairs={{0,1},{1,2},{2,3},{3,0},{4,5},{5,6},{6,7},{7,4},{8,9},{9,10},{10,1... | collective-permute-start | bytes 393224 | tf_op jit(solution)/shard_map/ppermute | solution.py:256
  135.3 4.0 %collective-permute-start.7 = (bf16[64,1024]{1,0:T(8,128)(2,1)S(1)}, bf16[64,1024]{1,0:T(8,128)(2,1)S(1)}, u32[]{:S(2)}, u32[]{:S(2)}) collective-permute-start(bf16[64,1024]{1,0:T(8,128)(2,1)S(1)} %get-tuple-element.53), channel_id=1, source_target_pairs={{0,2},{1,3},{2,0},{3,1},{4,6},{5,7},{6,4},{7,5},{8,10},{9,11},{10,... | collective-permute-start | bytes 393224 | tf_op jit(solution)/shard_map/ppermute | solution.py:256
  139.3 3.1 %collective-permute-start.8 = (bf16[64,1024]{1,0:T(8,128)(2,1)S(1)}, bf16[64,1024]{1,0:T(8,128)(2,1)S(1)}, u32[]{:S(2)}, u32[]{:S(2)}) collective-permute-start(bf16[64,1024]{1,0:T(8,128)(2,1)S(1)} %get-tuple-element.54), channel_id=1, source_target_pairs={{0,3},{1,0},{2,1},{3,2},{4,7},{5,4},{6,5},{7,6},{8,11},{9,8},{10,9... | collective-permute-start | bytes 393224 | tf_op jit(solution)/shard_map/ppermute | solution.py:256
  142.4 0.0 collective-permute-done.6.p1
  142.4 3.7 %collective-permute-done.7.p2 = bf16[64,1024]{1,0:T(8,128)(2,1)S(1)} collective-permute-done((bf16[64,1024]{1,0:T(8,128)(2,1)S(1)}, bf16[64,1024]{1,0:T(8,128)(2,1)S(1)}, u32[]{:S(2)}, u32[]{:S(2)}) %collective-permute-start.7) | collective-permute-done | bytes 131104 | tf_op jit(solution)/shard_map/ppermute | solution.py:256
  146.1 1.8 %collective-permute-done.8.p3 = bf16[64,1024]{1,0:T(8,128)(2,1)S(1)} collective-permute-done((bf16[64,1024]{1,0:T(8,128)(2,1)S(1)}, bf16[64,1024]{1,0:T(8,128)(2,1)S(1)}, u32[]{:S(2)}, u32[]{:S(2)}) %collective-permute-start.8) | collective-permute-done | bytes 131104 | tf_op jit(solution)/shard_map/ppermute | solution.py:256
  147.9 0.0 all-to-all-done.3.parts
  147.9 1.3 gather.1
  149.1 9.0 %psum.7 = f32[1,256]{1,0:T(1,128)} all-reduce(f32[1,256]{1,0:T(1,128)S(1)} %get-tuple-element.62), channel_id=1, replica_groups=mesh['dp'=4,'pipe'=8,'zhi'=2,'yhi'=2,'ylo'=4] {'dp'}, use_global_device_ids=true, to_apply=%region_0.0 | all-reduce | flops 256 | bytes 2048 | tf_op jit(solution)/shard_map/psum | solution.py:337
  158.1 1.4 join.1
  159.5 0.0 collective-permute-done.1
  159.5 0.8 copy.14
  (1 shorter events, 0.0 us)
Async XLA Ops:
  7.2 106.3 %all-gather.2.cloned.1.call-start = ((), (), s32[]{:S(2)}) async-start(), calls=%async_computation.4 | async-start | bytes 2359296 | tf_op jit(solution)/shard_map/all_gather | solution.py:277
  8.1 15.7 %collective-permute-start = (bf16[64,1024]{1,0:T(8,128)(2,1)S(1)}, bf16[64,1024]{1,0:T(8,128)(2,1)S(1)}, u32[]{:S(2)}, u32[]{:S(2)}) collective-permute-start(bf16[64,1024]{1,0:T(8,128)(2,1)S(1)} %pad_maximum_fusion.1), channel_id=1, source_target_pairs={{0,8},{1,9},{2,10},{3,11},{4,12},{5,13},{6,14},{7,15},{16,24},{17,... | collective-permute-start | bytes 393224 | tf_op jit(solution)/shard_map/ppermute | solution.py:263
  19.7 1.0 copy-start.2
  20.7 0.8 copy-start.4
  21.5 0.8 copy-start.5
  22.4 12.8 %copy-start.6 = (bf16[1,1,64,4096]{3,2,1,0:T(8,128)(2,1)S(1)}, bf16[1,1,64,4096]{3,2,1,0:T(8,128)(2,1)}, u32[]{:S(2)}) copy-start(bf16[1,1,64,4096]{3,2,1,0:T(8,128)(2,1)} %param.14) | copy-start | bytes 1572868
  24.5 37.4 %all-to-all-start = ((bf16[16,64,256]{2,1,0:T(8,128)(2,1)}), bf16[16,64,256]{2,1,0:T(8,128)(2,1)S(1)}, u32[]{:S(2)}, u32[]{:S(2)}) async-start(bf16[16,64,256]{2,1,0:T(8,128)(2,1)} %get-tuple-element.37), calls=%async_computation | async-start | bytes 1048576 | tf_op jit(solution)/shard_map/all_to_all | solution.py:253
  35.2 21.3 %collective-permute-start.2 = (bf16[64,4096]{1,0:T(8,128)(2,1)S(1)}, bf16[64,4096]{1,0:T(8,128)(2,1)S(1)}, u32[]{:S(2)}, u32[]{:S(2)}) collective-permute-start(bf16[64,4096]{1,0:T(8,128)(2,1)S(1)} %bitcast.28), channel_id=1, source_target_pairs={{0,112},{16,0},{32,16},{48,32},{64,48},{80,64},{96,80},{112,96},{1... | collective-permute-start | bytes 1572872 | tf_op jit(solution)/shard_map/ppermute | solution.py:256
  39.1 18.8 %collective-permute-start.3 = (bf16[64,1024]{1,0:T(8,128)(2,1)S(1)}, bf16[64,1024]{1,0:T(8,128)(2,1)S(1)}, u32[]{:S(2)}, u32[]{:S(2)}) collective-permute-start(bf16[64,1024]{1,0:T(8,128)(2,1)S(1)} %get-tuple-element.39), channel_id=1, source_target_pairs={{0,1},{1,2},{2,3},{3,0},{4,5},{5,6},{6,7},{7,4},{8,9},{9,10},{10,1... | collective-permute-start | bytes 393224 | tf_op jit(solution)/shard_map/ppermute | solution.py:256
  42.6 15.6 %collective-permute-start.4 = (bf16[64,1024]{1,0:T(8,128)(2,1)S(1)}, bf16[64,1024]{1,0:T(8,128)(2,1)S(1)}, u32[]{:S(2)}, u32[]{:S(2)}) collective-permute-start(bf16[64,1024]{1,0:T(8,128)(2,1)S(1)} %get-tuple-element.40), channel_id=1, source_target_pairs={{0,2},{1,3},{2,0},{3,1},{4,6},{5,7},{6,4},{7,5},{8,10},{9,11},{10,... | collective-permute-start | bytes 393224 | tf_op jit(solution)/shard_map/ppermute | solution.py:256
  46.6 22.7 %copy-start = (bf16[1,4096]{1,0:T(2,128)(2,1)S(1)}, bf16[1,4096]{1,0:T(2,128)(2,1)}, u32[]{:S(2)}) copy-start(bf16[1,4096]{1,0:T(2,128)(2,1)} %gain.1) | copy-start | bytes 24580
  46.6 15.3 %collective-permute-start.5 = (bf16[64,1024]{1,0:T(8,128)(2,1)S(1)}, bf16[64,1024]{1,0:T(8,128)(2,1)S(1)}, u32[]{:S(2)}, u32[]{:S(2)}) collective-permute-start(bf16[64,1024]{1,0:T(8,128)(2,1)S(1)} %get-tuple-element.41), channel_id=1, source_target_pairs={{0,3},{1,0},{2,1},{3,2},{4,7},{5,4},{6,5},{7,6},{8,11},{9,8},{10,9... | collective-permute-start | bytes 393224 | tf_op jit(solution)/shard_map/ppermute | solution.py:256
  61.9 24.9 %all-to-all-start.1 = ((bf16[4,64,1024]{2,1,0:T(8,128)(2,1)}), bf16[4,64,1024]{2,1,0:T(8,128)(2,1)S(1)}, u32[]{:S(2)}, u32[]{:S(2)}) async-start(bf16[4,64,1024]{2,1,0:T(8,128)(2,1)} %pack.1), calls=%async_computation.1 | async-start | bytes 1048576 | tf_op jit(solution)/shard_map/all_to_all | solution.py:253
  96.1 17.4 %copy-start.3 = (bf16[1,1,64,4096]{3,2,1,0:T(8,128)(2,1)S(1)}, bf16[1,1,64,4096]{3,2,1,0:T(8,128)(2,1)}, u32[]{:S(2)}) copy-start(bf16[1,1,64,4096]{3,2,1,0:T(8,128)(2,1)} %param.8) | copy-start | bytes 1572868
  103.4 44.4 %all-to-all-start.3 = ((bf16[16,80,256]{2,1,0:T(8,128)(2,1)}), bf16[16,80,256]{2,1,0:T(8,128)(2,1)S(1)}, u32[]{:S(2)}, u32[]{:S(2)}) async-start(bf16[16,80,256]{2,1,0:T(8,128)(2,1)} %get-tuple-element.50), calls=%async_computation.3 | async-start | bytes 1310720 | tf_op jit(solution)/shard_map/all_to_all | solution.py:253
  113.5 1.6 copy-start.1
  122.2 37.3 %collective-permute-start.1 = (bf16[64,4096]{1,0:T(8,128)(2,1)S(1)}, bf16[64,4096]{1,0:T(8,128)(2,1)S(1)}, u32[]{:S(2)}, u32[]{:S(2)}) collective-permute-start(bf16[64,4096]{1,0:T(8,128)(2,1)S(1)} %forward_first.1), channel_id=1, source_target_pairs={{0,16},{16,32},{32,48},{48,64},{64,80},{80,96},{96,112},{112,0},{1... | collective-permute-start | bytes 1572872 | tf_op jit(solution)/shard_map/ppermute | solution.py:256
  131.7 10.6 %collective-permute-start.6 = (bf16[64,1024]{1,0:T(8,128)(2,1)S(1)}, bf16[64,1024]{1,0:T(8,128)(2,1)S(1)}, u32[]{:S(2)}, u32[]{:S(2)}) collective-permute-start(bf16[64,1024]{1,0:T(8,128)(2,1)S(1)} %get-tuple-element.52), channel_id=1, source_target_pairs={{0,1},{1,2},{2,3},{3,0},{4,5},{5,6},{6,7},{7,4},{8,9},{9,10},{10,1... | collective-permute-start | bytes 393224 | tf_op jit(solution)/shard_map/ppermute | solution.py:256
  135.3 10.8 %collective-permute-start.7 = (bf16[64,1024]{1,0:T(8,128)(2,1)S(1)}, bf16[64,1024]{1,0:T(8,128)(2,1)S(1)}, u32[]{:S(2)}, u32[]{:S(2)}) collective-permute-start(bf16[64,1024]{1,0:T(8,128)(2,1)S(1)} %get-tuple-element.53), channel_id=1, source_target_pairs={{0,2},{1,3},{2,0},{3,1},{4,6},{5,7},{6,4},{7,5},{8,10},{9,11},{10,... | collective-permute-start | bytes 393224 | tf_op jit(solution)/shard_map/ppermute | solution.py:256
  139.3 8.6 %collective-permute-start.8 = (bf16[64,1024]{1,0:T(8,128)(2,1)S(1)}, bf16[64,1024]{1,0:T(8,128)(2,1)S(1)}, u32[]{:S(2)}, u32[]{:S(2)}) collective-permute-start(bf16[64,1024]{1,0:T(8,128)(2,1)S(1)} %get-tuple-element.54), channel_id=1, source_target_pairs={{0,3},{1,0},{2,1},{3,2},{4,7},{5,4},{6,5},{7,6},{8,11},{9,8},{10,9... | collective-permute-start | bytes 393224 | tf_op jit(solution)/shard_map/ppermute | solution.py:256
Sparse Core Ops, SparseCore 0:
  24.7 64.5 all-gather.1

commit v3 on v2

--- a/solution.py
+++ b/solution.py
@@ -73,22 +73,11 @@
     bias[...] = jnp.where(ahead <= where[0] * shape[1], 0.0, -jnp.inf).astype(F32)
 
 
-def assemble(where, pieces, full):
-    rows = pieces[0].shape[0]
-    for k, piece in enumerate(pieces):
-        at = pl.multiple_of(lax.rem(where[2] - k + FOUR, FOUR) * rows, rows)
-        full[pl.ds(at, rows), :] = piece[...]
-
-
-def open_body(where, query, keys, values, kv, q0, q1, q2, q3):
+def open_body(where, keys, values, kv):
     for s in range(kv.shape[0]):
         cols = slice((s % FOUR) * HD, (s % FOUR + 1) * HD)
         kv[s, :, :HD] = keys[:, cols]
         kv[s, :, HD:] = values[:, cols]
-    width = q0.shape[1]
-    for k, out in enumerate((q0, q1, q2, q3)):
-        at = pl.multiple_of(lax.rem(where[2] + k, FOUR) * width, width)
-        out[...] = query[:, pl.ds(at, width)]
 
 
 def pack_body(where, full, out):
@@ -97,11 +86,10 @@
         out[place] = full[:, place * width : (place + 1) * width]
 
 
-def join_body(where, p0, p1, p2, p3, out):
-    width = p0.shape[1]
-    for k, piece in enumerate((p0, p1, p2, p3)):
-        at = pl.multiple_of(lax.rem(where[2] - k + FOUR, FOUR) * width, width)
-        out[:, pl.ds(at, width)] = piece[...]
+def join_body(where, parts, out):
+    width = parts.shape[2]
+    for place in range(FOUR):
+        out[:, place * width : (place + 1) * width] = parts[place]
 
 
 def gather_body(where, parts, keys, values, share):
@@ -119,13 +107,12 @@
     share[...] = terms[0:1] + terms[1:2] + terms[2:3]
 
 
-def forward_body(heads, where, q0, q1, q2, q3, kv, out, lse, q_s, vt_s, bias):
-    assemble(where, (q0, q1, q2, q3), q_s)
+def forward_body(heads, where, q, kv, out, lse, vt_s, bias):
     set_bias(where, bias)
     vt_s[...] = kv[:, HD:].T
     for h in range(heads):
         cols = slice(h * HD, (h + 1) * HD)
-        out[:, cols], lse[h : h + 1, :] = attend(kv[:, :HD], vt_s[...], bias, q_s[:, cols])
+        out[:, cols], lse[h : h + 1, :] = attend(kv[:, :HD], vt_s[...], bias, q[:, cols])
 
 
 def stats_body(heads, where, act, up, gain, stats):
@@ -145,23 +132,24 @@
 
 
 def backward_body(
-    heads, width, where, q0, q1, q2, q3, kv, up, gain, act, lse, stats,
-    dq0, dq1, dq2, dq3, dkv, q_s, kt_s, bias, dk_s, dv_s, dq_s,
+    heads, width, where, q, kv, up, gain, act, lse, stats,
+    dq, dkv, sums, kt_s, bias, dk_s, dv_s,
 ):
-    assemble(where, (q0, q1, q2, q3), q_s)
     set_bias(where, bias)
     kt_s[...] = kv[:, :HD].T
     totals = (stats[0] + stats[1]) + (stats[2] + stats[3])
     inverse_row = lax.rsqrt(totals[0:1] / width + EPSILON)
     inverse = column(inverse_row)
     shrink = column(inverse_row * inverse_row * inverse_row * (totals[1:2] / width))
-    sums = []
+    per = heads // FOUR
     for h in range(heads):
         cols = slice(h * HD, (h + 1) * HD)
-        queries = q_s[:, cols]
+        queries = q[:, cols]
         act_h = act[:, cols].astype(F32)
         upstream = up[:, cols].astype(F32)
-        sums.append(jnp.sum(upstream * act_h * inverse, axis=0, keepdims=True))
+        sums[h // per : h // per + 1, (h % per) * HD : (h % per + 1) * HD] = jnp.sum(
+            upstream * act_h * inverse, axis=0, keepdims=True
+        )
         grad = (gain[:, cols].astype(F32) * upstream * inverse - act_h * shrink).astype(BF16)
         dots = row_of(grad.astype(F32) * act_h)
         scores = dot_nt(kv[:, :HD], queries) * SCALE + bias[...]
@@ -176,27 +164,27 @@
         else:
             dv_s[...] += dv
             dk_s[...] += dk
-        dq_s[:, cols] = dot_nn(kt_s[...], grad_scores).T.astype(BF16)
-    tokens = dq0.shape[0]
-    for k, out in enumerate((dq0, dq1, dq2, dq3)):
-        at = pl.multiple_of(lax.rem(where[2] + k, FOUR) * tokens, tokens)
-        out[...] = dq_s[pl.ds(at, tokens), :]
-    per = heads // FOUR
-    extra = dkv.shape[1] - tokens
+        dq[:, cols] = dot_nn(kt_s[...], grad_scores).T.astype(BF16)
+    tokens = dk_s.shape[0] // dkv.shape[0]
     for s in range(dkv.shape[0]):
         rows = slice(s * tokens, (s + 1) * tokens)
         dkv[s, :tokens, :HD] = dk_s[rows].astype(BF16)
         dkv[s, :tokens, HD:] = dv_s[rows].astype(BF16)
-        j = s % FOUR
-        value = jnp.concatenate(sums[j * per : (j + 1) * per], axis=1)
+        dkv[s, tokens:, :] = jnp.zeros((dkv.shape[1] - tokens, 2 * HD), BF16)
+
+
+def insert_body(where, sums, dkv, out):
+    del dkv
+    for s in range(out.shape[0]):
+        value = sums[s % FOUR : s % FOUR + 1]
         value = jnp.where(where[2] == s // FOUR, value, 0.0)
         terms = []
         for _ in range(3):
             term = value.astype(BF16).astype(F32)
             terms.append(term)
             value = value - term
-        terms.append(jnp.zeros((extra - 3, value.shape[1]), F32))
-        dkv[s, tokens:] = jnp.concatenate(terms, axis=0).astype(BF16)
+        terms.append(jnp.zeros((out.shape[1] - 3, value.shape[1]), F32))
+        out[s] = jnp.concatenate(terms, axis=0).astype(BF16)
 
 
 def first_body(where, q, kv, gain, out, k_s, vt_s, q_s, o_s, bias):
@@ -255,39 +243,39 @@
     def along(value, axis, step, count):
         return lax.ppermute(value, axis, [(i, (i + step) % count) for i in range(count)])
 
-    def ahead(pieces):
-        return [pieces[0]] + [along(pieces[k], "ylo", k, FOUR) for k in range(1, FOUR)]
-
-    piece = sds((tokens, cols), BF16)
+    up_raw = along(grad_output[0, 0], "pipe", -1, pipes)
     kv1 = jnp.concatenate([key_first[0, 0], value_first[0, 0]], axis=1)
+    def by_heads(full):
+        return call(pack_body, sds((FOUR, tokens, cols), BF16), (where, full), micros=1.4, name="pack")
+
+    q2 = swap(by_heads(query_second[0, 0]), "ylo")
+    packed = call(
+        open_body,
+        sds((places, tokens, 2 * HD), BF16),
+        (where, key_second[0, 0], value_second[0, 0]),
+        name="open_second",
+    )
+    up = by_heads(up_raw)
     other = lax.ppermute(kv1, "zhi", [(0, 1)])
-    up_raw = along(grad_output[0, 0], "pipe", -1, pipes)
-    packed, *q2 = call(
-        open_body,
-        (sds((places, tokens, 2 * HD), BF16),) + (piece,) * 4,
-        (where, query_second[0, 0], key_second[0, 0], value_second[0, 0]),
-        name="open_second",
-    )
-    kv1, other, packed = lax.optimization_barrier((kv1, other, packed))
+    packed, q2, up, other = lax.optimization_barrier((packed, q2, up, other))
+    q2 = q2.reshape(n, cols)
     kv = swap(packed, SEQ).reshape(length, 2 * HD)
-    q2 = ahead(q2)
-    up = call(pack_body, sds((FOUR, tokens, cols), BF16), (where, up_raw), name="pack")
-    kv, up, q2 = lax.optimization_barrier((kv, up, q2))
+    kv, up = lax.optimization_barrier((kv, up))
     up = swap(up, "ylo").reshape(n, cols)
+    kv1, other, kv = lax.optimization_barrier((kv1, other, kv))
     kv_first = lax.all_gather(
         jnp.concatenate([kv1, other], axis=0), ROW, axis=0, tiled=True
     )
 
     turned = pltpu.VMEM((HD, length), BF16)
     bias = pltpu.VMEM((length, n), F32)
-    rows = pltpu.VMEM((n, cols), BF16)
     total = pltpu.VMEM((length, HD), F32)
 
     out2, lse = call(
         functools.partial(forward_body, heads),
         (sds((n, cols), BF16), sds((heads, n), F32)),
-        (where, *q2, kv),
-        [rows, turned, bias],
+        (where, q2, kv),
+        [turned, bias],
         micros=6.4,
         name="forward_second",
     )
@@ -300,16 +288,33 @@
         ),
         "ylo",
     )
-    *dq, dkv = call(
+    dq, dkv, sums = call(
         functools.partial(backward_body, heads, width),
-        (piece,) * 4 + (sds((places, tokens + 16, 2 * HD), BF16),),
-        (where, *q2, kv, up, gain_cols, out2, lse, stats),
-        [rows, turned, bias, total, total, rows],
+        (
+            sds((n, cols), BF16),
+            sds((places, tokens + 16, 2 * HD), BF16),
+            sds((FOUR, 2 * HD), F32),
+        ),
+        (where, q2, kv, up, gain_cols, out2, lse, stats),
+        [turned, bias, total, total],
         micros=7.0,
         name="backward",
     )
+    dq = swap(dq.reshape(FOUR, tokens, cols), "ylo")
+    sums = lax.psum(sums, "dp")
+    below = pl.BlockSpec((places, 16, 2 * HD), lambda i: (0, tokens // 16, 0))
+    dkv = pl.pallas_call(
+        insert_body,
+        grid=(1,),
+        in_specs=[SMEM, pl.BlockSpec((FOUR, 2 * HD), lambda i: (0, 0)), below],
+        out_specs=below,
+        out_shape=sds(dkv.shape, BF16),
+        input_output_aliases={2: 0},
+        cost_estimate=pl.CostEstimate(flops=10**9, bytes_accessed=0, transcendentals=0),
+        name="insert",
+    )(where, sums, dkv)
+    dkv, dq = lax.optimization_barrier((dkv, dq))
     dkv = swap(dkv, SEQ)
-    dq = ahead(dq)
 
     normed = call(
         first_body,
@@ -326,16 +331,14 @@
         name="forward_first",
     )
     next_input = along(normed, "pipe", 1, pipes)
-
-    dkv, normed, dq = lax.optimization_barrier((dkv, normed, dq))
     grad_key, grad_value, share = call(
         gather_body,
         (sds((tokens, kv_width), BF16),) * 2 + (sds((1, 2 * HD), F32),),
         (where, dkv),
         name="gather",
     )
-    grad_gain = lax.psum(share, "dp")
-    grad_query = call(join_body, sds((tokens, width), BF16), (where, *dq), name="join")
+    grad_gain = share
+    grad_query = call(join_body, sds((tokens, width), BF16), (where, dq), name="join")
     return (
         next_input[None, None],
         grad_query[None, None],

time: 169 us -> 158 us (0.935)
  the two profiles are of different devices: /device:TPU:1 before, /device:TPU:64 now
where the time goes in v3:
time: 158 us
  blocking collectives  51.9 us (33%)
  starting transfers between devices  32.5 us (21%)
  Pallas kernels  29.3 us (19%)
  waiting for transfers between devices  24.8 us (16%)
  between operations  14.2 us (9%)
  local copies, waits for them, and re-layouts  4.31 us (3%)
    all_to_all x2, blocking collectives, swap(): return lax.all_to_all(packed, axes, split_axis=0, concat_axis=0, tiled=True)  40.7 us
    pallas_call x9, Pallas kernels, call(): pl.pallas_call(body, out_shape=outs, in_specs=[SMEM] + [VMEM] * (len(inpu...  27.6 us
    all_to_all x4, waiting for transfers between devices, swap(): return lax.all_to_all(packed, axes, split_axis=0, concat_axis=0, tiled=True)  20.6 us
    all_to_all x4, starting transfers between devices, swap(): return lax.all_to_all(packed, axes, split_axis=0, concat_axis=0, tiled=True)  18.6 us
    psum x1, blocking collectives, local(): sums = lax.psum(sums, 'dp')  11.2 us
    ppermute x1, starting transfers between devices, local(): other = lax.ppermute(kv1, 'zhi', [(0, 1)])  10 us
    unnamed x25, local copies, waits for them, and re-layouts  4.3 us
    ppermute x1, waiting for transfers between devices, local(): other = lax.ppermute(kv1, 'zhi', [(0, 1)])  4.18 us
  transfers between devices with their start and end apart: 8, of which 3 were waited for; matrix products, arithmetic and copies ran while one was open for 0% of the time, Pallas kernels for 18%

profile of v3, /device:TPU:64, one launch (start us, length us, event | category | flops | bytes accessed | tf_op | source)
XLA Modules:
  0.0 157.8 jit_solution(4511084470719690420)
XLA Ops:
  7.2 0.1 pad_add_fusion.where
  7.3 0.0 copy-start.2
  7.3 0.0 copy-start.5
  7.3 1.0 copy-done.5
  8.3 0.0 copy-start.11
  8.3 0.0 copy-start.9
  8.3 0.0 copy-start.10
  8.3 0.0 copy-start.7
  8.3 0.0 copy-start.8
  8.3 1.4 pack.2
  9.7 4.9 %all-to-all-start = ((bf16[4,64,1024]{2,1,0:T(8,128)(2,1)}), bf16[4,64,1024]{2,1,0:T(8,128)(2,1)S(1)}, u32[]{:S(2)}, u32[]{:S(2)}) async-start(bf16[4,64,1024]{2,1,0:T(8,128)(2,1)} %pack.2), calls=%async_computation | async-start | bytes 1048576 | tf_op jit(solution)/shard_map/all_to_all | solution.py:241
  14.6 0.0 all-gather.2.cloned.1.call-start
  14.6 0.0 copy-done.11
  14.6 1.9 %collective-permute-start = (bf16[64,4096]{1,0:T(8,128)(2,1)S(1)}, bf16[64,4096]{1,0:T(8,128)(2,1)S(1)}, u32[]{:S(2)}, u32[]{:S(2)}) collective-permute-start(bf16[64,4096]{1,0:T(8,128)(2,1)S(1)} %bitcast.32), channel_id=1, source_target_pairs={{0,112},{16,0},{32,16},{48,32},{64,48},{80,64},{96,80},{112,96},{1... | collective-permute-start | bytes 1572872 | tf_op jit(solution)/shard_map/ppermute | solution.py:244
  16.5 0.0 copy-done.9
  16.5 0.0 copy-done.10
  16.5 10.0 %collective-permute-start.1 = (bf16[64,1024]{1,0:T(8,128)(2,1)S(1)}, bf16[64,1024]{1,0:T(8,128)(2,1)S(1)}, u32[]{:S(2)}, u32[]{:S(2)}) collective-permute-start(bf16[64,1024]{1,0:T(8,128)(2,1)S(1)} %pad_maximum_fusion.1), channel_id=1, source_target_pairs={{0,8},{1,9},{2,10},{3,11},{4,12},{5,13},{6,14},{7,15},{16,24},{17,... | collective-permute-start | bytes 393224 | tf_op jit(solution)/shard_map/ppermute | solution.py:259
  26.6 0.0 copy-done.7
  26.6 0.0 copy-done.8
  26.6 0.6 open_second.1
  27.2 0.0 collective-permute-done.full
  27.2 1.4 pack.3
  28.6 0.0 copy-start.1
  28.6 4.2 %collective-permute-done.1 = bf16[64,1024]{1,0:T(8,128)(2,1)S(1)} collective-permute-done((bf16[64,1024]{1,0:T(8,128)(2,1)S(1)}, bf16[64,1024]{1,0:T(8,128)(2,1)S(1)}, u32[]{:S(2)}, u32[]{:S(2)}) %collective-permute-start.1) | collective-permute-done | bytes 131104 | tf_op jit(solution)/shard_map/ppermute | solution.py:259
  32.8 0.0 all-to-all-done
  32.8 31.4 %all_to_all.30 = bf16[16,64,256]{2,1,0:T(8,128)(2,1)S(1)} all-to-all(bf16[16,64,256]{2,1,0:T(8,128)(2,1)S(1)} %open_second.1), channel_id=1, replica_groups=mesh['dp'=4,'pipe'=8,'zhi'=2,'yhi'=2,'ylo'=4] {'zhi','yhi','ylo'}, dimensions={0} | all-to-all | bytes 1048576 | tf_op jit(solution)/shard_map/all_to_all | solution.py:241
  64.1 0.7 pad_maximum_fusion
  64.8 0.0 all-gather.2.cloned.1.call-update
  64.9 3.5 %all-to-all-start.2 = ((bf16[4,64,1024]{2,1,0:T(8,128)(2,1)}), bf16[4,64,1024]{2,1,0:T(8,128)(2,1)S(1)}, u32[]{:S(2)}, u32[]{:S(2)}) async-start(bf16[4,64,1024]{2,1,0:T(8,128)(2,1)} %pack.3), calls=%async_computation.2 | async-start | bytes 1048576 | tf_op jit(solution)/shard_map/all_to_all | solution.py:241
  68.4 0.0 copy-done.1
  68.4 6.5 %forward_second.1 = (bf16[256,1024]{1,0:T(8,128)(2,1)S(1)}, f32[8,256]{1,0:T(8,128)S(1)}) custom-call(s32[4]{0:T(128)S(1)} %pad_add_fusion.where, bf16[256,1024]{1,0:T(8,128)(2,1)S(1)} %bitcast.19, bf16[1024,256]{1,0:T(8,128)(2,1)S(1)} %bitcast.21), custom_call_target="tpu_custom_call" | custom-call | flops 6400000000 | tf_op jit(solution)/shard_map/forward_second/pallas_call | solution.py:27
  74.9 8.7 %all-to-all-done.2 = bf16[4,64,1024]{2,1,0:T(8,128)(2,1)S(1)} async-done(((bf16[4,64,1024]{2,1,0:T(8,128)(2,1)}), bf16[4,64,1024]{2,1,0:T(8,128)(2,1)S(1)}, u32[]{:S(2)}, u32[]{:S(2)}) %all-to-all-start.2) | async-done | bytes 524320 | tf_op jit(solution)/shard_map/all_to_all | solution.py:241
  83.6 0.8 stats.1
  84.4 9.4 %all_to_all.31.stats = f32[4,8,256]{2,1,0:T(8,128)S(1)} all-to-all(f32[4,8,256]{2,1,0:T(8,128)S(1)} %stats.1), channel_id=1, replica_groups=mesh['dp'=4,'pipe'=8,'zhi'=2,'yhi'=2,'ylo'=4] {'ylo'}, dimensions={0} | all-to-all | bytes 65536 | tf_op jit(solution)/shard_map/all_to_all | solution.py:241
  93.8 0.0 copy-done.2
  93.8 7.2 %backward.1 = (bf16[256,1024]{1,0:T(8,128)(2,1)}, bf16[16,80,256]{2,1,0:T(8,128)(2,1)S(1)}, f32[4,256]{1,0:T(4,128)S(1)}) custom-call(s32[4]{0:T(128)S(1)} %pad_add_fusion.where, bf16[256,1024]{1,0:T(8,128)(2,1)S(1)} %bitcast.20, bf16[1024,256]{1,0:T(8,128)(2,1)S(1)} %bitcast.22, bf16[256,1024]{1,0:T(8,128)(2,1)S(1)} %bitcast.24, ...), custom_call_target="tpu_custom_call" | custom-call | flops 7000000000 | tf_op jit(solution)/shard_map/backward/pallas_call | solution.py:27
  101.0 0.0 copy-start
  101.0 0.8 copy-done
  101.8 3.5 %all-to-all-start.4 = ((bf16[4,64,1024]{2,1,0:T(8,128)(2,1)}), bf16[4,64,1024]{2,1,0:T(8,128)(2,1)S(1)}, u32[]{:S(2)}, u32[]{:S(2)}) async-start(bf16[4,64,1024]{2,1,0:T(8,128)(2,1)} %bitcast.15), calls=%async_computation.4 | async-start | bytes 1048576 | tf_op jit(solution)/shard_map/all_to_all | solution.py:241
  105.3 11.2 %psum.7.sums = f32[4,256]{1,0:T(4,128)} all-reduce(f32[4,256]{1,0:T(4,128)S(1)} %get-tuple-element.35), channel_id=1, replica_groups=mesh['dp'=4,'pipe'=8,'zhi'=2,'yhi'=2,'ylo'=4] {'dp'}, use_global_device_ids=true, to_apply=%region_0.0 | all-reduce | flops 1024 | bytes 8192 | tf_op jit(solution)/shard_map/psum | solution.py:304
  116.5 0.0 copy-start.3
  116.5 0.0 copy-start.6
  116.5 1.7 %insert.1 = bf16[16,80,256]{2,1,0:T(8,128)(2,1)} custom-call(s32[4]{0:T(128)} %copy-done.2, f32[4,256]{1,0:T(4,128)} %psum.7.sums, bf16[16,80,256]{2,1,0:T(8,128)(2,1)} %copy-done), custom_call_target="tpu_custom_call", output_to_operand_aliasing={{}: (2, {})} | custom-call | flops 1000000000 | tf_op jit(solution)/shard_map/insert/pallas_call | solution.py:306
  118.2 0.0 all-to-all-done.4.parts
  118.2 6.8 %all-to-all-start.5 = ((bf16[16,80,256]{2,1,0:T(8,128)(2,1)}), bf16[16,80,256]{2,1,0:T(8,128)(2,1)S(1)}, u32[]{:S(2)}, u32[]{:S(2)}) async-start(bf16[16,80,256]{2,1,0:T(8,128)(2,1)} %insert.1), calls=%async_computation.5 | async-start | bytes 1310720 | tf_op jit(solution)/shard_map/all_to_all | solution.py:241
  125.0 0.0 all-gather.2.cloned.1.call-done.kv
  125.1 0.0 copy-done.3
  125.1 0.0 copy-done.6
  125.1 0.0 copy-start.4
  125.1 1.6 %copy-done.4 = bf16[1024,1024]{1,0:T(8,128)(2,1)S(1)} copy-done((bf16[1024,1024]{1,0:T(8,128)(2,1)S(1)}, bf16[1024,1024]{1,0:T(8,128)(2,1)}, u32[]{:S(2)}) %copy-start.4) | copy-done | bytes 2097176
  126.7 7.0 %forward_first.1 = bf16[64,4096]{1,0:T(8,128)(2,1)S(1)} custom-call(s32[4]{0:T(128)S(1)} %copy-done.3, bf16[64,4096]{1,0:T(8,128)(2,1)S(1)} %bitcast.26, bf16[1024,1024]{1,0:T(8,128)(2,1)S(1)} %copy-done.4, bf16[1,4096]{1,0:T(2,128)(2,1)S(1)} %copy-done.1), custom_call_target="tpu_custom_call" | custom-call | flops 7000000000 | tf_op jit(solution)/shard_map/forward_first/pallas_call | solution.py:27
  133.7 1.9 %collective-permute-start.2 = (bf16[64,4096]{1,0:T(8,128)(2,1)S(1)}, bf16[64,4096]{1,0:T(8,128)(2,1)S(1)}, u32[]{:S(2)}, u32[]{:S(2)}) collective-permute-start(bf16[64,4096]{1,0:T(8,128)(2,1)S(1)} %forward_first.1), channel_id=1, source_target_pairs={{0,16},{16,32},{32,48},{48,64},{64,80},{80,96},{96,112},{112,0},{1... | collective-permute-start | bytes 1572872 | tf_op jit(solution)/shard_map/ppermute | solution.py:244
  135.6 1.4 join.1
  137.0 11.9 %all-to-all-done.5.parts = bf16[16,80,256]{2,1,0:T(8,128)(2,1)S(1)} async-done(((bf16[16,80,256]{2,1,0:T(8,128)(2,1)}), bf16[16,80,256]{2,1,0:T(8,128)(2,1)S(1)}, u32[]{:S(2)}, u32[]{:S(2)}) %all-to-all-start.5) | async-done | bytes 655392 | tf_op jit(solution)/shard_map/all_to_all | solution.py:241
  148.9 1.2 gather.1
  150.1 0.0 collective-permute-done.2
  150.1 0.8 copy.16
  (2 shorter events, 0.0 us)
Async XLA Ops:
  7.3 86.5 %copy-start.2 = (s32[4]{0:T(128)}, s32[4]{0:T(128)S(1)}, u32[]{:S(2)}) copy-start(s32[4]{0:T(128)S(1)} %pad_add_fusion.where) | copy-start | bytes 52
  7.3 1.0 copy-start.5
  8.3 6.3 %copy-start.11 = (bf16[1,1,64,4096]{3,2,1,0:T(8,128)(2,1)S(1)}, bf16[1,1,64,4096]{3,2,1,0:T(8,128)(2,1)}, u32[]{:S(2)}) copy-start(bf16[1,1,64,4096]{3,2,1,0:T(8,128)(2,1)} %param.14) | copy-start | bytes 1572868
  8.3 8.2 %copy-start.9 = (bf16[1,1,64,512]{3,2,1,0:T(8,128)(2,1)S(1)}, bf16[1,1,64,512]{3,2,1,0:T(8,128)(2,1)}, u32[]{:S(2)}) copy-start(bf16[1,1,64,512]{3,2,1,0:T(8,128)(2,1)} %param.10) | copy-start | bytes 196612
  8.3 8.2 %copy-start.10 = (bf16[1,1,64,512]{3,2,1,0:T(8,128)(2,1)S(1)}, bf16[1,1,64,512]{3,2,1,0:T(8,128)(2,1)}, u32[]{:S(2)}) copy-start(bf16[1,1,64,512]{3,2,1,0:T(8,128)(2,1)} %param.9) | copy-start | bytes 196612
  8.3 18.3 %copy-start.7 = (bf16[1,1,64,512]{3,2,1,0:T(8,128)(2,1)S(1)}, bf16[1,1,64,512]{3,2,1,0:T(8,128)(2,1)}, u32[]{:S(2)}) copy-start(bf16[1,1,64,512]{3,2,1,0:T(8,128)(2,1)} %param.12) | copy-start | bytes 196612
  8.3 18.3 %copy-start.8 = (bf16[1,1,64,512]{3,2,1,0:T(8,128)(2,1)S(1)}, bf16[1,1,64,512]{3,2,1,0:T(8,128)(2,1)}, u32[]{:S(2)}) copy-start(bf16[1,1,64,512]{3,2,1,0:T(8,128)(2,1)} %param.13) | copy-start | bytes 196612
  9.7 23.1 %all-to-all-start = ((bf16[4,64,1024]{2,1,0:T(8,128)(2,1)}), bf16[4,64,1024]{2,1,0:T(8,128)(2,1)S(1)}, u32[]{:S(2)}, u32[]{:S(2)}) async-start(bf16[4,64,1024]{2,1,0:T(8,128)(2,1)} %pack.2), calls=%async_computation | async-start | bytes 1048576 | tf_op jit(solution)/shard_map/all_to_all | solution.py:241
  14.6 110.5 %all-gather.2.cloned.1.call-start = ((), (), s32[]{:S(2)}) async-start(), calls=%async_computation.6 | async-start | bytes 2359296 | tf_op jit(solution)/shard_map/all_gather | solution.py:266
  14.6 12.6 %collective-permute-start = (bf16[64,4096]{1,0:T(8,128)(2,1)S(1)}, bf16[64,4096]{1,0:T(8,128)(2,1)S(1)}, u32[]{:S(2)}, u32[]{:S(2)}) collective-permute-start(bf16[64,4096]{1,0:T(8,128)(2,1)S(1)} %bitcast.32), channel_id=1, source_target_pairs={{0,112},{16,0},{32,16},{48,32},{64,48},{80,64},{96,80},{112,96},{1... | collective-permute-start | bytes 1572872 | tf_op jit(solution)/shard_map/ppermute | solution.py:244
  16.5 16.2 %collective-permute-start.1 = (bf16[64,1024]{1,0:T(8,128)(2,1)S(1)}, bf16[64,1024]{1,0:T(8,128)(2,1)S(1)}, u32[]{:S(2)}, u32[]{:S(2)}) collective-permute-start(bf16[64,1024]{1,0:T(8,128)(2,1)S(1)} %pad_maximum_fusion.1), channel_id=1, source_target_pairs={{0,8},{1,9},{2,10},{3,11},{4,12},{5,13},{6,14},{7,15},{16,24},{17,... | collective-permute-start | bytes 393224 | tf_op jit(solution)/shard_map/ppermute | solution.py:259
  28.6 39.8 %copy-start.1 = (bf16[1,4096]{1,0:T(2,128)(2,1)S(1)}, bf16[1,4096]{1,0:T(2,128)(2,1)}, u32[]{:S(2)}) copy-start(bf16[1,4096]{1,0:T(2,128)(2,1)} %gain.1) | copy-start | bytes 24580
  64.9 18.7 %all-to-all-start.2 = ((bf16[4,64,1024]{2,1,0:T(8,128)(2,1)}), bf16[4,64,1024]{2,1,0:T(8,128)(2,1)S(1)}, u32[]{:S(2)}, u32[]{:S(2)}) async-start(bf16[4,64,1024]{2,1,0:T(8,128)(2,1)} %pack.3), calls=%async_computation.2 | async-start | bytes 1048576 | tf_op jit(solution)/shard_map/all_to_all | solution.py:241
  101.0 0.8 copy-start
  101.8 16.4 %all-to-all-start.4 = ((bf16[4,64,1024]{2,1,0:T(8,128)(2,1)}), bf16[4,64,1024]{2,1,0:T(8,128)(2,1)S(1)}, u32[]{:S(2)}, u32[]{:S(2)}) async-start(bf16[4,64,1024]{2,1,0:T(8,128)(2,1)} %bitcast.15), calls=%async_computation.4 | async-start | bytes 1048576 | tf_op jit(solution)/shard_map/all_to_all | solution.py:241
  116.5 8.6 %copy-start.3 = (s32[4]{0:T(128)S(1)}, s32[4]{0:T(128)}, u32[]{:S(2)}) copy-start(s32[4]{0:T(128)} %copy-done.2) | copy-start | bytes 52
  116.5 8.6 %copy-start.6 = (bf16[1,1,64,4096]{3,2,1,0:T(8,128)(2,1)S(1)}, bf16[1,1,64,4096]{3,2,1,0:T(8,128)(2,1)}, u32[]{:S(2)}) copy-start(bf16[1,1,64,4096]{3,2,1,0:T(8,128)(2,1)} %param.8) | copy-start | bytes 1572868
  118.2 30.6 %all-to-all-start.5 = ((bf16[16,80,256]{2,1,0:T(8,128)(2,1)}), bf16[16,80,256]{2,1,0:T(8,128)(2,1)S(1)}, u32[]{:S(2)}, u32[]{:S(2)}) async-start(bf16[16,80,256]{2,1,0:T(8,128)(2,1)} %insert.1), calls=%async_computation.5 | async-start | bytes 1310720 | tf_op jit(solution)/shard_map/all_to_all | solution.py:241
  125.1 1.6 %copy-start.4 = (bf16[1024,1024]{1,0:T(8,128)(2,1)S(1)}, bf16[1024,1024]{1,0:T(8,128)(2,1)}, u32[]{:S(2)}) copy-start(bf16[1024,1024]{1,0:T(8,128)(2,1)} %all-gather.2.cloned.1.call-done.kv) | copy-start | bytes 6291460
  133.7 16.4 %collective-permute-start.2 = (bf16[64,4096]{1,0:T(8,128)(2,1)S(1)}, bf16[64,4096]{1,0:T(8,128)(2,1)S(1)}, u32[]{:S(2)}, u32[]{:S(2)}) collective-permute-start(bf16[64,4096]{1,0:T(8,128)(2,1)S(1)} %forward_first.1), channel_id=1, source_target_pairs={{0,16},{16,32},{32,48},{48,64},{64,80},{80,96},{96,112},{112,0},{1... | collective-permute-start | bytes 1572872 | tf_op jit(solution)/shard_map/ppermute | solution.py:244
Sparse Core Ops, SparseCore 0:
  65.0 42.8 all-gather.1

commit v4 on v3

--- a/solution.py
+++ b/solution.py
@@ -58,6 +58,14 @@
     return jnp.sum(block.T, axis=0, keepdims=True)
 
 
+def head_at(where, place):
+    return place + where[4] * (FOUR - 1 - 2 * place)
+
+
+def head_columns(where, place, width):
+    return pl.ds(pl.multiple_of(head_at(where, place) * width, width), width)
+
+
 def attend(keys, values_t, bias, queries):
     scores = dot_nt(keys, queries) + bias[...]
     highest = jnp.max(scores, axis=0, keepdims=True)
@@ -73,32 +81,40 @@
     bias[...] = jnp.where(ahead <= where[0] * shape[1], 0.0, -jnp.inf).astype(F32)
 
 
-def open_body(where, keys, values, kv):
-    for s in range(kv.shape[0]):
-        cols = slice((s % FOUR) * HD, (s % FOUR + 1) * HD)
-        kv[s, :, :HD] = keys[:, cols]
-        kv[s, :, HD:] = values[:, cols]
+def load_keys(where, blocks, at, full):
+    n = blocks[0].shape[0]
+    for i, block in enumerate(blocks):
+        group = where[0] if i == 0 else where[4 + i]
+        full[pl.ds(pl.multiple_of(group * n, n), n), :] = block[:, at : at + HD]
+
+
+def open_body(where, query, keys, values, out):
+    width = query.shape[1] // FOUR
+    for place in range(FOUR):
+        cols = head_columns(where, place, HD)
+        out[place, :, :width] = query[:, head_columns(where, place, width)]
+        out[place, :, width : width + HD] = keys[:, cols]
+        out[place, :, width + HD :] = values[:, cols]
 
 
 def pack_body(where, full, out):
-    width = out.shape[2]
     for place in range(FOUR):
-        out[place] = full[:, place * width : (place + 1) * width]
+        out[place] = full[:, head_columns(where, place, out.shape[2])]
 
 
 def join_body(where, parts, out):
-    width = parts.shape[2]
     for place in range(FOUR):
-        out[:, place * width : (place + 1) * width] = parts[place]
+        out[:, head_columns(where, place, parts.shape[2])] = parts[place]
 
 
 def gather_body(where, parts, keys, values, share):
     tokens = keys.shape[0]
     for h in range(FOUR):
         cols = slice(h * HD, (h + 1) * HD)
-        total = parts[h, :tokens].astype(F32)
-        for s in range(h + FOUR, parts.shape[0], FOUR):
-            total = total + parts[s, :tokens].astype(F32)
+        total = 0.0
+        for group in range(parts.shape[0] // FOUR):
+            place = FOUR - 1 - h if group % 2 else h
+            total = total + parts[group * FOUR + place, :tokens].astype(F32)
         keys[:, cols] = total[:, :HD].astype(BF16)
         values[:, cols] = total[:, HD:].astype(BF16)
     terms = parts[0, tokens:].astype(F32)
@@ -107,12 +123,15 @@
     share[...] = terms[0:1] + terms[1:2] + terms[2:3]
 
 
-def forward_body(heads, where, q, kv, out, lse, vt_s, bias):
+def forward_body(heads, where, q, kv1, kv2, kv3, out, lse, k_s, v_s, bias):
     set_bias(where, bias)
-    vt_s[...] = kv[:, HD:].T
+    blocks = (q.at[:, heads * HD :], kv1, kv2, kv3)
+    load_keys(where, blocks, 0, k_s)
+    load_keys(where, blocks, HD, v_s)
+    values_t = v_s[...].T
     for h in range(heads):
         cols = slice(h * HD, (h + 1) * HD)
-        out[:, cols], lse[h : h + 1, :] = attend(kv[:, :HD], vt_s[...], bias, q[:, cols])
+        out[:, cols], lse[h : h + 1, :] = attend(k_s[...], values_t, bias, q[:, cols])
 
 
 def stats_body(heads, where, act, up, gain, stats):
@@ -132,11 +151,14 @@
 
 
 def backward_body(
-    heads, width, where, q, kv, up, gain, act, lse, stats,
-    dq, dkv, sums, kt_s, bias, dk_s, dv_s,
+    heads, width, where, q, kv1, kv2, kv3, up, gain, act, lse, stats,
+    dq, dkv, sums, k_s, v_s, bias, dk_s, dv_s,
 ):
     set_bias(where, bias)
-    kt_s[...] = kv[:, :HD].T
+    blocks = (q.at[:, heads * HD :], kv1, kv2, kv3)
+    load_keys(where, blocks, 0, k_s)
+    load_keys(where, blocks, HD, v_s)
+    keys_t = k_s[...].T
     totals = (stats[0] + stats[1]) + (stats[2] + stats[3])
     inverse_row = lax.rsqrt(totals[0:1] / width + EPSILON)
     inverse = column(inverse_row)
@@ -152,9 +174,9 @@
         )
         grad = (gain[:, cols].astype(F32) * upstream * inverse - act_h * shrink).astype(BF16)
         dots = row_of(grad.astype(F32) * act_h)
-        scores = dot_nt(kv[:, :HD], queries) * SCALE + bias[...]
+        scores = dot_nt(k_s[...], queries) * SCALE + bias[...]
         probs = jnp.exp(scores - lse[h : h + 1, :])
-        grad_weights = dot_nt(kv[:, HD:], grad)
+        grad_weights = dot_nt(v_s[...], grad)
         grad_scores = (probs * (grad_weights - dots) * SCALE).astype(BF16)
         dv = dot_nn(probs.astype(BF16), grad)
         dk = dot_nn(grad_scores, queries)
@@ -164,7 +186,7 @@
         else:
             dv_s[...] += dv
             dk_s[...] += dk
-        dq[:, cols] = dot_nn(kt_s[...], grad_scores).T.astype(BF16)
+        dq[:, cols] = dot_nn(keys_t, grad_scores).T.astype(BF16)
     tokens = dk_s.shape[0] // dkv.shape[0]
     for s in range(dkv.shape[0]):
         rows = slice(s * tokens, (s + 1) * tokens)
@@ -234,8 +256,19 @@
     length = tokens * places
     pipes = lax.axis_size("pipe")
     zhi, yhi, ylo = (lax.axis_index(axis) for axis in SEQ)
-    where = jnp.stack([zhi * 2 + yhi, zhi, ylo, yhi * FOUR + ylo]).astype(jnp.int32)
-    gain_cols = lax.dynamic_slice_in_dim(gain, ylo * cols, cols, 1)
+    group = zhi * 2 + yhi
+    mine = ylo + yhi * (FOUR - 1 - 2 * ylo)
+    where = jnp.stack(
+        [group, zhi, mine, yhi * FOUR + ylo, yhi, zhi * 2 + 1 - yhi, 2 - zhi * 2 + yhi, 3 - group]
+    ).astype(jnp.int32)
+    gain_cols = lax.dynamic_slice_in_dim(gain, mine * cols, cols, 1)
+
+    def device(z, h, y):
+        return (z * 2 + h) * FOUR + y
+
+    near = [(device(z, 0, y), device(z, 1, 3 - y)) for z in range(2) for y in range(FOUR)]
+    far = [(device(0, h, y), device(1, h, y)) for h in range(2) for y in range(FOUR)]
+    cross = [(device(0, h, y), device(1, 1 - h, 3 - y)) for h in range(2) for y in range(FOUR)]
 
     def swap(packed, axes):
         return lax.all_to_all(packed, axes, split_axis=0, concat_axis=0, tiled=True)
@@ -245,28 +278,26 @@
 
     up_raw = along(grad_output[0, 0], "pipe", -1, pipes)
     kv1 = jnp.concatenate([key_first[0, 0], value_first[0, 0]], axis=1)
-    def by_heads(full):
-        return call(pack_body, sds((FOUR, tokens, cols), BF16), (where, full), micros=1.4, name="pack")
-
-    q2 = swap(by_heads(query_second[0, 0]), "ylo")
-    packed = call(
+    other = lax.ppermute(kv1, "zhi", [(0, 1)])
+    qkv = call(
         open_body,
-        sds((places, tokens, 2 * HD), BF16),
-        (where, key_second[0, 0], value_second[0, 0]),
+        sds((FOUR, tokens, cols + 2 * HD), BF16),
+        (where, query_second[0, 0], key_second[0, 0], value_second[0, 0]),
         name="open_second",
     )
-    up = by_heads(up_raw)
-    other = lax.ppermute(kv1, "zhi", [(0, 1)])
-    packed, q2, up, other = lax.optimization_barrier((packed, q2, up, other))
-    q2 = q2.reshape(n, cols)
-    kv = swap(packed, SEQ).reshape(length, 2 * HD)
-    kv, up = lax.optimization_barrier((kv, up))
+    qkv = swap(qkv, "ylo")
+    up = call(
+        pack_body, sds((FOUR, tokens, cols), BF16), (where, up_raw), micros=1.4, name="pack"
+    )
+    qkv, up, other = lax.optimization_barrier((qkv, up, other))
+    qkv = qkv.reshape(n, cols + 2 * HD)
+    kvs = [lax.ppermute(qkv[:, cols:], SEQ, pairs) for pairs in (near, far, cross)]
     up = swap(up, "ylo").reshape(n, cols)
-    kv1, other, kv = lax.optimization_barrier((kv1, other, kv))
     kv_first = lax.all_gather(
         jnp.concatenate([kv1, other], axis=0), ROW, axis=0, tiled=True
     )
 
+    long = pltpu.VMEM((length, HD), BF16)
     turned = pltpu.VMEM((HD, length), BF16)
     bias = pltpu.VMEM((length, n), F32)
     total = pltpu.VMEM((length, HD), F32)
@@ -274,8 +305,8 @@
     out2, lse = call(
         functools.partial(forward_body, heads),
         (sds((n, cols), BF16), sds((heads, n), F32)),
-        (where, q2, kv),
-        [turned, bias],
+        (where, qkv, *kvs),
+        [long, long, bias],
         micros=6.4,
         name="forward_second",
     )
@@ -295,8 +326,8 @@
             sds((places, tokens + 16, 2 * HD), BF16),
             sds((FOUR, 2 * HD), F32),
         ),
-        (where, q2, kv, up, gain_cols, out2, lse, stats),
-        [turned, bias, total, total],
+        (where, qkv, *kvs, up, gain_cols, out2, lse, stats),
+        [long, long, bias, total, total],
         micros=7.0,
         name="backward",
     )
@@ -321,7 +352,7 @@
         sds((tokens, width), BF16),
         (where, query_first[0, 0], kv_first, gain),
         [
-            pltpu.VMEM((length, HD), BF16),
+            long,
             turned,
             pltpu.VMEM((n, HD), BF16),
             pltpu.VMEM((tokens, width), BF16),

time: 158 us -> 150 us (0.949)
  the two profiles are of different devices: /device:TPU:64 before, /device:TPU:1 now
where the time goes in v4:
time: 150 us; the launch traced here: 148 us
  starting transfers between devices  70.9 us (47%)
  Pallas kernels  28.9 us (19%)
  blocking collectives  17 us (11%)
  between operations  14.2 us (9%)
  waiting for transfers between devices  10.3 us (7%)
  local copies, waits for them, and re-layouts  6.07 us (4%)
    all_to_all x4, starting transfers between devices, swap(): return lax.all_to_all(packed, axes, split_axis=0, concat_axis=0, tiled=True)  28.3 us
    pallas_call x8, Pallas kernels, call(): pl.pallas_call(body, out_shape=outs, in_specs=[SMEM] + [VMEM] * (len(inpu...  27.2 us
    ppermute x3, starting transfers between devices, local(): lax.ppermute(qkv[:, cols:], SEQ, pairs)  18.5 us
    ppermute x2, starting transfers between devices, along(): lax.ppermute(value, axis, [(i, (i + step) % count) for i in range(count)])  17.4 us
    psum x1, blocking collectives, local(): sums = lax.psum(sums, 'dp')  9.06 us
    all_to_all x1, blocking collectives, swap(): return lax.all_to_all(packed, axes, split_axis=0, concat_axis=0, tiled=True)  7.98 us
    ppermute x1, starting transfers between devices, local(): other = lax.ppermute(kv1, 'zhi', [(0, 1)])  6.59 us
    unnamed x25, local copies, waits for them, and re-layouts  5.97 us
  transfers between devices with their start and end apart: 11, of which 4 were waited for; matrix products, arithmetic and copies ran while one was open for 0% of the time, Pallas kernels for 19%

profile of v4, /device:TPU:1, one launch (start us, length us, event | category | flops | bytes accessed | tf_op | source)
XLA Modules:
  0.0 148.2 jit_solution(11610045397440036318)
XLA Ops:
  7.2 0.1 stack.35.where
  7.3 0.0 copy-start.2
  7.3 0.0 copy-start.5
  7.3 1.0 copy-done.5
  8.3 0.0 copy-start.7
  8.3 0.8 copy-done.7
  9.2 0.0 copy-start.8
  9.2 0.8 copy-done.8
  10.0 0.0 copy-start.11
  10.0 0.0 copy-start.9
  10.0 0.0 copy-start.10
  10.0 1.4 open_second.1
  11.4 5.4 %all-to-all-start = ((bf16[4,64,1280]{2,1,0:T(8,128)(2,1)}), bf16[4,64,1280]{2,1,0:T(8,128)(2,1)S(1)}, u32[]{:S(2)}, u32[]{:S(2)}) async-start(bf16[4,64,1280]{2,1,0:T(8,128)(2,1)} %open_second.1), calls=%async_computation | async-start | bytes 1310720 | tf_op jit(solution)/shard_map/all_to_all | solution.py:274
  16.9 0.0 all-gather.2.cloned.1.call-start
  16.9 0.0 copy-done.11
  16.9 6.9 %collective-permute-start = (bf16[64,4096]{1,0:T(8,128)(2,1)S(1)}, bf16[64,4096]{1,0:T(8,128)(2,1)S(1)}, u32[]{:S(2)}, u32[]{:S(2)}) collective-permute-start(bf16[64,4096]{1,0:T(8,128)(2,1)S(1)} %bitcast.36), channel_id=1, source_target_pairs={{0,112},{16,0},{32,16},{48,32},{64,48},{80,64},{96,80},{112,96},{1... | collective-permute-start | bytes 1572872 | tf_op jit(solution)/shard_map/ppermute | solution.py:277
  23.8 0.0 copy-done.9
  23.8 0.0 copy-done.10
  23.8 6.6 %collective-permute-start.1 = (bf16[64,1024]{1,0:T(8,128)(2,1)S(1)}, bf16[64,1024]{1,0:T(8,128)(2,1)S(1)}, u32[]{:S(2)}, u32[]{:S(2)}) collective-permute-start(bf16[64,1024]{1,0:T(8,128)(2,1)S(1)} %pad_maximum_fusion.1), channel_id=1, source_target_pairs={{0,8},{1,9},{2,10},{3,11},{4,12},{5,13},{6,14},{7,15},{16,24},{17,... | collective-permute-start | bytes 393224 | tf_op jit(solution)/shard_map/ppermute | solution.py:281
  30.4 0.0 collective-permute-done.full
  30.4 1.4 pack.1
  31.8 0.0 copy-start.1
  31.8 0.8 collective-permute-done.1
  32.6 0.0 all-to-all-done
  32.6 0.7 pad_maximum_fusion
  33.3 0.0 all-gather.2.cloned.1.call-update
  33.3 4.6 %all-to-all-start.1 = ((bf16[4,64,1024]{2,1,0:T(8,128)(2,1)}), bf16[4,64,1024]{2,1,0:T(8,128)(2,1)S(1)}, u32[]{:S(2)}, u32[]{:S(2)}) async-start(bf16[4,64,1024]{2,1,0:T(8,128)(2,1)} %pack.1), calls=%async_computation.1 | async-start | bytes 1048576 | tf_op jit(solution)/shard_map/all_to_all | solution.py:274
  37.9 6.6 %collective-permute-start.3 = (bf16[256,256]{1,0:T(8,128)(2,1)S(1)}, bf16[256,256]{1,0:T(8,128)(2,1)S(1)}, u32[]{:S(2)}, u32[]{:S(2)}) collective-permute-start(bf16[256,256]{1,0:T(8,128)(2,1)S(1)} %slice.6), channel_id=1, source_target_pairs={{0,7},{1,6},{2,5},{3,4},{8,15},{9,14},{10,13},{11,12},{16,23},{17,... | collective-permute-start | bytes 393224 | tf_op jit(solution)/shard_map/ppermute | solution.py:294
  44.5 10.6 %collective-permute-start.4 = (bf16[256,256]{1,0:T(8,128)(2,1)S(1)}, bf16[256,256]{1,0:T(8,128)(2,1)S(1)}, u32[]{:S(2)}, u32[]{:S(2)}) collective-permute-start(bf16[256,256]{1,0:T(8,128)(2,1)S(1)} %slice.6), channel_id=1, source_target_pairs={{0,8},{1,9},{2,10},{3,11},{4,12},{5,13},{6,14},{7,15},{16,24},{17,... | collective-permute-start | bytes 393224 | tf_op jit(solution)/shard_map/ppermute | solution.py:294
  55.2 1.3 collective-permute-start.5
  56.5 0.0 copy-done.1
  56.5 0.0 collective-permute-done.3.kv1
  56.5 0.6 collective-permute-done.4.kv2
  57.1 3.5 %collective-permute-done.5.kv3 = bf16[256,256]{1,0:T(8,128)(2,1)S(1)} collective-permute-done((bf16[256,256]{1,0:T(8,128)(2,1)S(1)}, bf16[256,256]{1,0:T(8,128)(2,1)S(1)}, u32[]{:S(2)}, u32[]{:S(2)}) %collective-permute-start.5) | collective-permute-done | bytes 131104 | tf_op jit(solution)/shard_map/ppermute | solution.py:294
  60.6 6.6 %forward_second.1 = (bf16[256,1024]{1,0:T(8,128)(2,1)S(1)}, f32[8,256]{1,0:T(8,128)S(1)}) custom-call(s32[8]{0:T(128)S(1)} %stack.35.where, bf16[256,1280]{1,0:T(8,128)(2,1)S(1)} %bitcast.23, bf16[256,256]{1,0:T(8,128)(2,1)S(1)} %collective-permute-done.3.kv1, bf16[256,256]{1,0:T(8,128)(2,1)S(1)} %collective-permute-done.4.kv2, ...), custom_call_target="tpu_custom_call" | custom-call | flops 6400000000 | tf_op jit(solution)/shard_map/forward_second/pallas_call | solution.py:27
  67.1 0.0 all-to-all-done.1
  67.1 0.9 stats.1
  68.0 8.0 %all_to_all.25.stats = f32[4,8,256]{2,1,0:T(8,128)S(1)} all-to-all(f32[4,8,256]{2,1,0:T(8,128)S(1)} %stats.1), channel_id=1, replica_groups=mesh['dp'=4,'pipe'=8,'zhi'=2,'yhi'=2,'ylo'=4] {'ylo'}, dimensions={0} | all-to-all | bytes 65536 | tf_op jit(solution)/shard_map/all_to_all | solution.py:274
  76.0 0.0 copy-done.2
  76.0 7.3 %backward.1 = (bf16[256,1024]{1,0:T(8,128)(2,1)}, bf16[16,80,256]{2,1,0:T(8,128)(2,1)S(1)}, f32[4,256]{1,0:T(4,128)S(1)}) custom-call(s32[8]{0:T(128)S(1)} %stack.35.where, bf16[256,1280]{1,0:T(8,128)(2,1)S(1)} %bitcast.24, bf16[256,256]{1,0:T(8,128)(2,1)S(1)} %collective-permute-done.3.kv1, bf16[256,256]{1,0:T(8,128)(2,1)S(1)} %collective-permute-done.4.kv2, ...), custom_call_target="tpu_custom_call" | custom-call | flops 7000000000 | tf_op jit(solution)/shard_map/backward/pallas_call | solution.py:27
  83.3 0.0 copy-start
  83.3 0.8 copy-done
  84.1 3.5 %all-to-all-start.3 = ((bf16[4,64,1024]{2,1,0:T(8,128)(2,1)}), bf16[4,64,1024]{2,1,0:T(8,128)(2,1)S(1)}, u32[]{:S(2)}, u32[]{:S(2)}) async-start(bf16[4,64,1024]{2,1,0:T(8,128)(2,1)} %bitcast.18), calls=%async_computation.3 | async-start | bytes 1048576 | tf_op jit(solution)/shard_map/all_to_all | solution.py:274
  87.6 9.1 %psum.7.sums = f32[4,256]{1,0:T(4,128)} all-reduce(f32[4,256]{1,0:T(4,128)S(1)} %get-tuple-element.23), channel_id=1, replica_groups=mesh['dp'=4,'pipe'=8,'zhi'=2,'yhi'=2,'ylo'=4] {'dp'}, use_global_device_ids=true, to_apply=%region_0.0 | all-reduce | flops 1024 | bytes 8192 | tf_op jit(solution)/shard_map/psum | solution.py:335
  96.6 0.0 copy-start.3
  96.6 0.0 copy-start.6
  96.6 1.8 %insert.1 = bf16[16,80,256]{2,1,0:T(8,128)(2,1)} custom-call(s32[8]{0:T(128)} %copy-done.2, f32[4,256]{1,0:T(4,128)} %psum.7.sums, bf16[16,80,256]{2,1,0:T(8,128)(2,1)} %copy-done), custom_call_target="tpu_custom_call", output_to_operand_aliasing={{}: (2, {})} | custom-call | flops 1000000000 | tf_op jit(solution)/shard_map/insert/pallas_call | solution.py:337
  98.4 0.0 all-to-all-done.3.parts
  98.4 14.9 %all-to-all-start.4 = ((bf16[16,80,256]{2,1,0:T(8,128)(2,1)}), bf16[16,80,256]{2,1,0:T(8,128)(2,1)S(1)}, u32[]{:S(2)}, u32[]{:S(2)}) async-start(bf16[16,80,256]{2,1,0:T(8,128)(2,1)} %insert.1), calls=%async_computation.4 | async-start | bytes 1310720 | tf_op jit(solution)/shard_map/all_to_all | solution.py:274
  113.3 0.0 all-gather.2.cloned.1.call-done.kv
  113.3 0.0 copy-done.3
  113.3 0.0 copy-done.6
  113.3 0.0 copy-start.4
  113.3 1.6 %copy-done.4 = bf16[1024,1024]{1,0:T(8,128)(2,1)S(1)} copy-done((bf16[1024,1024]{1,0:T(8,128)(2,1)S(1)}, bf16[1024,1024]{1,0:T(8,128)(2,1)}, u32[]{:S(2)}) %copy-start.4) | copy-done | bytes 2097176
  114.9 7.0 %forward_first.1 = bf16[64,4096]{1,0:T(8,128)(2,1)S(1)} custom-call(s32[8]{0:T(128)S(1)} %copy-done.3, bf16[64,4096]{1,0:T(8,128)(2,1)S(1)} %bitcast.28, bf16[1024,1024]{1,0:T(8,128)(2,1)S(1)} %copy-done.4, bf16[1,4096]{1,0:T(2,128)(2,1)S(1)} %copy-done.1), custom_call_target="tpu_custom_call" | custom-call | flops 7000000000 | tf_op jit(solution)/shard_map/forward_first/pallas_call | solution.py:27
  122.0 10.5 %collective-permute-start.2 = (bf16[64,4096]{1,0:T(8,128)(2,1)S(1)}, bf16[64,4096]{1,0:T(8,128)(2,1)S(1)}, u32[]{:S(2)}, u32[]{:S(2)}) collective-permute-start(bf16[64,4096]{1,0:T(8,128)(2,1)S(1)} %forward_first.1), channel_id=1, source_target_pairs={{0,16},{16,32},{32,48},{48,64},{64,80},{80,96},{96,112},{112,0},{1... | collective-permute-start | bytes 1572872 | tf_op jit(solution)/shard_map/ppermute | solution.py:277
  132.5 1.4 join.1
  133.9 0.0 all-to-all-done.4.parts
  133.9 1.2 gather.1
  135.1 5.5 %collective-permute-done.2 = bf16[64,4096]{1,0:T(8,128)(2,1)S(1)} collective-permute-done((bf16[64,4096]{1,0:T(8,128)(2,1)S(1)}, bf16[64,4096]{1,0:T(8,128)(2,1)S(1)}, u32[]{:S(2)}, u32[]{:S(2)}) %collective-permute-start.2) | collective-permute-done | bytes 524320 | tf_op jit(solution)/shard_map/ppermute | solution.py:277
  140.6 0.8 copy.16
  (3 shorter events, 0.0 us)
Async XLA Ops:
  7.3 68.7 %copy-start.2 = (s32[8]{0:T(128)}, s32[8]{0:T(128)S(1)}, u32[]{:S(2)}) copy-start(s32[8]{0:T(128)S(1)} %stack.35.where) | copy-start | bytes 100
  7.3 1.0 copy-start.5
  8.3 0.8 copy-start.7
  9.2 0.8 copy-start.8
  10.0 6.9 %copy-start.11 = (bf16[1,1,64,4096]{3,2,1,0:T(8,128)(2,1)S(1)}, bf16[1,1,64,4096]{3,2,1,0:T(8,128)(2,1)}, u32[]{:S(2)}) copy-start(bf16[1,1,64,4096]{3,2,1,0:T(8,128)(2,1)} %param.14) | copy-start | bytes 1572868
  10.0 13.8 %copy-start.9 = (bf16[1,1,64,512]{3,2,1,0:T(8,128)(2,1)S(1)}, bf16[1,1,64,512]{3,2,1,0:T(8,128)(2,1)}, u32[]{:S(2)}) copy-start(bf16[1,1,64,512]{3,2,1,0:T(8,128)(2,1)} %param.10) | copy-start | bytes 196612
  10.0 13.8 %copy-start.10 = (bf16[1,1,64,512]{3,2,1,0:T(8,128)(2,1)S(1)}, bf16[1,1,64,512]{3,2,1,0:T(8,128)(2,1)}, u32[]{:S(2)}) copy-start(bf16[1,1,64,512]{3,2,1,0:T(8,128)(2,1)} %param.9) | copy-start | bytes 196612
  11.4 21.1 %all-to-all-start = ((bf16[4,64,1280]{2,1,0:T(8,128)(2,1)}), bf16[4,64,1280]{2,1,0:T(8,128)(2,1)S(1)}, u32[]{:S(2)}, u32[]{:S(2)}) async-start(bf16[4,64,1280]{2,1,0:T(8,128)(2,1)} %open_second.1), calls=%async_computation | async-start | bytes 1310720 | tf_op jit(solution)/shard_map/all_to_all | solution.py:274
  16.9 96.4 %all-gather.2.cloned.1.call-start = ((), (), s32[]{:S(2)}) async-start(), calls=%async_computation.5 | async-start | bytes 2359296 | tf_op jit(solution)/shard_map/all_gather | solution.py:296
  16.9 13.6 %collective-permute-start = (bf16[64,4096]{1,0:T(8,128)(2,1)S(1)}, bf16[64,4096]{1,0:T(8,128)(2,1)S(1)}, u32[]{:S(2)}, u32[]{:S(2)}) collective-permute-start(bf16[64,4096]{1,0:T(8,128)(2,1)S(1)} %bitcast.36), channel_id=1, source_target_pairs={{0,112},{16,0},{32,16},{48,32},{64,48},{80,64},{96,80},{112,96},{1... | collective-permute-start | bytes 1572872 | tf_op jit(solution)/shard_map/ppermute | solution.py:277
  23.8 8.7 %collective-permute-start.1 = (bf16[64,1024]{1,0:T(8,128)(2,1)S(1)}, bf16[64,1024]{1,0:T(8,128)(2,1)S(1)}, u32[]{:S(2)}, u32[]{:S(2)}) collective-permute-start(bf16[64,1024]{1,0:T(8,128)(2,1)S(1)} %pad_maximum_fusion.1), channel_id=1, source_target_pairs={{0,8},{1,9},{2,10},{3,11},{4,12},{5,13},{6,14},{7,15},{16,24},{17,... | collective-permute-start | bytes 393224 | tf_op jit(solution)/shard_map/ppermute | solution.py:281
  31.8 24.7 %copy-start.1 = (bf16[1,4096]{1,0:T(2,128)(2,1)S(1)}, bf16[1,4096]{1,0:T(2,128)(2,1)}, u32[]{:S(2)}) copy-start(bf16[1,4096]{1,0:T(2,128)(2,1)} %gain.1) | copy-start | bytes 24580
  33.3 33.8 %all-to-all-start.1 = ((bf16[4,64,1024]{2,1,0:T(8,128)(2,1)}), bf16[4,64,1024]{2,1,0:T(8,128)(2,1)S(1)}, u32[]{:S(2)}, u32[]{:S(2)}) async-start(bf16[4,64,1024]{2,1,0:T(8,128)(2,1)} %pack.1), calls=%async_computation.1 | async-start | bytes 1048576 | tf_op jit(solution)/shard_map/all_to_all | solution.py:274
  37.9 18.6 %collective-permute-start.3 = (bf16[256,256]{1,0:T(8,128)(2,1)S(1)}, bf16[256,256]{1,0:T(8,128)(2,1)S(1)}, u32[]{:S(2)}, u32[]{:S(2)}) collective-permute-start(bf16[256,256]{1,0:T(8,128)(2,1)S(1)} %slice.6), channel_id=1, source_target_pairs={{0,7},{1,6},{2,5},{3,4},{8,15},{9,14},{10,13},{11,12},{16,23},{17,... | collective-permute-start | bytes 393224 | tf_op jit(solution)/shard_map/ppermute | solution.py:294
  44.5 12.6 %collective-permute-start.4 = (bf16[256,256]{1,0:T(8,128)(2,1)S(1)}, bf16[256,256]{1,0:T(8,128)(2,1)S(1)}, u32[]{:S(2)}, u32[]{:S(2)}) collective-permute-start(bf16[256,256]{1,0:T(8,128)(2,1)S(1)} %slice.6), channel_id=1, source_target_pairs={{0,8},{1,9},{2,10},{3,11},{4,12},{5,13},{6,14},{7,15},{16,24},{17,... | collective-permute-start | bytes 393224 | tf_op jit(solution)/shard_map/ppermute | solution.py:294
  55.2 5.4 %collective-permute-start.5 = (bf16[256,256]{1,0:T(8,128)(2,1)S(1)}, bf16[256,256]{1,0:T(8,128)(2,1)S(1)}, u32[]{:S(2)}, u32[]{:S(2)}) collective-permute-start(bf16[256,256]{1,0:T(8,128)(2,1)S(1)} %slice.6), channel_id=1, source_target_pairs={{0,15},{1,14},{2,13},{3,12},{4,11},{5,10},{6,9},{7,8},{16,31},{17,... | collective-permute-start | bytes 393224 | tf_op jit(solution)/shard_map/ppermute | solution.py:294
  83.3 0.8 copy-start
  84.1 14.3 %all-to-all-start.3 = ((bf16[4,64,1024]{2,1,0:T(8,128)(2,1)}), bf16[4,64,1024]{2,1,0:T(8,128)(2,1)S(1)}, u32[]{:S(2)}, u32[]{:S(2)}) async-start(bf16[4,64,1024]{2,1,0:T(8,128)(2,1)} %bitcast.18), calls=%async_computation.3 | async-start | bytes 1048576 | tf_op jit(solution)/shard_map/all_to_all | solution.py:274
  96.6 16.7 %copy-start.3 = (s32[8]{0:T(128)S(1)}, s32[8]{0:T(128)}, u32[]{:S(2)}) copy-start(s32[8]{0:T(128)} %copy-done.2) | copy-start | bytes 100
  96.6 16.7 %copy-start.6 = (bf16[1,1,64,4096]{3,2,1,0:T(8,128)(2,1)S(1)}, bf16[1,1,64,4096]{3,2,1,0:T(8,128)(2,1)}, u32[]{:S(2)}) copy-start(bf16[1,1,64,4096]{3,2,1,0:T(8,128)(2,1)} %param.8) | copy-start | bytes 1572868
  98.4 35.5 %all-to-all-start.4 = ((bf16[16,80,256]{2,1,0:T(8,128)(2,1)}), bf16[16,80,256]{2,1,0:T(8,128)(2,1)S(1)}, u32[]{:S(2)}, u32[]{:S(2)}) async-start(bf16[16,80,256]{2,1,0:T(8,128)(2,1)} %insert.1), calls=%async_computation.4 | async-start | bytes 1310720 | tf_op jit(solution)/shard_map/all_to_all | solution.py:274
  113.3 1.6 %copy-start.4 = (bf16[1024,1024]{1,0:T(8,128)(2,1)S(1)}, bf16[1024,1024]{1,0:T(8,128)(2,1)}, u32[]{:S(2)}) copy-start(bf16[1024,1024]{1,0:T(8,128)(2,1)} %all-gather.2.cloned.1.call-done.kv) | copy-start | bytes 6291460
  122.0 18.6 %collective-permute-start.2 = (bf16[64,4096]{1,0:T(8,128)(2,1)S(1)}, bf16[64,4096]{1,0:T(8,128)(2,1)S(1)}, u32[]{:S(2)}, u32[]{:S(2)}) collective-permute-start(bf16[64,4096]{1,0:T(8,128)(2,1)S(1)} %forward_first.1), channel_id=1, source_target_pairs={{0,16},{16,32},{32,48},{48,64},{64,80},{80,96},{96,112},{112,0},{1... | collective-permute-start | bytes 1572872 | tf_op jit(solution)/shard_map/ppermute | solution.py:277
Sparse Core Ops, SparseCore 0:
  33.4 50.4 all-gather.1

commit v5 on v4

--- a/solution.py
+++ b/solution.py
@@ -12,6 +12,7 @@
 HD = 128
 EPSILON = 1e-05
 SCALE = 1.0 / math.sqrt(HD)
+BINARY = SCALE / math.log(2.0)
 F32 = jnp.float32
 BF16 = jnp.bfloat16
 
@@ -66,13 +67,22 @@
     return pl.ds(pl.multiple_of(head_at(where, place) * width, width), width)
 
 
-def attend(keys, values_t, bias, queries):
-    scores = dot_nt(keys, queries) + bias[...]
+def attend(scores, values_t, bias):
+    scores = scores + bias[...]
     highest = jnp.max(scores, axis=0, keepdims=True)
-    exponent = jnp.exp((scores - highest) * SCALE)
+    exponent = jnp.exp2((scores - highest) * BINARY)
     total = jnp.sum(exponent, axis=0, keepdims=True)
     out = dot_nn(values_t, exponent.astype(BF16)) * (1.0 / total)
-    return out.T.astype(BF16), highest * SCALE + jnp.log(total)
+    return out.T.astype(BF16), highest * BINARY + jnp.log2(total)
+
+
+def ahead_of(count, make):
+    after = make(0)
+    for i in range(count):
+        now = after
+        if i + 1 < count:
+            after = make(i + 1)
+        yield i, now
 
 
 def set_bias(where, bias):
@@ -123,24 +133,20 @@
     share[...] = terms[0:1] + terms[1:2] + terms[2:3]
 
 
-def forward_body(heads, where, q, kv1, kv2, kv3, out, lse, k_s, v_s, bias):
+def forward_body(heads, where, q, kv1, kv2, kv3, up, gain, out, lse, stats, k_s, v_s, bias):
     set_bias(where, bias)
     blocks = (q.at[:, heads * HD :], kv1, kv2, kv3)
     load_keys(where, blocks, 0, k_s)
     load_keys(where, blocks, HD, v_s)
     values_t = v_s[...].T
-    for h in range(heads):
-        cols = slice(h * HD, (h + 1) * HD)
-        out[:, cols], lse[h : h + 1, :] = attend(k_s[...], values_t, bias, q[:, cols])
-
-
-def stats_body(heads, where, act, up, gain, stats):
-    n = act.shape[0]
+    n = bias.shape[1]
     square = jnp.zeros((n, HD), F32)
     cross = jnp.zeros((n, HD), F32)
-    for h in range(heads):
+    for h, scores in ahead_of(heads, lambda h: dot_nt(k_s[...], q[:, h * HD : (h + 1) * HD])):
         cols = slice(h * HD, (h + 1) * HD)
-        value = act[:, cols].astype(F32)
+        result, lse[h : h + 1, :] = attend(scores, values_t, bias)
+        out[:, cols] = result
+        value = result.astype(F32)
         square = square + value * value
         cross = cross + gain[:, cols].astype(F32) * up[:, cols].astype(F32) * value
     rows = jnp.concatenate(
@@ -152,7 +158,7 @@
 
 def backward_body(
     heads, width, where, q, kv1, kv2, kv3, up, gain, act, lse, stats,
-    dq, dkv, sums, k_s, v_s, bias, dk_s, dv_s,
+    dq, dkv, k_s, v_s, bias, dk_s, dv_s,
 ):
     set_bias(where, bias)
     blocks = (q.at[:, heads * HD :], kv1, kv2, kv3)
@@ -163,19 +169,17 @@
     inverse_row = lax.rsqrt(totals[0:1] / width + EPSILON)
     inverse = column(inverse_row)
     shrink = column(inverse_row * inverse_row * inverse_row * (totals[1:2] / width))
-    per = heads // FOUR
+    sums = []
     for h in range(heads):
         cols = slice(h * HD, (h + 1) * HD)
         queries = q[:, cols]
         act_h = act[:, cols].astype(F32)
         upstream = up[:, cols].astype(F32)
-        sums[h // per : h // per + 1, (h % per) * HD : (h % per + 1) * HD] = jnp.sum(
-            upstream * act_h * inverse, axis=0, keepdims=True
-        )
+        sums.append(jnp.sum(upstream * act_h * inverse, axis=0, keepdims=True))
         grad = (gain[:, cols].astype(F32) * upstream * inverse - act_h * shrink).astype(BF16)
         dots = row_of(grad.astype(F32) * act_h)
-        scores = dot_nt(k_s[...], queries) * SCALE + bias[...]
-        probs = jnp.exp(scores - lse[h : h + 1, :])
+        scores = dot_nt(k_s[...], queries) * BINARY + bias[...]
+        probs = jnp.exp2(scores - lse[h : h + 1, :])
         grad_weights = dot_nt(v_s[...], grad)
         grad_scores = (probs * (grad_weights - dots) * SCALE).astype(BF16)
         dv = dot_nn(probs.astype(BF16), grad)
@@ -188,25 +192,22 @@
             dk_s[...] += dk
         dq[:, cols] = dot_nn(keys_t, grad_scores).T.astype(BF16)
     tokens = dk_s.shape[0] // dkv.shape[0]
+    per = heads // FOUR
+    extra = dkv.shape[1] - tokens
     for s in range(dkv.shape[0]):
         rows = slice(s * tokens, (s + 1) * tokens)
         dkv[s, :tokens, :HD] = dk_s[rows].astype(BF16)
         dkv[s, :tokens, HD:] = dv_s[rows].astype(BF16)
-        dkv[s, tokens:, :] = jnp.zeros((dkv.shape[1] - tokens, 2 * HD), BF16)
-
-
-def insert_body(where, sums, dkv, out):
-    del dkv
-    for s in range(out.shape[0]):
-        value = sums[s % FOUR : s % FOUR + 1]
+        j = s % FOUR
+        value = jnp.concatenate(sums[j * per : (j + 1) * per], axis=1)
         value = jnp.where(where[2] == s // FOUR, value, 0.0)
         terms = []
         for _ in range(3):
             term = value.astype(BF16).astype(F32)
             terms.append(term)
             value = value - term
-        terms.append(jnp.zeros((out.shape[1] - 3, value.shape[1]), F32))
-        out[s] = jnp.concatenate(terms, axis=0).astype(BF16)
+        terms.append(jnp.zeros((extra - 3, value.shape[1]), F32))
+        dkv[s, tokens:] = jnp.concatenate(terms, axis=0).astype(BF16)
 
 
 def first_body(where, q, kv, gain, out, k_s, vt_s, q_s, o_s, bias):
@@ -231,7 +232,7 @@
             start = g * (heads // kv_heads) + part * together
             for i in range(together):
                 q_s[i * tokens : (i + 1) * tokens, :] = q[:, (start + i) * HD : (start + i + 1) * HD]
-            result, _ = attend(k_s[...], vt_s[...], bias, q_s[...])
+            result, _ = attend(dot_nt(k_s[...], q_s[...]), vt_s[...], bias)
             for i in range(together):
                 piece = result[i * tokens : (i + 1) * tokens]
                 o_s[:, (start + i) * HD : (start + i + 1) * HD] = piece
@@ -279,12 +280,20 @@
     up_raw = along(grad_output[0, 0], "pipe", -1, pipes)
     kv1 = jnp.concatenate([key_first[0, 0], value_first[0, 0]], axis=1)
     other = lax.ppermute(kv1, "zhi", [(0, 1)])
-    qkv = call(
+    qkv = pl.pallas_call(
         open_body,
-        sds((FOUR, tokens, cols + 2 * HD), BF16),
-        (where, query_second[0, 0], key_second[0, 0], value_second[0, 0]),
+        grid=(1,),
+        in_specs=[
+            SMEM,
+            pl.BlockSpec((tokens, width), lambda i: (0, 0)),
+            pl.BlockSpec((tokens, kv_width), lambda i: (0, 0)),
+            pl.BlockSpec((tokens, kv_width), lambda i: (0, 0)),
+        ],
+        out_specs=pl.BlockSpec((FOUR, tokens, cols + 2 * HD), lambda i: (0, 0, 0)),
+        out_shape=sds((FOUR, tokens, cols + 2 * HD), BF16),
+        cost_estimate=pl.CostEstimate(flops=10**9, bytes_accessed=0, transcendentals=0),
         name="open_second",
-    )
+    )(where, query_second[0, 0], key_second[0, 0], value_second[0, 0])
     qkv = swap(qkv, "ylo")
     up = call(
         pack_body, sds((FOUR, tokens, cols), BF16), (where, up_raw), micros=1.4, name="pack"
@@ -302,49 +311,26 @@
     bias = pltpu.VMEM((length, n), F32)
     total = pltpu.VMEM((length, HD), F32)
 
-    out2, lse = call(
+    out2, lse, stats = call(
         functools.partial(forward_body, heads),
-        (sds((n, cols), BF16), sds((heads, n), F32)),
-        (where, qkv, *kvs),
+        (sds((n, cols), BF16), sds((heads, n), F32), sds((FOUR, 8, n), F32)),
+        (where, qkv, *kvs, up, gain_cols),
         [long, long, bias],
         micros=6.4,
         name="forward_second",
     )
-    stats = swap(
-        call(
-            functools.partial(stats_body, heads),
-            sds((FOUR, 8, n), F32),
-            (where, out2, up, gain_cols),
-            name="stats",
-        ),
-        "ylo",
-    )
-    dq, dkv, sums = call(
+    stats = swap(stats, "ylo")
+    dq, dkv = call(
         functools.partial(backward_body, heads, width),
         (
             sds((n, cols), BF16),
             sds((places, tokens + 16, 2 * HD), BF16),
-            sds((FOUR, 2 * HD), F32),
         ),
         (where, qkv, *kvs, up, gain_cols, out2, lse, stats),
         [long, long, bias, total, total],
         micros=7.0,
         name="backward",
     )
-    dq = swap(dq.reshape(FOUR, tokens, cols), "ylo")
-    sums = lax.psum(sums, "dp")
-    below = pl.BlockSpec((places, 16, 2 * HD), lambda i: (0, tokens // 16, 0))
-    dkv = pl.pallas_call(
-        insert_body,
-        grid=(1,),
-        in_specs=[SMEM, pl.BlockSpec((FOUR, 2 * HD), lambda i: (0, 0)), below],
-        out_specs=below,
-        out_shape=sds(dkv.shape, BF16),
-        input_output_aliases={2: 0},
-        cost_estimate=pl.CostEstimate(flops=10**9, bytes_accessed=0, transcendentals=0),
-        name="insert",
-    )(where, sums, dkv)
-    dkv, dq = lax.optimization_barrier((dkv, dq))
     dkv = swap(dkv, SEQ)
 
     normed = call(
@@ -362,13 +348,15 @@
         name="forward_first",
     )
     next_input = along(normed, "pipe", 1, pipes)
+    dq, dkv, normed = lax.optimization_barrier((dq, dkv, normed))
+    dq = swap(dq.reshape(FOUR, tokens, cols), "ylo")
     grad_key, grad_value, share = call(
         gather_body,
         (sds((tokens, kv_width), BF16),) * 2 + (sds((1, 2 * HD), F32),),
         (where, dkv),
         name="gather",
     )
-    grad_gain = share
+    grad_gain = lax.psum(share, "dp")
     grad_query = call(join_body, sds((tokens, width), BF16), (where, dq), name="join")
     return (
         next_input[None, None],

time: 150 us -> 145 us (0.967)
  local copies, waits for them, and re-layouts: 6.07 us -> 3.02 us
  Pallas kernels: 28.9 us -> 26.4 us
  waiting for transfers between devices: 10.3 us -> 12.8 us
  starting transfers between devices: 70.9 us -> 69.4 us
    all_to_all x4, waiting for transfers between devices: 0.01 us -> 7.96 us  [swap(): return lax.all_to_all(packed, axes, split_axis=0, concat_axis=0, tiled=True)]
    ppermute x2, waiting for transfers between devices: 5.46 us -> 0.01 us  [along(): lax.ppermute(value, axis, [(i, (i + step) % count) for i in range(count)])]
    unnamed x25 -> x15, local copies, waits for them, and re-layouts: 5.97 us -> 2.4 us
    all_to_all x4, starting transfers between devices: 28.3 us -> 25.4 us  [swap(): return lax.all_to_all(packed, axes, split_axis=0, concat_axis=0, tiled=True)]
    pallas_call x8 -> x6, Pallas kernels: 27.2 us -> 24.4 us  [call(): pl.pallas_call(body, out_shape=outs, in_specs=[SMEM] + [VMEM] * (len(inpu...]
  transfers between devices with their start and end apart: 11 -> 11, of which waited for: 4 -> 4; matrix products, arithmetic and copies ran while one was open for 0% -> 0% of each run, Pallas kernels for 19% -> 16%
where the time goes in v5:
time: 145 us; the launch traced here: 144 us
  starting transfers between devices  69.4 us (48%)
  Pallas kernels  26.4 us (18%)
  blocking collectives  17.6 us (12%)
  between operations  14.2 us (10%)
  waiting for transfers between devices  12.8 us (9%)
  local copies, waits for them, and re-layouts  3.02 us (2%)
    all_to_all x4, starting transfers between devices, swap(): return lax.all_to_all(packed, axes, split_axis=0, concat_axis=0, tiled=True)  25.4 us
    pallas_call x6, Pallas kernels, call(): pl.pallas_call(body, out_shape=outs, in_specs=[SMEM] + [VMEM] * (len(inpu...  24.4 us
    ppermute x2, starting transfers between devices, along(): lax.ppermute(value, axis, [(i, (i + step) % count) for i in range(count)])  18.9 us
    ppermute x3, starting transfers between devices, local(): lax.ppermute(qkv[:, cols:], SEQ, pairs)  18.5 us
    psum x1, blocking collectives, local(): grad_gain = lax.psum(share, 'dp')  9.44 us
    all_to_all x1, blocking collectives, swap(): return lax.all_to_all(packed, axes, split_axis=0, concat_axis=0, tiled=True)  8.15 us
    all_to_all x4, waiting for transfers between devices, swap(): return lax.all_to_all(packed, axes, split_axis=0, concat_axis=0, tiled=True)  7.96 us
    ppermute x1, starting transfers between devices, local(): other = lax.ppermute(kv1, 'zhi', [(0, 1)])  6.59 us
  transfers between devices with their start and end apart: 11, of which 4 were waited for; matrix products, arithmetic and copies ran while one was open for 0% of the time, Pallas kernels for 16%

profile of v5, /device:TPU:1, one launch (start us, length us, event | category | flops | bytes accessed | tf_op | source)
XLA Modules:
  0.0 144.2 jit_solution(6978563342219471212)
XLA Ops:
  7.2 0.6 stack.35.where
  7.8 0.0 copy-start.6
  7.8 0.0 copy-start.4
  7.8 0.0 copy-start.5
  7.8 0.0 copy-start.1
  7.8 2.1 %open_second.1 = bf16[4,64,1280]{2,1,0:T(8,128)(2,1)} custom-call(s32[8]{0:T(128)} %stack.35.where, bf16[64,4096]{1,0:T(8,128)(2,1)} %bitcast.33, bf16[64,512]{1,0:T(8,128)(2,1)} %bitcast.35, bf16[64,512]{1,0:T(8,128)(2,1)} %bitcast.36), custom_call_target="tpu_custom_call" | custom-call | flops 1000000000 | tf_op jit(solution)/shard_map/open_second/pallas_call | solution.py:283
  9.9 5.4 %all-to-all-start = ((bf16[4,64,1280]{2,1,0:T(8,128)(2,1)}), bf16[4,64,1280]{2,1,0:T(8,128)(2,1)S(1)}, u32[]{:S(2)}, u32[]{:S(2)}) async-start(bf16[4,64,1280]{2,1,0:T(8,128)(2,1)} %open_second.1), calls=%async_computation | async-start | bytes 1310720 | tf_op jit(solution)/shard_map/all_to_all | solution.py:275
  15.3 0.0 all-gather.2.cloned.1.call-start
  15.3 0.0 copy-done.6
  15.3 6.9 %collective-permute-start = (bf16[64,4096]{1,0:T(8,128)(2,1)S(1)}, bf16[64,4096]{1,0:T(8,128)(2,1)S(1)}, u32[]{:S(2)}, u32[]{:S(2)}) collective-permute-start(bf16[64,4096]{1,0:T(8,128)(2,1)S(1)} %bitcast.34), channel_id=1, source_target_pairs={{0,112},{16,0},{32,16},{48,32},{64,48},{80,64},{96,80},{112,96},{1... | collective-permute-start | bytes 1572872 | tf_op jit(solution)/shard_map/ppermute | solution.py:278
  22.2 0.0 copy-done.4
  22.2 0.0 copy-done.5
  22.3 6.6 %collective-permute-start.1 = (bf16[64,1024]{1,0:T(8,128)(2,1)S(1)}, bf16[64,1024]{1,0:T(8,128)(2,1)S(1)}, u32[]{:S(2)}, u32[]{:S(2)}) collective-permute-start(bf16[64,1024]{1,0:T(8,128)(2,1)S(1)} %pad_maximum_fusion.1), channel_id=1, source_target_pairs={{0,8},{1,9},{2,10},{3,11},{4,12},{5,13},{6,14},{7,15},{16,24},{17,... | collective-permute-start | bytes 393224 | tf_op jit(solution)/shard_map/ppermute | solution.py:282
  28.9 0.0 collective-permute-done.full
  28.9 0.0 copy-done.1
  28.9 1.4 pack.1
  30.2 0.0 copy-start
  30.2 0.8 collective-permute-done.1
  31.0 0.0 all-to-all-done
  31.0 0.7 pad_maximum_fusion
  31.7 0.0 all-gather.2.cloned.1.call-update
  31.8 4.6 %all-to-all-start.1 = ((bf16[4,64,1024]{2,1,0:T(8,128)(2,1)}), bf16[4,64,1024]{2,1,0:T(8,128)(2,1)S(1)}, u32[]{:S(2)}, u32[]{:S(2)}) async-start(bf16[4,64,1024]{2,1,0:T(8,128)(2,1)} %pack.1), calls=%async_computation.1 | async-start | bytes 1048576 | tf_op jit(solution)/shard_map/all_to_all | solution.py:275
  36.4 6.6 %collective-permute-start.3 = (bf16[256,256]{1,0:T(8,128)(2,1)S(1)}, bf16[256,256]{1,0:T(8,128)(2,1)S(1)}, u32[]{:S(2)}, u32[]{:S(2)}) collective-permute-start(bf16[256,256]{1,0:T(8,128)(2,1)S(1)} %slice.6), channel_id=1, source_target_pairs={{0,7},{1,6},{2,5},{3,4},{8,15},{9,14},{10,13},{11,12},{16,23},{17,... | collective-permute-start | bytes 393224 | tf_op jit(solution)/shard_map/ppermute | solution.py:303
  43.0 10.6 %collective-permute-start.4 = (bf16[256,256]{1,0:T(8,128)(2,1)S(1)}, bf16[256,256]{1,0:T(8,128)(2,1)S(1)}, u32[]{:S(2)}, u32[]{:S(2)}) collective-permute-start(bf16[256,256]{1,0:T(8,128)(2,1)S(1)} %slice.6), channel_id=1, source_target_pairs={{0,8},{1,9},{2,10},{3,11},{4,12},{5,13},{6,14},{7,15},{16,24},{17,... | collective-permute-start | bytes 393224 | tf_op jit(solution)/shard_map/ppermute | solution.py:303
  53.6 1.3 collective-permute-start.5
  54.9 0.0 copy-done
  55.0 0.0 collective-permute-done.3.kv1
  55.0 0.6 collective-permute-done.4.kv2
  55.5 3.5 %collective-permute-done.5.kv3 = bf16[256,256]{1,0:T(8,128)(2,1)S(1)} collective-permute-done((bf16[256,256]{1,0:T(8,128)(2,1)S(1)}, bf16[256,256]{1,0:T(8,128)(2,1)S(1)}, u32[]{:S(2)}, u32[]{:S(2)}) %collective-permute-start.5) | collective-permute-done | bytes 131104 | tf_op jit(solution)/shard_map/ppermute | solution.py:303
  59.0 0.0 all-to-all-done.1
  59.0 6.4 %forward_second.1 = (bf16[256,1024]{1,0:T(8,128)(2,1)S(1)}, f32[8,256]{1,0:T(8,128)S(1)}, f32[4,8,256]{2,1,0:T(8,128)S(1)}) custom-call(s32[8]{0:T(128)S(1)} %copy-done.1, bf16[256,1280]{1,0:T(8,128)(2,1)S(1)} %bitcast.23, bf16[256,256]{1,0:T(8,128)(2,1)S(1)} %collective-permute-done.3.kv1, bf16[256,256]{1,0:T(8,128)(2,1)S(1)} %collective-permute-done.4.kv2, ...), custom_call_target="tpu_custom_call" | custom-call | flops 6400000000 | tf_op jit(solution)/shard_map/forward_second/pallas_call | solution.py:28
  65.4 8.1 %all_to_all.25.stats = f32[4,8,256]{2,1,0:T(8,128)S(1)} all-to-all(f32[4,8,256]{2,1,0:T(8,128)S(1)} %get-tuple-element.23), channel_id=1, replica_groups=mesh['dp'=4,'pipe'=8,'zhi'=2,'yhi'=2,'ylo'=4] {'ylo'}, dimensions={0} | all-to-all | bytes 65536 | tf_op jit(solution)/shard_map/all_to_all | solution.py:275
  73.6 0.0 copy-start.3
  73.6 7.4 %backward.1 = (bf16[256,1024]{1,0:T(8,128)(2,1)}, bf16[16,80,256]{2,1,0:T(8,128)(2,1)}) custom-call(s32[8]{0:T(128)S(1)} %copy-done.1, bf16[256,1280]{1,0:T(8,128)(2,1)S(1)} %bitcast.24, bf16[256,256]{1,0:T(8,128)(2,1)S(1)} %collective-permute-done.3.kv1, bf16[256,256]{1,0:T(8,128)(2,1)S(1)} %collective-permute-done.4.kv2, ...), custom_call_target="tpu_custom_call" | custom-call | flops 7000000000 | tf_op jit(solution)/shard_map/backward/pallas_call | solution.py:28
  80.9 11.9 %all-to-all-start.3 = ((bf16[16,80,256]{2,1,0:T(8,128)(2,1)}), bf16[16,80,256]{2,1,0:T(8,128)(2,1)S(1)}, u32[]{:S(2)}, u32[]{:S(2)}) async-start(bf16[16,80,256]{2,1,0:T(8,128)(2,1)} %get-tuple-element.25), calls=%async_computation.3 | async-start | bytes 1310720 | tf_op jit(solution)/shard_map/all_to_all | solution.py:275
  92.8 0.0 all-gather.2.cloned.1.call-done.kv
  92.9 0.0 copy-done.3
  92.9 0.0 copy-start.2
  92.9 1.6 %copy-done.2 = bf16[1024,1024]{1,0:T(8,128)(2,1)S(1)} copy-done((bf16[1024,1024]{1,0:T(8,128)(2,1)S(1)}, bf16[1024,1024]{1,0:T(8,128)(2,1)}, u32[]{:S(2)}) %copy-start.2) | copy-done | bytes 2097176
  94.5 6.6 %forward_first.1 = bf16[64,4096]{1,0:T(8,128)(2,1)S(1)} custom-call(s32[8]{0:T(128)S(1)} %copy-done.1, bf16[64,4096]{1,0:T(8,128)(2,1)S(1)} %bitcast.27, bf16[1024,1024]{1,0:T(8,128)(2,1)S(1)} %copy-done.2, bf16[1,4096]{1,0:T(2,128)(2,1)S(1)} %copy-done), custom_call_target="tpu_custom_call" | custom-call | flops 7000000000 | tf_op jit(solution)/shard_map/forward_first/pallas_call | solution.py:28
  101.1 8.0 %all-to-all-done.3.parts = bf16[16,80,256]{2,1,0:T(8,128)(2,1)S(1)} async-done(((bf16[16,80,256]{2,1,0:T(8,128)(2,1)}), bf16[16,80,256]{2,1,0:T(8,128)(2,1)S(1)}, u32[]{:S(2)}, u32[]{:S(2)}) %all-to-all-start.3) | async-done | bytes 655392 | tf_op jit(solution)/shard_map/all_to_all | solution.py:275
  109.0 3.5 %all-to-all-start.4 = ((bf16[4,64,1024]{2,1,0:T(8,128)(2,1)}), bf16[4,64,1024]{2,1,0:T(8,128)(2,1)S(1)}, u32[]{:S(2)}, u32[]{:S(2)}) async-start(bf16[4,64,1024]{2,1,0:T(8,128)(2,1)} %bitcast.18), calls=%async_computation.4 | async-start | bytes 1048576 | tf_op jit(solution)/shard_map/all_to_all | solution.py:275
  112.5 12.0 %collective-permute-start.2 = (bf16[64,4096]{1,0:T(8,128)(2,1)S(1)}, bf16[64,4096]{1,0:T(8,128)(2,1)S(1)}, u32[]{:S(2)}, u32[]{:S(2)}) collective-permute-start(bf16[64,4096]{1,0:T(8,128)(2,1)S(1)} %forward_first.1), channel_id=1, source_target_pairs={{0,16},{16,32},{32,48},{48,64},{64,80},{80,96},{96,112},{112,0},{1... | collective-permute-start | bytes 1572872 | tf_op jit(solution)/shard_map/ppermute | solution.py:278
  124.5 1.3 gather.1
  125.8 9.4 %psum.7 = f32[1,256]{1,0:T(1,128)} all-reduce(f32[1,256]{1,0:T(1,128)S(1)} %get-tuple-element.30), channel_id=1, replica_groups=mesh['dp'=4,'pipe'=8,'zhi'=2,'yhi'=2,'ylo'=4] {'dp'}, use_global_device_ids=true, to_apply=%region_0.0 | all-reduce | flops 256 | bytes 2048 | tf_op jit(solution)/shard_map/psum | solution.py:359
  135.2 0.0 collective-permute-done.2
  135.2 0.0 all-to-all-done.4.parts
  135.2 1.4 join.1
  136.6 0.8 copy.14
  (3 shorter events, 0.0 us)
Async XLA Ops:
  7.8 7.5 %copy-start.6 = (bf16[1,1,64,4096]{3,2,1,0:T(8,128)(2,1)S(1)}, bf16[1,1,64,4096]{3,2,1,0:T(8,128)(2,1)}, u32[]{:S(2)}) copy-start(bf16[1,1,64,4096]{3,2,1,0:T(8,128)(2,1)} %param.14) | copy-start | bytes 1572868
  7.8 14.4 %copy-start.4 = (bf16[1,1,64,512]{3,2,1,0:T(8,128)(2,1)S(1)}, bf16[1,1,64,512]{3,2,1,0:T(8,128)(2,1)}, u32[]{:S(2)}) copy-start(bf16[1,1,64,512]{3,2,1,0:T(8,128)(2,1)} %param.10) | copy-start | bytes 196612
  7.8 14.4 %copy-start.5 = (bf16[1,1,64,512]{3,2,1,0:T(8,128)(2,1)S(1)}, bf16[1,1,64,512]{3,2,1,0:T(8,128)(2,1)}, u32[]{:S(2)}) copy-start(bf16[1,1,64,512]{3,2,1,0:T(8,128)(2,1)} %param.9) | copy-start | bytes 196612
  7.8 21.1 %copy-start.1 = (s32[8]{0:T(128)S(1)}, s32[8]{0:T(128)}, u32[]{:S(2)}) copy-start(s32[8]{0:T(128)} %stack.35.where) | copy-start | bytes 100
  9.9 21.1 %all-to-all-start = ((bf16[4,64,1280]{2,1,0:T(8,128)(2,1)}), bf16[4,64,1280]{2,1,0:T(8,128)(2,1)S(1)}, u32[]{:S(2)}, u32[]{:S(2)}) async-start(bf16[4,64,1280]{2,1,0:T(8,128)(2,1)} %open_second.1), calls=%async_computation | async-start | bytes 1310720 | tf_op jit(solution)/shard_map/all_to_all | solution.py:275
  15.3 77.6 %all-gather.2.cloned.1.call-start = ((), (), s32[]{:S(2)}) async-start(), calls=%async_computation.5 | async-start | bytes 2359296 | tf_op jit(solution)/shard_map/all_gather | solution.py:305
  15.3 13.6 %collective-permute-start = (bf16[64,4096]{1,0:T(8,128)(2,1)S(1)}, bf16[64,4096]{1,0:T(8,128)(2,1)S(1)}, u32[]{:S(2)}, u32[]{:S(2)}) collective-permute-start(bf16[64,4096]{1,0:T(8,128)(2,1)S(1)} %bitcast.34), channel_id=1, source_target_pairs={{0,112},{16,0},{32,16},{48,32},{64,48},{80,64},{96,80},{112,96},{1... | collective-permute-start | bytes 1572872 | tf_op jit(solution)/shard_map/ppermute | solution.py:278
  22.3 8.7 %collective-permute-start.1 = (bf16[64,1024]{1,0:T(8,128)(2,1)S(1)}, bf16[64,1024]{1,0:T(8,128)(2,1)S(1)}, u32[]{:S(2)}, u32[]{:S(2)}) collective-permute-start(bf16[64,1024]{1,0:T(8,128)(2,1)S(1)} %pad_maximum_fusion.1), channel_id=1, source_target_pairs={{0,8},{1,9},{2,10},{3,11},{4,12},{5,13},{6,14},{7,15},{16,24},{17,... | collective-permute-start | bytes 393224 | tf_op jit(solution)/shard_map/ppermute | solution.py:282
  30.2 24.7 %copy-start = (bf16[1,4096]{1,0:T(2,128)(2,1)S(1)}, bf16[1,4096]{1,0:T(2,128)(2,1)}, u32[]{:S(2)}) copy-start(bf16[1,4096]{1,0:T(2,128)(2,1)} %gain.1) | copy-start | bytes 24580
  31.8 27.3 %all-to-all-start.1 = ((bf16[4,64,1024]{2,1,0:T(8,128)(2,1)}), bf16[4,64,1024]{2,1,0:T(8,128)(2,1)S(1)}, u32[]{:S(2)}, u32[]{:S(2)}) async-start(bf16[4,64,1024]{2,1,0:T(8,128)(2,1)} %pack.1), calls=%async_computation.1 | async-start | bytes 1048576 | tf_op jit(solution)/shard_map/all_to_all | solution.py:275
  36.4 18.6 %collective-permute-start.3 = (bf16[256,256]{1,0:T(8,128)(2,1)S(1)}, bf16[256,256]{1,0:T(8,128)(2,1)S(1)}, u32[]{:S(2)}, u32[]{:S(2)}) collective-permute-start(bf16[256,256]{1,0:T(8,128)(2,1)S(1)} %slice.6), channel_id=1, source_target_pairs={{0,7},{1,6},{2,5},{3,4},{8,15},{9,14},{10,13},{11,12},{16,23},{17,... | collective-permute-start | bytes 393224 | tf_op jit(solution)/shard_map/ppermute | solution.py:303
  43.0 12.6 %collective-permute-start.4 = (bf16[256,256]{1,0:T(8,128)(2,1)S(1)}, bf16[256,256]{1,0:T(8,128)(2,1)S(1)}, u32[]{:S(2)}, u32[]{:S(2)}) collective-permute-start(bf16[256,256]{1,0:T(8,128)(2,1)S(1)} %slice.6), channel_id=1, source_target_pairs={{0,8},{1,9},{2,10},{3,11},{4,12},{5,13},{6,14},{7,15},{16,24},{17,... | collective-permute-start | bytes 393224 | tf_op jit(solution)/shard_map/ppermute | solution.py:303
  53.6 5.4 %collective-permute-start.5 = (bf16[256,256]{1,0:T(8,128)(2,1)S(1)}, bf16[256,256]{1,0:T(8,128)(2,1)S(1)}, u32[]{:S(2)}, u32[]{:S(2)}) collective-permute-start(bf16[256,256]{1,0:T(8,128)(2,1)S(1)} %slice.6), channel_id=1, source_target_pairs={{0,15},{1,14},{2,13},{3,12},{4,11},{5,10},{6,9},{7,8},{16,31},{17,... | collective-permute-start | bytes 393224 | tf_op jit(solution)/shard_map/ppermute | solution.py:303
  73.6 19.3 %copy-start.3 = (bf16[1,1,64,4096]{3,2,1,0:T(8,128)(2,1)S(1)}, bf16[1,1,64,4096]{3,2,1,0:T(8,128)(2,1)}, u32[]{:S(2)}) copy-start(bf16[1,1,64,4096]{3,2,1,0:T(8,128)(2,1)} %param.8) | copy-start | bytes 1572868
  80.9 28.1 %all-to-all-start.3 = ((bf16[16,80,256]{2,1,0:T(8,128)(2,1)}), bf16[16,80,256]{2,1,0:T(8,128)(2,1)S(1)}, u32[]{:S(2)}, u32[]{:S(2)}) async-start(bf16[16,80,256]{2,1,0:T(8,128)(2,1)} %get-tuple-element.25), calls=%async_computation.3 | async-start | bytes 1310720 | tf_op jit(solution)/shard_map/all_to_all | solution.py:275
  92.9 1.6 %copy-start.2 = (bf16[1024,1024]{1,0:T(8,128)(2,1)S(1)}, bf16[1024,1024]{1,0:T(8,128)(2,1)}, u32[]{:S(2)}) copy-start(bf16[1024,1024]{1,0:T(8,128)(2,1)} %all-gather.2.cloned.1.call-done.kv) | copy-start | bytes 6291460
  109.0 26.2 %all-to-all-start.4 = ((bf16[4,64,1024]{2,1,0:T(8,128)(2,1)}), bf16[4,64,1024]{2,1,0:T(8,128)(2,1)S(1)}, u32[]{:S(2)}, u32[]{:S(2)}) async-start(bf16[4,64,1024]{2,1,0:T(8,128)(2,1)} %bitcast.18), calls=%async_computation.4 | async-start | bytes 1048576 | tf_op jit(solution)/shard_map/all_to_all | solution.py:275
  112.5 22.7 %collective-permute-start.2 = (bf16[64,4096]{1,0:T(8,128)(2,1)S(1)}, bf16[64,4096]{1,0:T(8,128)(2,1)S(1)}, u32[]{:S(2)}, u32[]{:S(2)}) collective-permute-start(bf16[64,4096]{1,0:T(8,128)(2,1)S(1)} %forward_first.1), channel_id=1, source_target_pairs={{0,16},{16,32},{32,48},{48,64},{64,80},{80,96},{96,112},{112,0},{1... | collective-permute-start | bytes 1572872 | tf_op jit(solution)/shard_map/ppermute | solution.py:278
Sparse Core Ops, SparseCore 0:
  31.9 50.2 all-gather.1

commit v6 on v5

--- a/solution.py
+++ b/solution.py
@@ -260,7 +260,7 @@
     group = zhi * 2 + yhi
     mine = ylo + yhi * (FOUR - 1 - 2 * ylo)
     where = jnp.stack(
-        [group, zhi, mine, yhi * FOUR + ylo, yhi, zhi * 2 + 1 - yhi, 2 - zhi * 2 + yhi, 3 - group]
+        [group, zhi, mine, yhi * FOUR + ylo, yhi, 3 - group, 2 - zhi * 2 + yhi, zhi * 2 + 1 - yhi]
     ).astype(jnp.int32)
     gain_cols = lax.dynamic_slice_in_dim(gain, mine * cols, cols, 1)
 
@@ -300,7 +300,7 @@
     )
     qkv, up, other = lax.optimization_barrier((qkv, up, other))
     qkv = qkv.reshape(n, cols + 2 * HD)
-    kvs = [lax.ppermute(qkv[:, cols:], SEQ, pairs) for pairs in (near, far, cross)]
+    kvs = [lax.ppermute(qkv[:, cols:], SEQ, pairs) for pairs in (cross, far, near)]
     up = swap(up, "ylo").reshape(n, cols)
     kv_first = lax.all_gather(
         jnp.concatenate([kv1, other], axis=0), ROW, axis=0, tiled=True

time: 145 us -> 146 us (level)
  waiting for transfers between devices: 12.8 us -> 22.3 us
  starting transfers between devices: 69.4 us -> 62 us
    ppermute x3, waiting for transfers between devices: 4.05 us -> 11.9 us  [local(): lax.ppermute(qkv[:, cols:], SEQ, pairs)]
    all_to_all x4, starting transfers between devices: 25.4 us -> 20.1 us  [swap(): return lax.all_to_all(packed, axes, split_axis=0, concat_axis=0, tiled=True)]
    ppermute x2, starting transfers between devices: 18.9 us -> 16.8 us  [along(): lax.ppermute(value, axis, [(i, (i + step) % count) for i in range(count)])]
    all_to_all x4, waiting for transfers between devices: 7.96 us -> 9.6 us  [swap(): return lax.all_to_all(packed, axes, split_axis=0, concat_axis=0, tiled=True)]
where the time goes in v6:
time: 146 us; the launch traced here: 145 us
  starting transfers between devices  62 us (42%)
  Pallas kernels  26.4 us (18%)
  waiting for transfers between devices  22.3 us (15%)
  blocking collectives  16.7 us (11%)
  between operations  14.2 us (10%)
  local copies, waits for them, and re-layouts  3.02 us (2%)
    pallas_call x6, Pallas kernels, call(): pl.pallas_call(body, out_shape=outs, in_specs=[SMEM] + [VMEM] * (len(inpu...  24.3 us
    all_to_all x4, starting transfers between devices, swap(): return lax.all_to_all(packed, axes, split_axis=0, concat_axis=0, tiled=True)  20.1 us
    ppermute x3, starting transfers between devices, local(): lax.ppermute(qkv[:, cols:], SEQ, pairs)  18.5 us
    ppermute x2, starting transfers between devices, along(): lax.ppermute(value, axis, [(i, (i + step) % count) for i in range(count)])  16.8 us
    ppermute x3, waiting for transfers between devices, local(): lax.ppermute(qkv[:, cols:], SEQ, pairs)  11.9 us
    psum x1, blocking collectives, local(): grad_gain = lax.psum(share, 'dp')  9.62 us
    all_to_all x4, waiting for transfers between devices, swap(): return lax.all_to_all(packed, axes, split_axis=0, concat_axis=0, tiled=True)  9.6 us
    all_to_all x1, blocking collectives, swap(): return lax.all_to_all(packed, axes, split_axis=0, concat_axis=0, tiled=True)  7.06 us
  transfers between devices with their start and end apart: 11, of which 4 were waited for; matrix products, arithmetic and copies ran while one was open for 0% of the time, Pallas kernels for 16%

profile of v6, /device:TPU:1, one launch (start us, length us, event | category | flops | bytes accessed | tf_op | source)
XLA Modules:
  0.0 145.4 jit_solution(17814090040809384863)
XLA Ops:
  7.2 0.6 stack.35.where
  7.8 0.0 copy-start.6
  7.8 0.0 copy-start.4
  7.8 0.0 copy-start.5
  7.8 0.0 copy-start.1
  7.8 2.1 %open_second.1 = bf16[4,64,1280]{2,1,0:T(8,128)(2,1)} custom-call(s32[8]{0:T(128)} %stack.35.where, bf16[64,4096]{1,0:T(8,128)(2,1)} %bitcast.33, bf16[64,512]{1,0:T(8,128)(2,1)} %bitcast.35, bf16[64,512]{1,0:T(8,128)(2,1)} %bitcast.36), custom_call_target="tpu_custom_call" | custom-call | flops 1000000000 | tf_op jit(solution)/shard_map/open_second/pallas_call | solution.py:283
  9.9 5.4 %all-to-all-start = ((bf16[4,64,1280]{2,1,0:T(8,128)(2,1)}), bf16[4,64,1280]{2,1,0:T(8,128)(2,1)S(1)}, u32[]{:S(2)}, u32[]{:S(2)}) async-start(bf16[4,64,1280]{2,1,0:T(8,128)(2,1)} %open_second.1), calls=%async_computation | async-start | bytes 1310720 | tf_op jit(solution)/shard_map/all_to_all | solution.py:275
  15.3 0.0 all-gather.2.cloned.1.call-start
  15.3 0.0 copy-done.6
  15.3 6.9 %collective-permute-start = (bf16[64,4096]{1,0:T(8,128)(2,1)S(1)}, bf16[64,4096]{1,0:T(8,128)(2,1)S(1)}, u32[]{:S(2)}, u32[]{:S(2)}) collective-permute-start(bf16[64,4096]{1,0:T(8,128)(2,1)S(1)} %bitcast.34), channel_id=1, source_target_pairs={{0,112},{16,0},{32,16},{48,32},{64,48},{80,64},{96,80},{112,96},{1... | collective-permute-start | bytes 1572872 | tf_op jit(solution)/shard_map/ppermute | solution.py:278
  22.2 0.0 copy-done.4
  22.2 0.0 copy-done.5
  22.3 6.6 %collective-permute-start.1 = (bf16[64,1024]{1,0:T(8,128)(2,1)S(1)}, bf16[64,1024]{1,0:T(8,128)(2,1)S(1)}, u32[]{:S(2)}, u32[]{:S(2)}) collective-permute-start(bf16[64,1024]{1,0:T(8,128)(2,1)S(1)} %pad_maximum_fusion.1), channel_id=1, source_target_pairs={{0,8},{1,9},{2,10},{3,11},{4,12},{5,13},{6,14},{7,15},{16,24},{17,... | collective-permute-start | bytes 393224 | tf_op jit(solution)/shard_map/ppermute | solution.py:282
  28.9 0.0 collective-permute-done.full
  28.9 0.0 copy-done.1
  28.9 1.4 pack.1
  30.2 0.0 copy-start
  30.2 0.8 collective-permute-done.1
  31.0 0.0 all-to-all-done
  31.0 0.7 pad_maximum_fusion
  31.7 0.0 all-gather.2.cloned.1.call-update
  31.8 4.6 %all-to-all-start.1 = ((bf16[4,64,1024]{2,1,0:T(8,128)(2,1)}), bf16[4,64,1024]{2,1,0:T(8,128)(2,1)S(1)}, u32[]{:S(2)}, u32[]{:S(2)}) async-start(bf16[4,64,1024]{2,1,0:T(8,128)(2,1)} %pack.1), calls=%async_computation.1 | async-start | bytes 1048576 | tf_op jit(solution)/shard_map/all_to_all | solution.py:275
  36.4 15.0 %collective-permute-start.3 = (bf16[256,256]{1,0:T(8,128)(2,1)S(1)}, bf16[256,256]{1,0:T(8,128)(2,1)S(1)}, u32[]{:S(2)}, u32[]{:S(2)}) collective-permute-start(bf16[256,256]{1,0:T(8,128)(2,1)S(1)} %slice.6), channel_id=1, source_target_pairs={{0,15},{1,14},{2,13},{3,12},{4,11},{5,10},{6,9},{7,8},{16,31},{17,... | collective-permute-start | bytes 393224 | tf_op jit(solution)/shard_map/ppermute | solution.py:303
  51.4 1.3 collective-permute-start.4
  52.7 2.2 %collective-permute-start.5 = (bf16[256,256]{1,0:T(8,128)(2,1)S(1)}, bf16[256,256]{1,0:T(8,128)(2,1)S(1)}, u32[]{:S(2)}, u32[]{:S(2)}) collective-permute-start(bf16[256,256]{1,0:T(8,128)(2,1)S(1)} %slice.6), channel_id=1, source_target_pairs={{0,7},{1,6},{2,5},{3,4},{8,15},{9,14},{10,13},{11,12},{16,23},{17,... | collective-permute-start | bytes 393224 | tf_op jit(solution)/shard_map/ppermute | solution.py:303
  54.9 0.0 copy-done
  54.9 2.0 %collective-permute-done.3.kv1 = bf16[256,256]{1,0:T(8,128)(2,1)S(1)} collective-permute-done((bf16[256,256]{1,0:T(8,128)(2,1)S(1)}, bf16[256,256]{1,0:T(8,128)(2,1)S(1)}, u32[]{:S(2)}, u32[]{:S(2)}) %collective-permute-start.3) | collective-permute-done | bytes 131104 | tf_op jit(solution)/shard_map/ppermute | solution.py:303
  57.0 0.0 collective-permute-done.4.kv2
  57.0 9.9 %collective-permute-done.5.kv3 = bf16[256,256]{1,0:T(8,128)(2,1)S(1)} collective-permute-done((bf16[256,256]{1,0:T(8,128)(2,1)S(1)}, bf16[256,256]{1,0:T(8,128)(2,1)S(1)}, u32[]{:S(2)}, u32[]{:S(2)}) %collective-permute-start.5) | collective-permute-done | bytes 131104 | tf_op jit(solution)/shard_map/ppermute | solution.py:303
  66.9 0.0 all-to-all-done.1
  66.9 6.4 %forward_second.1 = (bf16[256,1024]{1,0:T(8,128)(2,1)S(1)}, f32[8,256]{1,0:T(8,128)S(1)}, f32[4,8,256]{2,1,0:T(8,128)S(1)}) custom-call(s32[8]{0:T(128)S(1)} %copy-done.1, bf16[256,1280]{1,0:T(8,128)(2,1)S(1)} %bitcast.23, bf16[256,256]{1,0:T(8,128)(2,1)S(1)} %collective-permute-done.3.kv1, bf16[256,256]{1,0:T(8,128)(2,1)S(1)} %collective-permute-done.4.kv2, ...), custom_call_target="tpu_custom_call" | custom-call | flops 6400000000 | tf_op jit(solution)/shard_map/forward_second/pallas_call | solution.py:28
  73.3 7.1 %all_to_all.25.stats = f32[4,8,256]{2,1,0:T(8,128)S(1)} all-to-all(f32[4,8,256]{2,1,0:T(8,128)S(1)} %get-tuple-element.23), channel_id=1, replica_groups=mesh['dp'=4,'pipe'=8,'zhi'=2,'yhi'=2,'ylo'=4] {'ylo'}, dimensions={0} | all-to-all | bytes 65536 | tf_op jit(solution)/shard_map/all_to_all | solution.py:275
  80.3 0.0 copy-start.3
  80.3 7.4 %backward.1 = (bf16[256,1024]{1,0:T(8,128)(2,1)}, bf16[16,80,256]{2,1,0:T(8,128)(2,1)}) custom-call(s32[8]{0:T(128)S(1)} %copy-done.1, bf16[256,1280]{1,0:T(8,128)(2,1)S(1)} %bitcast.24, bf16[256,256]{1,0:T(8,128)(2,1)S(1)} %collective-permute-done.3.kv1, bf16[256,256]{1,0:T(8,128)(2,1)S(1)} %collective-permute-done.4.kv2, ...), custom_call_target="tpu_custom_call" | custom-call | flops 7000000000 | tf_op jit(solution)/shard_map/backward/pallas_call | solution.py:28
  87.7 6.6 %all-to-all-start.3 = ((bf16[16,80,256]{2,1,0:T(8,128)(2,1)}), bf16[16,80,256]{2,1,0:T(8,128)(2,1)S(1)}, u32[]{:S(2)}, u32[]{:S(2)}) async-start(bf16[16,80,256]{2,1,0:T(8,128)(2,1)} %get-tuple-element.25), calls=%async_computation.3 | async-start | bytes 1310720 | tf_op jit(solution)/shard_map/all_to_all | solution.py:275
  94.3 0.0 all-gather.2.cloned.1.call-done.kv
  94.3 0.0 copy-done.3
  94.3 0.0 copy-start.2
  94.3 1.6 %copy-done.2 = bf16[1024,1024]{1,0:T(8,128)(2,1)S(1)} copy-done((bf16[1024,1024]{1,0:T(8,128)(2,1)S(1)}, bf16[1024,1024]{1,0:T(8,128)(2,1)}, u32[]{:S(2)}) %copy-start.2) | copy-done | bytes 2097176
  95.9 6.6 %forward_first.1 = bf16[64,4096]{1,0:T(8,128)(2,1)S(1)} custom-call(s32[8]{0:T(128)S(1)} %copy-done.1, bf16[64,4096]{1,0:T(8,128)(2,1)S(1)} %bitcast.27, bf16[1024,1024]{1,0:T(8,128)(2,1)S(1)} %copy-done.2, bf16[1,4096]{1,0:T(2,128)(2,1)S(1)} %copy-done), custom_call_target="tpu_custom_call" | custom-call | flops 7000000000 | tf_op jit(solution)/shard_map/forward_first/pallas_call | solution.py:28
  102.5 9.6 %all-to-all-done.3.parts = bf16[16,80,256]{2,1,0:T(8,128)(2,1)S(1)} async-done(((bf16[16,80,256]{2,1,0:T(8,128)(2,1)}), bf16[16,80,256]{2,1,0:T(8,128)(2,1)S(1)}, u32[]{:S(2)}, u32[]{:S(2)}) %all-to-all-start.3) | async-done | bytes 655392 | tf_op jit(solution)/shard_map/all_to_all | solution.py:275
  112.1 3.5 %all-to-all-start.4 = ((bf16[4,64,1024]{2,1,0:T(8,128)(2,1)}), bf16[4,64,1024]{2,1,0:T(8,128)(2,1)S(1)}, u32[]{:S(2)}, u32[]{:S(2)}) async-start(bf16[4,64,1024]{2,1,0:T(8,128)(2,1)} %bitcast.18), calls=%async_computation.4 | async-start | bytes 1048576 | tf_op jit(solution)/shard_map/all_to_all | solution.py:275
  115.6 9.9 %collective-permute-start.2 = (bf16[64,4096]{1,0:T(8,128)(2,1)S(1)}, bf16[64,4096]{1,0:T(8,128)(2,1)S(1)}, u32[]{:S(2)}, u32[]{:S(2)}) collective-permute-start(bf16[64,4096]{1,0:T(8,128)(2,1)S(1)} %forward_first.1), channel_id=1, source_target_pairs={{0,16},{16,32},{32,48},{48,64},{64,80},{80,96},{96,112},{112,0},{1... | collective-permute-start | bytes 1572872 | tf_op jit(solution)/shard_map/ppermute | solution.py:278
  125.5 1.3 gather.1
  126.8 9.6 %psum.7 = f32[1,256]{1,0:T(1,128)} all-reduce(f32[1,256]{1,0:T(1,128)S(1)} %get-tuple-element.30), channel_id=1, replica_groups=mesh['dp'=4,'pipe'=8,'zhi'=2,'yhi'=2,'ylo'=4] {'dp'}, use_global_device_ids=true, to_apply=%region_0.0 | all-reduce | flops 256 | bytes 2048 | tf_op jit(solution)/shard_map/psum | solution.py:359
  136.4 0.0 collective-permute-done.2
  136.4 0.0 all-to-all-done.4.parts
  136.4 1.4 join.1
  137.8 0.8 copy.14
  (3 shorter events, 0.0 us)
Async XLA Ops:
  7.8 7.5 %copy-start.6 = (bf16[1,1,64,4096]{3,2,1,0:T(8,128)(2,1)S(1)}, bf16[1,1,64,4096]{3,2,1,0:T(8,128)(2,1)}, u32[]{:S(2)}) copy-start(bf16[1,1,64,4096]{3,2,1,0:T(8,128)(2,1)} %param.14) | copy-start | bytes 1572868
  7.8 14.4 %copy-start.4 = (bf16[1,1,64,512]{3,2,1,0:T(8,128)(2,1)S(1)}, bf16[1,1,64,512]{3,2,1,0:T(8,128)(2,1)}, u32[]{:S(2)}) copy-start(bf16[1,1,64,512]{3,2,1,0:T(8,128)(2,1)} %param.10) | copy-start | bytes 196612
  7.8 14.4 %copy-start.5 = (bf16[1,1,64,512]{3,2,1,0:T(8,128)(2,1)S(1)}, bf16[1,1,64,512]{3,2,1,0:T(8,128)(2,1)}, u32[]{:S(2)}) copy-start(bf16[1,1,64,512]{3,2,1,0:T(8,128)(2,1)} %param.9) | copy-start | bytes 196612
  7.8 21.1 %copy-start.1 = (s32[8]{0:T(128)S(1)}, s32[8]{0:T(128)}, u32[]{:S(2)}) copy-start(s32[8]{0:T(128)} %stack.35.where) | copy-start | bytes 100
  9.9 21.1 %all-to-all-start = ((bf16[4,64,1280]{2,1,0:T(8,128)(2,1)}), bf16[4,64,1280]{2,1,0:T(8,128)(2,1)S(1)}, u32[]{:S(2)}, u32[]{:S(2)}) async-start(bf16[4,64,1280]{2,1,0:T(8,128)(2,1)} %open_second.1), calls=%async_computation | async-start | bytes 1310720 | tf_op jit(solution)/shard_map/all_to_all | solution.py:275
  15.3 79.0 %all-gather.2.cloned.1.call-start = ((), (), s32[]{:S(2)}) async-start(), calls=%async_computation.5 | async-start | bytes 2359296 | tf_op jit(solution)/shard_map/all_gather | solution.py:305
  15.3 13.6 %collective-permute-start = (bf16[64,4096]{1,0:T(8,128)(2,1)S(1)}, bf16[64,4096]{1,0:T(8,128)(2,1)S(1)}, u32[]{:S(2)}, u32[]{:S(2)}) collective-permute-start(bf16[64,4096]{1,0:T(8,128)(2,1)S(1)} %bitcast.34), channel_id=1, source_target_pairs={{0,112},{16,0},{32,16},{48,32},{64,48},{80,64},{96,80},{112,96},{1... | collective-permute-start | bytes 1572872 | tf_op jit(solution)/shard_map/ppermute | solution.py:278
  22.3 8.7 %collective-permute-start.1 = (bf16[64,1024]{1,0:T(8,128)(2,1)S(1)}, bf16[64,1024]{1,0:T(8,128)(2,1)S(1)}, u32[]{:S(2)}, u32[]{:S(2)}) collective-permute-start(bf16[64,1024]{1,0:T(8,128)(2,1)S(1)} %pad_maximum_fusion.1), channel_id=1, source_target_pairs={{0,8},{1,9},{2,10},{3,11},{4,12},{5,13},{6,14},{7,15},{16,24},{17,... | collective-permute-start | bytes 393224 | tf_op jit(solution)/shard_map/ppermute | solution.py:282
  30.2 24.7 %copy-start = (bf16[1,4096]{1,0:T(2,128)(2,1)S(1)}, bf16[1,4096]{1,0:T(2,128)(2,1)}, u32[]{:S(2)}) copy-start(bf16[1,4096]{1,0:T(2,128)(2,1)} %gain.1) | copy-start | bytes 24580
  31.8 35.1 %all-to-all-start.1 = ((bf16[4,64,1024]{2,1,0:T(8,128)(2,1)}), bf16[4,64,1024]{2,1,0:T(8,128)(2,1)S(1)}, u32[]{:S(2)}, u32[]{:S(2)}) async-start(bf16[4,64,1024]{2,1,0:T(8,128)(2,1)} %pack.1), calls=%async_computation.1 | async-start | bytes 1048576 | tf_op jit(solution)/shard_map/all_to_all | solution.py:275
  36.4 20.6 %collective-permute-start.3 = (bf16[256,256]{1,0:T(8,128)(2,1)S(1)}, bf16[256,256]{1,0:T(8,128)(2,1)S(1)}, u32[]{:S(2)}, u32[]{:S(2)}) collective-permute-start(bf16[256,256]{1,0:T(8,128)(2,1)S(1)} %slice.6), channel_id=1, source_target_pairs={{0,15},{1,14},{2,13},{3,12},{4,11},{5,10},{6,9},{7,8},{16,31},{17,... | collective-permute-start | bytes 393224 | tf_op jit(solution)/shard_map/ppermute | solution.py:303
  51.4 5.6 %collective-permute-start.4 = (bf16[256,256]{1,0:T(8,128)(2,1)S(1)}, bf16[256,256]{1,0:T(8,128)(2,1)S(1)}, u32[]{:S(2)}, u32[]{:S(2)}) collective-permute-start(bf16[256,256]{1,0:T(8,128)(2,1)S(1)} %slice.6), channel_id=1, source_target_pairs={{0,8},{1,9},{2,10},{3,11},{4,12},{5,13},{6,14},{7,15},{16,24},{17,... | collective-permute-start | bytes 393224 | tf_op jit(solution)/shard_map/ppermute | solution.py:303
  52.7 14.1 %collective-permute-start.5 = (bf16[256,256]{1,0:T(8,128)(2,1)S(1)}, bf16[256,256]{1,0:T(8,128)(2,1)S(1)}, u32[]{:S(2)}, u32[]{:S(2)}) collective-permute-start(bf16[256,256]{1,0:T(8,128)(2,1)S(1)} %slice.6), channel_id=1, source_target_pairs={{0,7},{1,6},{2,5},{3,4},{8,15},{9,14},{10,13},{11,12},{16,23},{17,... | collective-permute-start | bytes 393224 | tf_op jit(solution)/shard_map/ppermute | solution.py:303
  80.3 14.0 %copy-start.3 = (bf16[1,1,64,4096]{3,2,1,0:T(8,128)(2,1)S(1)}, bf16[1,1,64,4096]{3,2,1,0:T(8,128)(2,1)}, u32[]{:S(2)}) copy-start(bf16[1,1,64,4096]{3,2,1,0:T(8,128)(2,1)} %param.8) | copy-start | bytes 1572868
  87.7 24.4 %all-to-all-start.3 = ((bf16[16,80,256]{2,1,0:T(8,128)(2,1)}), bf16[16,80,256]{2,1,0:T(8,128)(2,1)S(1)}, u32[]{:S(2)}, u32[]{:S(2)}) async-start(bf16[16,80,256]{2,1,0:T(8,128)(2,1)} %get-tuple-element.25), calls=%async_computation.3 | async-start | bytes 1310720 | tf_op jit(solution)/shard_map/all_to_all | solution.py:275
  94.3 1.6 %copy-start.2 = (bf16[1024,1024]{1,0:T(8,128)(2,1)S(1)}, bf16[1024,1024]{1,0:T(8,128)(2,1)}, u32[]{:S(2)}) copy-start(bf16[1024,1024]{1,0:T(8,128)(2,1)} %all-gather.2.cloned.1.call-done.kv) | copy-start | bytes 6291460
  112.1 24.3 %all-to-all-start.4 = ((bf16[4,64,1024]{2,1,0:T(8,128)(2,1)}), bf16[4,64,1024]{2,1,0:T(8,128)(2,1)S(1)}, u32[]{:S(2)}, u32[]{:S(2)}) async-start(bf16[4,64,1024]{2,1,0:T(8,128)(2,1)} %bitcast.18), calls=%async_computation.4 | async-start | bytes 1048576 | tf_op jit(solution)/shard_map/all_to_all | solution.py:275
  115.6 20.8 %collective-permute-start.2 = (bf16[64,4096]{1,0:T(8,128)(2,1)S(1)}, bf16[64,4096]{1,0:T(8,128)(2,1)S(1)}, u32[]{:S(2)}, u32[]{:S(2)}) collective-permute-start(bf16[64,4096]{1,0:T(8,128)(2,1)S(1)} %forward_first.1), channel_id=1, source_target_pairs={{0,16},{16,32},{32,48},{48,64},{64,80},{80,96},{96,112},{112,0},{1... | collective-permute-start | bytes 1572872 | tf_op jit(solution)/shard_map/ppermute | solution.py:278
Sparse Core Ops, SparseCore 0:
  31.9 53.3 all-gather.1
